TPU v7x, 128 devices: a whole 4x4x4 slice. The times are simulated.
128 devices in a mesh: gx: 16 (over y_hi, x, core), gy: 8 (over y_lo, z).
Axes of the slice: x: 4, y: 4 (y_hi: 2, y_lo: 2; y = y_hi * 2 + y_lo), z: 4, core: 2. Of those that a mesh axis runs over, the one named last changes fastest.
Arguments:
- features: bfloat16 [128, 128, 8, 256], P('gx', 'gy'), may hold values from -6 to 6
- grad_out: bfloat16 [128, 128, 8, 256], P('gx', 'gy'), may hold values from -6 to 6
- weights: bfloat16 [27, 256, 256], replicated, may hold values from -0.078125 to 0.078125
- occupied: int32 [32, 32, 2], P('gx', 'gy'), may hold values 0 or 1
Outputs:
- grad_features: bfloat16 [128, 128, 8, 256], P('gx', 'gy')
- grad_weights: float32 [27, 256, 256], replicated
All inputs are finite; a program needn't handle non-finite values. No bound on the sum of `occupied` on one device may be relied on, other than what follows from the above.
Results may differ from a plain program's by a relative error of at most 0.0049.
Values may be sent and summed in bfloat16 or wider, within the bound.
No kernel may reach another device: no remote copies, remote signals or barrier semaphores. Data moves between devices by JAX's collectives and lax.ppermute only.
A program may use at most 128 MiB of HBM per device.

v0:
```python
import jax
import jax.numpy as jnp
from jax import lax
from jax.sharding import PartitionSpec as P


def with_halo(cells, sides, width):
    for axis, dim in sides:
        count = lax.axis_size(axis)
        ends = count - 1
        head = lax.slice_in_dim(cells, 0, width, axis=dim)
        tail = lax.slice_in_dim(cells, cells.shape[dim] - width, cells.shape[dim], axis=dim)
        cells = jnp.concatenate(
            [
                lax.ppermute(tail, axis, [(i, (i + 1) % count) for i in range(ends)]),
                cells,
                lax.ppermute(head, axis, [((i + 1) % count, i) for i in range(ends)]),
            ],
            axis=dim,
        )
    return cells


def offsets():
    return [(a, b, c) for a in (-1, 0, 1) for b in (-1, 0, 1) for c in (-1, 0, 1)]


def expand_mask(occupied):
    cells = jnp.repeat(jnp.repeat(jnp.repeat(occupied, 4, axis=0), 4, axis=1), 4, axis=2)
    return cells.astype(jnp.bfloat16)[..., None]


def dsilu(pre):
    sig = jax.nn.sigmoid(pre)
    return sig * (1.0 + pre * (1.0 - sig))


def pad_vertical(field):
    return jnp.pad(field, ((0, 0), (0, 0), (1, 1), (0, 0)))


def forward_conv(extended, weights, sx, sy, sz):
    chan = extended.shape[3]
    total = jnp.zeros((sx * sy * sz, chan), jnp.float32)
    for index, (ox, oy, oz) in enumerate(offsets()):
        piece = extended[1 + ox : 1 + ox + sx, 1 + oy : 1 + oy + sy, 1 + oz : 1 + oz + sz].reshape(
            -1, chan
        )
        total = total + jnp.dot(piece, weights[index], preferred_element_type=jnp.float32)
    return total.reshape(sx, sy, sz, chan)


def input_grads(dextended, weights, sx, sy, sz):
    chan = dextended.shape[3]
    total = jnp.zeros((sx * sy * sz, chan), jnp.float32)
    for index, (ox, oy, oz) in enumerate(offsets()):
        piece = dextended[1 - ox : 1 - ox + sx, 1 - oy : 1 - oy + sy, 1 - oz : 1 - oz + sz].reshape(
            -1, chan
        )
        total = total + jnp.dot(piece, weights[index].T, preferred_element_type=jnp.float32)
    return total.reshape(sx, sy, sz, chan)


def kernel_grads(source, center, sx, sy, sz):
    chan = center.shape[3]
    flat = center.reshape(-1, chan)
    grads = []
    for index, (ox, oy, oz) in enumerate(offsets()):
        block = source[1 + ox : 1 + ox + sx, 1 + oy : 1 + oy + sy, 1 + oz : 1 + oz + sz].reshape(
            -1, chan
        )
        grads.append(
            lax.dot_general(
                block, flat, (((0,), (0,)), ((), ())), preferred_element_type=jnp.float32
            )
        )
    return jnp.stack(grads)


def reduce_grads(local_grads):
    return lax.psum(local_grads, ("gx", "gy"))


def local(features, grad_out, weights, occupied):
    cellmask = expand_mask(occupied)
    masked = features * cellmask
    masked_grad = grad_out * cellmask
    sx, sy, sz, chan = masked.shape
    source = pad_vertical(with_halo(masked, (("gx", 0), ("gy", 1)), 1))
    pre = forward_conv(source, weights, sx, sy, sz)
    center = (masked_grad.astype(jnp.float32) * dsilu(pre)).astype(jnp.bfloat16)
    dextended = pad_vertical(with_halo(center, (("gx", 0), ("gy", 1)), 1))
    total = input_grads(dextended, weights, sx, sy, sz)
    grad_weights = reduce_grads(kernel_grads(source, center, sx, sy, sz))
    grad_features = (total * cellmask.astype(jnp.float32)).astype(jnp.bfloat16)
    return (grad_features, grad_weights)


def solution(mesh):
    return jax.shard_map(
        local,
        mesh=mesh,
        in_specs=(P("gx", "gy", None, None), P("gx", "gy", None, None), P(), P("gx", "gy", None)),
        out_specs=(P("gx", "gy", None, None), P()),
        check_vma=False,
    )
```

profile of v0, /device:TPU:1, one launch (start us, length us, event | category | flops | bytes accessed | tf_op | source)
XLA Modules:
  0.0 261.4 jit_solution(3765676015162737217)
XLA Ops:
  8.3 1.2 copy_multiply_fusion
  9.6 3.3 %collective-permute-start.1 = (bf16[1,16,8,256]{3,1,2,0:T(8,128)(2,1)S(1)}, bf16[1,16,8,256]{3,1,2,0:T(8,128)(2,1)S(1)}, u32[]{:S(2)}, u32[]{:S(2)}) collective-permute-start(bf16[1,16,8,256]{3,1,2,0:T(8,128)(2,1)S(1)} %get-tuple-element.65), channel_id=1, source_target_pairs={{8,0},{16,8},{24,16},{32,24},{40,32},{48,40},{56,48},{64,56},{72,6... | collective-permute-start | bytes 196616 | tf_op jit(solution)/shard_map/ppermute | solution.py:17
  12.9 3.1 %collective-permute-start = (bf16[1,16,8,256]{3,1,2,0:T(8,128)(2,1)S(1)}, bf16[1,16,8,256]{3,1,2,0:T(8,128)(2,1)S(1)}, u32[]{:S(2)}, u32[]{:S(2)}) collective-permute-start(bf16[1,16,8,256]{3,1,2,0:T(8,128)(2,1)S(1)} %get-tuple-element.64), channel_id=1, source_target_pairs={{0,8},{8,16},{16,24},{24,32},{32,40},{40,48},{48,56},{56,64},{64,7... | collective-permute-start | bytes 196616 | tf_op jit(solution)/shard_map/ppermute | solution.py:15
  17.4 1.3 collective-permute-start.3
  18.7 4.2 %collective-permute-start.2 = (bf16[10,1,8,256]{3,1,2,0:T(2,128)(2,1)S(1)}, bf16[10,1,8,256]{3,1,2,0:T(2,128)(2,1)S(1)}, u32[]{:S(2)}, u32[]{:S(2)}) collective-permute-start(bf16[10,1,8,256]{3,1,2,0:T(2,128)(2,1)S(1)} %get-tuple-element.56), channel_id=1, source_target_pairs={{0,1},{1,2},{2,3},{3,4},{4,5},{5,6},{6,7},{8,9},{9,10},{10,11},{11... | collective-permute-start | bytes 122888 | tf_op jit(solution)/shard_map/ppermute | solution.py:15
  23.4 1.2 collective-permute-done.2
  25.3 2.3 fusion.185
  43.8 1.9 collective-permute-start.5
  45.7 5.2 %collective-permute-start.4 = (bf16[1,16,8,256]{3,1,2,0:T(8,128)(2,1)S(1)}, bf16[1,16,8,256]{3,1,2,0:T(8,128)(2,1)S(1)}, u32[]{:S(2)}, u32[]{:S(2)}) collective-permute-start(bf16[1,16,8,256]{3,1,2,0:T(8,128)(2,1)S(1)} %get-tuple-element.60), channel_id=1, source_target_pairs={{0,8},{8,16},{16,24},{24,32},{32,40},{40,48},{48,56},{56,64},{64,7... | collective-permute-start | bytes 196616 | tf_op jit(solution)/shard_map/ppermute | solution.py:15
  50.9 1.1 fusion.40
  53.0 1.0 fusion.38
  55.1 1.1 fusion.37
  56.2 1.0 fusion.36
  57.2 1.0 fusion.35
  58.3 1.1 fusion.34
  60.4 1.1 fusion.32
  62.5 1.1 fusion.30
  64.6 1.1 fusion.28
  65.6 1.1 fusion.27
  66.7 1.0 fusion.26
  67.7 1.0 fusion.25
  69.8 1.1 fusion.23
  71.9 1.1 fusion.21
  74.0 1.1 fusion.20
  75.1 1.0 fusion.19
  76.1 1.0 fusion.18
  77.2 1.1 fusion.17
  78.6 1.3 collective-permute-start.7
  79.9 4.6 %collective-permute-start.6 = (bf16[10,1,8,256]{3,1,2,0:T(2,128)(2,1)S(1)}, bf16[10,1,8,256]{3,1,2,0:T(2,128)(2,1)S(1)}, u32[]{:S(2)}, u32[]{:S(2)}) collective-permute-start(bf16[10,1,8,256]{3,1,2,0:T(2,128)(2,1)S(1)} %get-tuple-element.52), channel_id=1, source_target_pairs={{0,1},{1,2},{2,3},{3,4},{4,5},{5,6},{6,7},{8,9},{9,10},{10,11},{11... | collective-permute-start | bytes 122888 | tf_op jit(solution)/shard_map/ppermute | solution.py:15
  86.7 2.4 fusion.184
  104.7 142.6 %all-reduce.4.cloned.1.call-done = f32[27,256,256]{2,1,0:T(8,128)} async-done(((f32[27,256,256]{2,1,0:T(8,128)}), f32[27,256,256]{2,1,0:T(8,128)}) %all-reduce.4.cloned.1.call-update) | async-done | bytes 7077904 | tf_op jit(solution)/shard_map/psum | solution.py:81
  247.4 6.7 %copy.134 = f32[27,256,256]{2,1,0:T(8,128)} copy(f32[27,256,256]{2,1,0:T(8,128)} %all-reduce.4.cloned.1.call-done) | data formatting | bytes 14155776
  (156 shorter events, 45.6 us)
Async XLA Ops:
  7.2 240.2 %all-reduce.4.cloned.1.call-start = ((), (), s32[]{:S(2)}) async-start(), calls=%async_computation | async-start | bytes 14155776 | tf_op jit(solution)/shard_map/psum | solution.py:81
  9.6 6.7 %collective-permute-start.1 = (bf16[1,16,8,256]{3,1,2,0:T(8,128)(2,1)S(1)}, bf16[1,16,8,256]{3,1,2,0:T(8,128)(2,1)S(1)}, u32[]{:S(2)}, u32[]{:S(2)}) collective-permute-start(bf16[1,16,8,256]{3,1,2,0:T(8,128)(2,1)S(1)} %get-tuple-element.65), channel_id=1, source_target_pairs={{8,0},{16,8},{24,16},{32,24},{40,32},{48,40},{56,48},{64,56},{72,6... | collective-permute-start | bytes 196616 | tf_op jit(solution)/shard_map/ppermute | solution.py:17
  12.9 4.4 %collective-permute-start = (bf16[1,16,8,256]{3,1,2,0:T(8,128)(2,1)S(1)}, bf16[1,16,8,256]{3,1,2,0:T(8,128)(2,1)S(1)}, u32[]{:S(2)}, u32[]{:S(2)}) collective-permute-start(bf16[1,16,8,256]{3,1,2,0:T(8,128)(2,1)S(1)} %get-tuple-element.64), channel_id=1, source_target_pairs={{0,8},{8,16},{16,24},{24,32},{32,40},{40,48},{48,56},{56,64},{64,7... | collective-permute-start | bytes 196616 | tf_op jit(solution)/shard_map/ppermute | solution.py:15
  17.4 5.9 %collective-permute-start.3 = (bf16[10,1,8,256]{3,1,2,0:T(2,128)(2,1)S(1)}, bf16[10,1,8,256]{3,1,2,0:T(2,128)(2,1)S(1)}, u32[]{:S(2)}, u32[]{:S(2)}) collective-permute-start(bf16[10,1,8,256]{3,1,2,0:T(2,128)(2,1)S(1)} %get-tuple-element.57), channel_id=1, source_target_pairs={{1,0},{2,1},{3,2},{4,3},{5,4},{6,5},{7,6},{9,8},{10,9},{11,10},{12... | collective-permute-start | bytes 122888 | tf_op jit(solution)/shard_map/ppermute | solution.py:17
  18.7 5.9 %collective-permute-start.2 = (bf16[10,1,8,256]{3,1,2,0:T(2,128)(2,1)S(1)}, bf16[10,1,8,256]{3,1,2,0:T(2,128)(2,1)S(1)}, u32[]{:S(2)}, u32[]{:S(2)}) collective-permute-start(bf16[10,1,8,256]{3,1,2,0:T(2,128)(2,1)S(1)} %get-tuple-element.56), channel_id=1, source_target_pairs={{0,1},{1,2},{2,3},{3,4},{4,5},{5,6},{6,7},{8,9},{9,10},{10,11},{11... | collective-permute-start | bytes 122888 | tf_op jit(solution)/shard_map/ppermute | solution.py:15
  31.8 2.0 copy-start
  41.1 1.0 copy-start.2
  43.8 34.6 %collective-permute-start.5 = (bf16[1,16,8,256]{3,1,2,0:T(8,128)(2,1)S(1)}, bf16[1,16,8,256]{3,1,2,0:T(8,128)(2,1)S(1)}, u32[]{:S(2)}, u32[]{:S(2)}) collective-permute-start(bf16[1,16,8,256]{3,1,2,0:T(8,128)(2,1)S(1)} %get-tuple-element.61), channel_id=1, source_target_pairs={{8,0},{16,8},{24,16},{32,24},{40,32},{48,40},{56,48},{64,56},{72,6... | collective-permute-start | bytes 196616 | tf_op jit(solution)/shard_map/ppermute | solution.py:17
  45.7 32.7 %collective-permute-start.4 = (bf16[1,16,8,256]{3,1,2,0:T(8,128)(2,1)S(1)}, bf16[1,16,8,256]{3,1,2,0:T(8,128)(2,1)S(1)}, u32[]{:S(2)}, u32[]{:S(2)}) collective-permute-start(bf16[1,16,8,256]{3,1,2,0:T(8,128)(2,1)S(1)} %get-tuple-element.60), channel_id=1, source_target_pairs={{0,8},{8,16},{16,24},{24,32},{32,40},{40,48},{48,56},{56,64},{64,7... | collective-permute-start | bytes 196616 | tf_op jit(solution)/shard_map/ppermute | solution.py:15
  78.6 6.4 %collective-permute-start.7 = (bf16[10,1,8,256]{3,1,2,0:T(2,128)(2,1)S(1)}, bf16[10,1,8,256]{3,1,2,0:T(2,128)(2,1)S(1)}, u32[]{:S(2)}, u32[]{:S(2)}) collective-permute-start(bf16[10,1,8,256]{3,1,2,0:T(2,128)(2,1)S(1)} %get-tuple-element.53), channel_id=1, source_target_pairs={{1,0},{2,1},{3,2},{4,3},{5,4},{6,5},{7,6},{9,8},{10,9},{11,10},{12... | collective-permute-start | bytes 122888 | tf_op jit(solution)/shard_map/ppermute | solution.py:17
  79.9 6.1 %collective-permute-start.6 = (bf16[10,1,8,256]{3,1,2,0:T(2,128)(2,1)S(1)}, bf16[10,1,8,256]{3,1,2,0:T(2,128)(2,1)S(1)}, u32[]{:S(2)}, u32[]{:S(2)}) collective-permute-start(bf16[10,1,8,256]{3,1,2,0:T(2,128)(2,1)S(1)} %get-tuple-element.52), channel_id=1, source_target_pairs={{0,1},{1,2},{2,3},{3,4},{4,5},{5,6},{6,7},{8,9},{9,10},{10,11},{11... | collective-permute-start | bytes 122888 | tf_op jit(solution)/shard_map/ppermute | solution.py:15
  86.7 2.6 copy-start.1
Sparse Core Ops, SparseCore 0:
  78.5 168.8 all-reduce.3
where the time goes:
time: 265 us; the launch traced here: 261 us
  waiting for transfers between devices  146 us (55%)
  matrix products  45.1 us (17%)
  starting transfers between devices  25 us (9%)
  local copies, waits for them, and re-layouts  23.5 us (9%)
  between operations  15.4 us (6%)
  other arithmetic  6.5 us (2%)
    psum x1, waiting for transfers between devices, reduce_grads(): return lax.psum(local_grads, ('gx', 'gy'))  143 us
    dot_general x27, matrix products, kernel_grads(): lax.dot_general(block, flat, (((0,), (0,)), ((), ())), preferred_element_...  28.3 us
    ppermute x4, starting transfers between devices, with_halo(): lax.ppermute(tail, axis, [(i, (i + 1) % count) for i in range(ends)])  17.1 us
    dot_general x27, matrix products, input_grads(): jnp.dot(piece, weights[index].T, preferred_element_type=jnp.float32)  8.87 us
    dot_general x27, matrix products, forward_conv(): jnp.dot(piece, weights[index], preferred_element_type=jnp.float32)  7.98 us
    ppermute x4, starting transfers between devices, with_halo(): lax.ppermute(head, axis, [((i + 1) % count, i) for i in range(ends)])  7.82 us
    slice x29, local copies, waits for them, and re-layouts, input_grads(): dextended[1 - ox:1 - ox + sx, 1 - oy:1 - oy + sy, 1 - oz:1 - oz + sz]  7.59 us
    unnamed x7, local copies, waits for them, and re-layouts  7.56 us
  transfers between devices with their start and end apart: 9, of which 4 were waited for; matrix products, arithmetic and copies ran while one was open for 18% of the time, Pallas kernels for 0%

commit v1 on v0

v1 whole, which is shorter than its diff:
```python
import functools

import jax
import jax.numpy as jnp
from jax import lax
from jax.experimental import pallas as pl
from jax.experimental.pallas import tpu as pltpu
from jax.sharding import PartitionSpec as P

AXES = ("gx", "gy")
F32, BF16 = jnp.float32, jnp.bfloat16
COUNT = 128
STAGES = ((0, 1), (1, 2), (2, 0))


def place(index):
    gx, gy = index // 8, index % 8
    return (gx // 2) % 4, (gx // 8) * 2 + gy // 4, gy % 4, gx % 2


def index_of(x, y, z, core):
    return ((y // 2) * 8 + x * 2 + core) * 8 + (y % 2) * 4 + z


def ring_pairs(stage, step):
    pairs = []
    for i in range(COUNT):
        *at, core = place(i)
        axis = STAGES[stage][core]
        at[axis] = (at[axis] + step) % 4
        pairs.append((i, index_of(*at, core)))
    return pairs


def core_pairs():
    return [(i, index_of(*place(i)[:3], 1 - place(i)[3])) for i in range(COUNT)]


def send(array, pairs):
    return lax.ppermute(array, AXES, pairs)


def where_am_i():
    gx, gy = lax.axis_index("gx"), lax.axis_index("gy")
    core = gx % 2
    at = jnp.stack([(gx // 2) % 4, (gx // 8) * 2 + gy // 4, gy % 4])
    mine = jnp.where(core == 0, at[STAGES[0][0]], at[STAGES[0][1]])
    other = jnp.where(core == 0, at[STAGES[0][1]], at[STAGES[0][0]])
    return jnp.stack([core, mine, other]).astype(jnp.int32)


def with_halo(cells, sides):
    for axis, dim in sides:
        count = lax.axis_size(axis)
        ends = count - 1
        head = lax.slice_in_dim(cells, 0, 1, axis=dim)
        tail = lax.slice_in_dim(cells, cells.shape[dim] - 1, cells.shape[dim], axis=dim)
        cells = jnp.concatenate(
            [
                lax.ppermute(tail, axis, [(i, i + 1) for i in range(ends)]),
                cells,
                lax.ppermute(head, axis, [(i + 1, i) for i in range(ends)]),
            ],
            axis=dim,
        )
    return cells


def three_views(cells):
    ext = with_halo(cells, (("gy", 1), ("gx", 0)))
    rows, wide, tall, chan = ext.shape
    return jnp.stack([ext[:, i : i + wide - 2].reshape(rows, (wide - 2) * tall, chan) for i in range(3)])


def roll_cells(field, step):
    cells, chan = field.shape
    tall = field.reshape(cells // 8, 8, chan)
    level = lax.broadcasted_iota(jnp.int32, tall.shape, 1)
    moved = pltpu.roll(tall, step % 8, 1)
    kept = jnp.where((level >= step) & (level < 8 + step), moved, 0.0)
    return kept.reshape(cells, chan)


def dsilu(pre):
    sig = jax.nn.sigmoid(pre)
    return sig * (1.0 + pre * (1.0 - sig))


def grads_kernel(at_ref, views, weights, mgrad, dpre, away, keep, shifted, turned):
    tile, chan = 256, 256
    lines = tile // 128

    for side in range(3):
        @pl.loop(0, 10)
        def _(row):
            turned[side, :, pl.ds(pl.multiple_of(row * 128, 128), 128)] = views[side, row].T

    @pl.loop(0, 8 // lines)
    def _(step):
        first = step * lines
        pieces = []
        for ox in range(3):
            for oy in range(3):
                pieces.append(views[oy, pl.ds(first + ox, lines)].reshape(tile, chan))
        left = jnp.concatenate(pieces, axis=1)
        pre = jnp.zeros((tile, chan), F32)
        for oz in range(3):
            part = jnp.dot(left, weights[:, oz].reshape(9 * chan, chan), preferred_element_type=F32)
            pre = pre + (part if oz == 1 else roll_cells(part, 1 - oz))
        here = pl.ds(pl.multiple_of(first * 128, tile), tile)
        value = (mgrad[here, :].astype(F32) * dsilu(pre)).astype(BF16)
        dpre[here, :] = value
        wide = value.astype(F32)
        shifted[here, 0:chan] = roll_cells(wide, -1).astype(BF16)
        shifted[here, chan : 2 * chan] = value
        shifted[here, 2 * chan : 3 * chan] = roll_cells(wide, 1).astype(BF16)

    core, mine, other = at_ref[0], at_ref[1], at_ref[2]

    for ox in range(3):
        @pl.loop(0, 3)
        def _(oy):
            rows = []
            for half, pos in ((core, mine), (1 - core, other)):
                for d in range(4):
                    start = pl.multiple_of(half * 128 + ((pos + d) & 3) * 32, 32)
                    rows.append(turned[oy, pl.ds(start, 32), ox * 128 : ox * 128 + 1024])
            left = jnp.concatenate(rows, axis=0)
            for oz in range(3):
                part = jnp.dot(left, shifted[:, oz * chan : (oz + 1) * chan], preferred_element_type=F32)
                keep[:, ox * 9 + oy * 3 + oz] = part[:128].reshape(4, 32, chan)
                away[:, ox * 9 + oy * 3 + oz] = part[128:].reshape(4, 32, chan).astype(BF16)


def input_kernel(views, weights, mask, out):
    tile, chan = 256, 256
    lines = tile // 128

    @pl.loop(0, 8 // lines)
    def _(step):
        first = step * lines
        pieces = []
        for ox in range(3):
            for oy in range(3):
                pieces.append(views[2 - oy, pl.ds(first + 2 - ox, lines)].reshape(tile, chan))
        left = jnp.concatenate(pieces, axis=1)
        total = jnp.zeros((tile, chan), F32)
        for oz in range(3):
            right = jnp.concatenate([weights[k, oz] for k in range(9)], axis=1)
            part = lax.dot_general(left, right, (((1,), (1,)), ((), ())), preferred_element_type=F32)
            total = total + (part if oz == 1 else roll_cells(part, oz - 1))
        here = pl.ds(pl.multiple_of(first * 128, tile), tile)
        out[here, :] = (total * mask[here, :]).astype(BF16)


def place_kernel(at_ref, *refs):
    pieces, out = refs[:8], refs[8]
    core, mine, other = at_ref[0], at_ref[1], at_ref[2]
    for d in range(4):
        for half, pos, piece in ((core, mine, pieces[d]), (1 - core, other, pieces[4 + d])):
            start = pl.multiple_of(half * 128 + ((pos - d) & 3) * 32, 32)
            out[:, pl.ds(start, 32), :] = piece[...].astype(F32)


VMEM = pl.BlockSpec(memory_space=pltpu.VMEM)
SMEM = pl.BlockSpec(memory_space=pltpu.SMEM)
PARAMS = dict(vmem_limit_bytes=36 * 2**20)


def local_grads(at, views, weights, mgrad):
    return pl.pallas_call(
        grads_kernel,
        out_shape=(
            jax.ShapeDtypeStruct((1024, 256), BF16),
            jax.ShapeDtypeStruct((4, 27, 32, 256), BF16),
            jax.ShapeDtypeStruct((4, 27, 32, 256), F32),
        ),
        in_specs=[SMEM, VMEM, VMEM, VMEM],
        out_specs=(VMEM, VMEM, VMEM),
        scratch_shapes=[pltpu.VMEM((1024, 768), BF16), pltpu.VMEM((3, 256, 1280), BF16)],
        compiler_params=pltpu.CompilerParams(**PARAMS),
        cost_estimate=pl.CostEstimate(flops=7_247_757_312, bytes_accessed=12_000_000, transcendentals=262144),
    )(at, views, weights, mgrad)


def input_grads(views, weights, mask):
    return pl.pallas_call(
        input_kernel,
        out_shape=jax.ShapeDtypeStruct((1024, 256), BF16),
        in_specs=[VMEM, VMEM, VMEM],
        out_specs=VMEM,
        compiler_params=pltpu.CompilerParams(**PARAMS),
        cost_estimate=pl.CostEstimate(flops=3_623_878_656, bytes_accessed=6_000_000, transcendentals=0),
    )(views, weights, mask)


def put_together(at, pieces):
    whole = pl.BlockSpec((9, 32, 256), lambda i: (i, 0, 0))
    return pl.pallas_call(
        place_kernel,
        grid=(3,),
        out_shape=jax.ShapeDtypeStruct((27, 256, 256), F32),
        in_specs=[SMEM] + [whole] * 8,
        out_specs=pl.BlockSpec((9, 256, 256), lambda i: (i, 0, 0)),
        compiler_params=pltpu.CompilerParams(**PARAMS),
        cost_estimate=pl.CostEstimate(flops=0, bytes_accessed=11_000_000, transcendentals=0),
    )(at, *pieces)


def from_ring(own, stage):
    one, two, three = (send(own, ring_pairs(stage, step)).astype(F32) for step in (1, 2, 3))
    return ((own.astype(F32) + two) + (one + three)).astype(BF16)


def all_sum(at, away, keep):
    both = keep + send(away, core_pairs()).astype(F32)
    got = [send(both[step].astype(BF16), ring_pairs(0, step)).astype(F32) for step in (1, 2, 3)]
    own = (both[0] + got[0] + got[1] + got[2]).astype(BF16)
    own = from_ring(own, 1)
    own = from_ring(own, 2)
    mine = [own] + [send(own, ring_pairs(0, step)) for step in (1, 2, 3)]
    other = [send(piece, core_pairs()) for piece in mine]
    return put_together(at, mine + other)


def local(features, grad_out, weights, occupied):
    at = where_am_i()
    cells = jnp.repeat(jnp.repeat(jnp.repeat(occupied, 4, axis=0), 4, axis=1), 4, axis=2)
    cellmask = cells.astype(BF16)[..., None]
    sx, sy, sz, chan = features.shape
    masked = features * cellmask
    mgrad = (grad_out * cellmask).reshape(-1, chan)
    packed = weights.reshape(9, 3, chan, chan)
    dpre, away, keep = local_grads(at, three_views(masked), packed, mgrad)
    grad_weights = all_sum(at, away, keep)
    mask = cells.astype(F32).reshape(-1, 1)
    grad_features = input_grads(three_views(dpre.reshape(masked.shape)), packed, mask)
    return grad_features.reshape(features.shape), grad_weights


def solution(mesh):
    return jax.shard_map(
        local,
        mesh=mesh,
        in_specs=(P("gx", "gy", None, None), P("gx", "gy", None, None), P(), P("gx", "gy", None)),
        out_specs=(P("gx", "gy", None, None), P()),
        check_vma=False,
    )
```

time: 265 us -> 129 us (0.49); the launches traced: 261 us -> 128 us
  waiting for transfers between devices: 146 us -> 40.6 us
  matrix products: 45.1 us -> 0 us
  starting transfers between devices: 25 us -> 55.2 us
  Pallas kernels: 0 us -> 21.6 us
  local copies, waits for them, and re-layouts: 23.5 us -> 5.01 us
  between operations: 15.4 us -> 0.99 us
    psum x1 -> x0, waiting for transfers between devices: 143 us -> none  [reduce_grads(): return lax.psum(local_grads, ('gx', 'gy'))]
    dot_general x81 -> x0, matrix products: 45.1 us -> none  [the longest x27 28.3 us: kernel_grads(): lax.dot_general(block, flat, (((0,), (0,)), ((), ())), preferred_element_...]
    ppermute x8 -> x25, waiting for transfers between devices: 3.26 us -> 40.6 us  [the longest x17 29.5 us: send(): return lax.ppermute(array, AXES, pairs)]
    ppermute x8 -> x25, starting transfers between devices: 24.9 us -> 55.2 us  [the longest x17 30.3 us: send(): return lax.ppermute(array, AXES, pairs)]
    pallas_call x0 -> x3, Pallas kernels: none -> 21.6 us  [the longest x1 12.6 us: local_grads(): pl.pallas_call(grads_kernel, out_shape=(jax.ShapeDtypeStruct((1024, 256),...]
    slice x59 -> x2, local copies, waits for them, and re-layouts: 15.1 us -> 0.01 us  [with_halo(): lax.slice_in_dim(cells, cells.shape[dim] - 1, cells.shape[dim], axis=dim)]
    unnamed x7 -> x5, local copies, waits for them, and re-layouts: 7.56 us -> 3.65 us
  transfers between devices with their start and end apart: 9 -> 25, of which waited for: 4 -> 11; matrix products, arithmetic and copies ran while one was open for 18% -> 1% of each run, Pallas kernels for 0% -> 4%
where the time goes in v1:
time: 129 us; the launch traced here: 128 us
  starting transfers between devices  55.2 us (43%)
  waiting for transfers between devices  40.6 us (31%)
  Pallas kernels  21.6 us (17%)
  local copies, waits for them, and re-layouts  5.01 us (4%)
  other arithmetic  4.86 us (4%)
    ppermute x17, starting transfers between devices, send(): return lax.ppermute(array, AXES, pairs)  30.3 us
    ppermute x17, waiting for transfers between devices, send(): return lax.ppermute(array, AXES, pairs)  29.5 us
    ppermute x4, starting transfers between devices, with_halo(): lax.ppermute(tail, axis, [(i, i + 1) for i in range(ends)])  18.5 us
    pallas_call x1, Pallas kernels, local_grads(): pl.pallas_call(grads_kernel, out_shape=(jax.ShapeDtypeStruct((1024, 256),...  12.6 us
    ppermute x4, waiting for transfers between devices, with_halo(): lax.ppermute(head, axis, [(i + 1, i) for i in range(ends)])  11.1 us
    ppermute x4, starting transfers between devices, with_halo(): lax.ppermute(head, axis, [(i + 1, i) for i in range(ends)])  6.43 us
    pallas_call x1, Pallas kernels, input_grads(): pl.pallas_call(input_kernel, out_shape=jax.ShapeDtypeStruct((1024, 256),...  5.29 us
    pallas_call x1, Pallas kernels, put_together(): pl.pallas_call(place_kernel, grid=(3,), out_shape=jax.ShapeDtypeStruct((2...  3.71 us
  transfers between devices with their start and end apart: 25, of which 11 were waited for; matrix products, arithmetic and copies ran while one was open for 1% of the time, Pallas kernels for 4%

profile of v1, /device:TPU:1, one launch (start us, length us, event | category | flops | bytes accessed | tf_op | source)
XLA Modules:
  0.0 128.2 jit_solution(4375291066374799088)
XLA Ops:
  1.9 1.4 %broadcast_multiply_fusion = (bf16[8,16,8,256]{3,2,1,0:T(8,128)(2,1)S(1)}, bf16[8,16,8,256]{3,2,1,0:T(8,128)(2,1)S(1)}) fusion(bf16[8,16,8,256]{3,2,1,0:T(8,128)(2,1)} %param.5, bf16[8,16,8]{2,1,0:T(8,128)(2,1)S(1)} %copy.19, bf16[8,16,8,256]{3,2,1,0:T(8,128)(2,1)} %param.4), kind=kLoop, calls=%fused_computation.21 | loop fusion | flops 524288 | bytes 2099200 | tf_op jit(solution)/shard_map/mul | solution.py:232
  3.3 4.4 %collective-permute-start = (bf16[8,1,8,256]{3,2,1,0:T(8,128)(2,1)S(1)}, bf16[8,1,8,256]{3,2,1,0:T(8,128)(2,1)S(1)}, u32[]{:S(2)}, u32[]{:S(2)}) collective-permute-start(bf16[8,1,8,256]{3,2,1,0:T(8,128)(2,1)S(1)} %get-tuple-element.25), channel_id=1, source_target_pairs={{0,1},{1,2},{2,3},{3,4},{4,5},{5,6},{6,7},{8,9},{9,10},{10,11},{11... | collective-permute-start | bytes 98312 | tf_op jit(solution)/shard_map/ppermute | solution.py:60
  9.1 3.5 %collective-permute-done.1 = bf16[8,1,8,256]{3,2,1,0:T(8,128)(2,1)S(1)} collective-permute-done((bf16[8,1,8,256]{3,2,1,0:T(8,128)(2,1)S(1)}, bf16[8,1,8,256]{3,2,1,0:T(8,128)(2,1)S(1)}, u32[]{:S(2)}, u32[]{:S(2)}) %collective-permute-start.1) | collective-permute-done | bytes 32800 | tf_op jit(solution)/shard_map/ppermute | solution.py:62
  12.6 4.9 %collective-permute-start.2 = (bf16[1,18,8,256]{3,2,1,0:T(8,128)(2,1)S(1)}, bf16[1,18,8,256]{3,2,1,0:T(8,128)(2,1)S(1)}, u32[]{:S(2)}, u32[]{:S(2)}) collective-permute-start(bf16[1,18,8,256]{3,2,1,0:T(8,128)(2,1)S(1)} %get-tuple-element.21), channel_id=1, source_target_pairs={{0,8},{8,16},{16,24},{24,32},{32,40},{40,48},{48,56},{56,64},{64,7... | collective-permute-start | bytes 221192 | tf_op jit(solution)/shard_map/ppermute | solution.py:60
  17.5 1.9 %collective-permute-start.3 = (bf16[1,18,8,256]{3,2,1,0:T(8,128)(2,1)S(1)}, bf16[1,18,8,256]{3,2,1,0:T(8,128)(2,1)S(1)}, u32[]{:S(2)}, u32[]{:S(2)}) collective-permute-start(bf16[1,18,8,256]{3,2,1,0:T(8,128)(2,1)S(1)} %get-tuple-element.22), channel_id=1, source_target_pairs={{8,0},{16,8},{24,16},{32,24},{40,32},{48,40},{56,48},{64,56},{72,6... | collective-permute-start | bytes 221192 | tf_op jit(solution)/shard_map/ppermute | solution.py:62
  19.5 3.7 %collective-permute-done.3 = bf16[1,18,8,256]{3,2,1,0:T(8,128)(2,1)S(1)} collective-permute-done((bf16[1,18,8,256]{3,2,1,0:T(8,128)(2,1)S(1)}, bf16[1,18,8,256]{3,2,1,0:T(8,128)(2,1)S(1)}, u32[]{:S(2)}, u32[]{:S(2)}) %collective-permute-start.3) | collective-permute-done | bytes 73760 | tf_op jit(solution)/shard_map/ppermute | solution.py:62
  23.7 1.8 %copy-done = bf16[27,256,256]{2,1,0:T(8,128)(2,1)S(1)} copy-done((bf16[27,256,256]{2,1,0:T(8,128)(2,1)S(1)}, bf16[27,256,256]{2,1,0:T(8,128)(2,1)}, u32[]{:S(2)}) %copy-start) | copy-done | bytes 3538968
  25.5 12.6 %shard_map.59 = (bf16[1024,256]{1,0:T(8,128)(2,1)S(1)}, bf16[4,27,32,256]{3,2,1,0:T(8,128)(2,1)S(1)}, f32[4,27,32,256]{3,2,1,0:T(8,128)S(1)}) custom-call(s32[3]{0:T(128)S(1)} %pad_add_fusion.at_ref, bf16[3,10,128,256]{3,2,1,0:T(8,128)(2,1)S(1)} %pad_maximum_fusion.views, bf16[9,3,256,256]{3,2,1,0:T(8,128)(2,1)S(1)} %bitcast.45, bf16[1024,256]{1,0:T(8,128)(2,1)S(1)} %bitcast.44), custom_call_target="tpu_custom_call" | custom-call | flops 7247757312 | bytes 12000000 | tf_op jit(solution)/shard_map/pallas_call | solution.py:171
  38.2 3.7 %collective-permute-done.8 = bf16[4,27,32,256]{3,2,1,0:T(8,128)(2,1)S(1)} collective-permute-done((bf16[4,27,32,256]{3,2,1,0:T(8,128)(2,1)S(1)}, bf16[4,27,32,256]{3,2,1,0:T(8,128)(2,1)S(1)}, u32[]{:S(2)}, u32[]{:S(2)}) %collective-permute-start.8) | collective-permute-done | bytes 1769504 | tf_op jit(solution)/shard_map/ppermute | solution.py:40
  42.9 1.4 %collective-permute-start.9 = (bf16[27,32,256]{2,1,0:T(8,128)(2,1)S(1)}, bf16[27,32,256]{2,1,0:T(8,128)(2,1)S(1)}, u32[]{:S(2)}, u32[]{:S(2)}) collective-permute-start(bf16[27,32,256]{2,1,0:T(8,128)(2,1)S(1)} %get-tuple-element.10), channel_id=1, source_target_pairs={{0,16},{1,17},{2,18},{3,19},{4,20},{5,21},{6,22},{7,23},{8,12},{9,... | collective-permute-start | bytes 1327112 | tf_op jit(solution)/shard_map/ppermute | solution.py:40
  44.3 3.6 %collective-permute-start.11 = (bf16[27,32,256]{2,1,0:T(8,128)(2,1)S(1)}, bf16[27,32,256]{2,1,0:T(8,128)(2,1)S(1)}, u32[]{:S(2)}, u32[]{:S(2)}) collective-permute-start(bf16[27,32,256]{2,1,0:T(8,128)(2,1)S(1)} %get-tuple-element.11), channel_id=1, source_target_pairs={{0,48},{1,49},{2,50},{3,51},{4,52},{5,53},{6,54},{7,55},{8,76},{9,... | collective-permute-start | bytes 1327112 | tf_op jit(solution)/shard_map/ppermute | solution.py:40
  47.9 1.6 %collective-permute-start.10 = (bf16[27,32,256]{2,1,0:T(8,128)(2,1)S(1)}, bf16[27,32,256]{2,1,0:T(8,128)(2,1)S(1)}, u32[]{:S(2)}, u32[]{:S(2)}) collective-permute-start(bf16[27,32,256]{2,1,0:T(8,128)(2,1)S(1)} %get-tuple-element.12), channel_id=1, source_target_pairs={{0,32},{1,33},{2,34},{3,35},{4,36},{5,37},{6,38},{7,39},{8,72},{9,... | collective-permute-start | bytes 1327112 | tf_op jit(solution)/shard_map/ppermute | solution.py:40
  49.5 4.3 %collective-permute-done.9 = bf16[27,32,256]{2,1,0:T(8,128)(2,1)S(1)} collective-permute-done((bf16[27,32,256]{2,1,0:T(8,128)(2,1)S(1)}, bf16[27,32,256]{2,1,0:T(8,128)(2,1)S(1)}, u32[]{:S(2)}, u32[]{:S(2)}) %collective-permute-start.9) | collective-permute-done | bytes 442400 | tf_op jit(solution)/shard_map/ppermute | solution.py:40
  53.8 4.1 %collective-permute-done.11 = bf16[27,32,256]{2,1,0:T(8,128)(2,1)S(1)} collective-permute-done((bf16[27,32,256]{2,1,0:T(8,128)(2,1)S(1)}, bf16[27,32,256]{2,1,0:T(8,128)(2,1)S(1)}, u32[]{:S(2)}, u32[]{:S(2)}) %collective-permute-start.11) | collective-permute-done | bytes 442400 | tf_op jit(solution)/shard_map/ppermute | solution.py:40
  57.9 1.8 %collective-permute-done.10 = bf16[27,32,256]{2,1,0:T(8,128)(2,1)S(1)} collective-permute-done((bf16[27,32,256]{2,1,0:T(8,128)(2,1)S(1)}, bf16[27,32,256]{2,1,0:T(8,128)(2,1)S(1)}, u32[]{:S(2)}, u32[]{:S(2)}) %collective-permute-start.10) | collective-permute-done | bytes 442400 | tf_op jit(solution)/shard_map/ppermute | solution.py:40
  60.0 3.0 %collective-permute-start.14 = (bf16[27,32,256]{2,1,0:T(8,128)(2,1)S(1)}, bf16[27,32,256]{2,1,0:T(8,128)(2,1)S(1)}, u32[]{:S(2)}, u32[]{:S(2)}) collective-permute-start(bf16[27,32,256]{2,1,0:T(8,128)(2,1)S(1)} %fusion.3), channel_id=1, source_target_pairs={{0,68},{1,69},{2,70},{3,71},{4,0},{5,1},{6,2},{7,3},{8,11},{9,8},{... | collective-permute-start | bytes 1327112 | tf_op jit(solution)/shard_map/ppermute | solution.py:40
  63.1 1.8 %collective-permute-start.12 = (bf16[27,32,256]{2,1,0:T(8,128)(2,1)S(1)}, bf16[27,32,256]{2,1,0:T(8,128)(2,1)S(1)}, u32[]{:S(2)}, u32[]{:S(2)}) collective-permute-start(bf16[27,32,256]{2,1,0:T(8,128)(2,1)S(1)} %fusion.3), channel_id=1, source_target_pairs={{0,64},{1,65},{2,66},{3,67},{4,68},{5,69},{6,70},{7,71},{8,10},{9,... | collective-permute-start | bytes 1327112 | tf_op jit(solution)/shard_map/ppermute | solution.py:40
  64.9 8.2 %collective-permute-done.14 = bf16[27,32,256]{2,1,0:T(8,128)(2,1)S(1)} collective-permute-done((bf16[27,32,256]{2,1,0:T(8,128)(2,1)S(1)}, bf16[27,32,256]{2,1,0:T(8,128)(2,1)S(1)}, u32[]{:S(2)}, u32[]{:S(2)}) %collective-permute-start.14) | collective-permute-done | bytes 442400 | tf_op jit(solution)/shard_map/ppermute | solution.py:40
  73.1 3.4 %collective-permute-done.13 = bf16[27,32,256]{2,1,0:T(8,128)(2,1)S(1)} collective-permute-done((bf16[27,32,256]{2,1,0:T(8,128)(2,1)S(1)}, bf16[27,32,256]{2,1,0:T(8,128)(2,1)S(1)}, u32[]{:S(2)}, u32[]{:S(2)}) %collective-permute-start.13) | collective-permute-done | bytes 442400 | tf_op jit(solution)/shard_map/ppermute | solution.py:40
  76.8 5.2 %collective-permute-start.17 = (bf16[27,32,256]{2,1,0:T(8,128)(2,1)S(1)}, bf16[27,32,256]{2,1,0:T(8,128)(2,1)S(1)}, u32[]{:S(2)}, u32[]{:S(2)}) collective-permute-start(bf16[27,32,256]{2,1,0:T(8,128)(2,1)S(1)} %add_convert_fusion.1), channel_id=1, source_target_pairs={{0,3},{1,0},{2,1},{3,2},{4,7},{5,4},{6,5},{7,6},{8,56},{9,57},{10,... | collective-permute-start | bytes 1327112 | tf_op jit(solution)/shard_map/ppermute | solution.py:40
  84.5 1.3 %collective-permute-start.5 = (bf16[8,1,8,256]{3,2,1,0:T(8,128)(2,1)S(1)}, bf16[8,1,8,256]{3,2,1,0:T(8,128)(2,1)S(1)}, u32[]{:S(2)}, u32[]{:S(2)}) collective-permute-start(bf16[8,1,8,256]{3,2,1,0:T(8,128)(2,1)S(1)} %get-tuple-element.24), channel_id=1, source_target_pairs={{1,0},{2,1},{3,2},{4,3},{5,4},{6,5},{7,6},{9,8},{10,9},{11,10},{12... | collective-permute-start | bytes 98312 | tf_op jit(solution)/shard_map/ppermute | solution.py:62
  85.8 4.0 %collective-permute-done.5 = bf16[8,1,8,256]{3,2,1,0:T(8,128)(2,1)S(1)} collective-permute-done((bf16[8,1,8,256]{3,2,1,0:T(8,128)(2,1)S(1)}, bf16[8,1,8,256]{3,2,1,0:T(8,128)(2,1)S(1)}, u32[]{:S(2)}, u32[]{:S(2)}) %collective-permute-start.5) | collective-permute-done | bytes 32800 | tf_op jit(solution)/shard_map/ppermute | solution.py:62
  89.8 7.9 %collective-permute-start.6 = (bf16[1,18,8,256]{3,2,1,0:T(8,128)(2,1)S(1)}, bf16[1,18,8,256]{3,2,1,0:T(8,128)(2,1)S(1)}, u32[]{:S(2)}, u32[]{:S(2)}) collective-permute-start(bf16[1,18,8,256]{3,2,1,0:T(8,128)(2,1)S(1)} %get-tuple-element.19), channel_id=1, source_target_pairs={{0,8},{8,16},{16,24},{24,32},{32,40},{40,48},{48,56},{56,64},{64,7... | collective-permute-start | bytes 221192 | tf_op jit(solution)/shard_map/ppermute | solution.py:60
  97.7 1.9 %collective-permute-start.7 = (bf16[1,18,8,256]{3,2,1,0:T(8,128)(2,1)S(1)}, bf16[1,18,8,256]{3,2,1,0:T(8,128)(2,1)S(1)}, u32[]{:S(2)}, u32[]{:S(2)}) collective-permute-start(bf16[1,18,8,256]{3,2,1,0:T(8,128)(2,1)S(1)} %get-tuple-element.20), channel_id=1, source_target_pairs={{8,0},{16,8},{24,16},{32,24},{40,32},{48,40},{56,48},{64,56},{72,6... | collective-permute-start | bytes 221192 | tf_op jit(solution)/shard_map/ppermute | solution.py:62
  103.7 1.5 %collective-permute-start.21 = (bf16[27,32,256]{2,1,0:T(8,128)(2,1)S(1)}, bf16[27,32,256]{2,1,0:T(8,128)(2,1)S(1)}, u32[]{:S(2)}, u32[]{:S(2)}) collective-permute-start(bf16[27,32,256]{2,1,0:T(8,128)(2,1)S(1)} %add_convert_fusion.refs_0_), channel_id=1, source_target_pairs={{0,8},{1,9},{2,10},{3,11},{4,12},{5,13},{6,14},{7,15},{8,0},{9,1},... | collective-permute-start | bytes 1327112 | tf_op jit(solution)/shard_map/ppermute | solution.py:40
  105.2 2.3 %collective-permute-done.20.refs_3_ = bf16[27,32,256]{2,1,0:T(8,128)(2,1)S(1)} collective-permute-done((bf16[27,32,256]{2,1,0:T(8,128)(2,1)S(1)}, bf16[27,32,256]{2,1,0:T(8,128)(2,1)S(1)}, u32[]{:S(2)}, u32[]{:S(2)}) %collective-permute-start.20) | collective-permute-done | bytes 442400 | tf_op jit(solution)/shard_map/ppermute | solution.py:40
  107.5 5.7 %collective-permute-start.24 = (bf16[27,32,256]{2,1,0:T(8,128)(2,1)S(1)}, bf16[27,32,256]{2,1,0:T(8,128)(2,1)S(1)}, u32[]{:S(2)}, u32[]{:S(2)}) collective-permute-start(bf16[27,32,256]{2,1,0:T(8,128)(2,1)S(1)} %collective-permute-done.20.refs_3_), channel_id=1, source_target_pairs={{0,8},{1,9},{2,10},{3,11},{4,12},{5,13},{6,14},{7,15},{8,0},{9,1},... | collective-permute-start | bytes 1327112 | tf_op jit(solution)/shard_map/ppermute | solution.py:40
  113.2 1.6 %collective-permute-done.18.refs_1_ = bf16[27,32,256]{2,1,0:T(8,128)(2,1)S(1)} collective-permute-done((bf16[27,32,256]{2,1,0:T(8,128)(2,1)S(1)}, bf16[27,32,256]{2,1,0:T(8,128)(2,1)S(1)}, u32[]{:S(2)}, u32[]{:S(2)}) %collective-permute-start.18) | collective-permute-done | bytes 442400 | tf_op jit(solution)/shard_map/ppermute | solution.py:40
  114.8 2.3 %collective-permute-start.22 = (bf16[27,32,256]{2,1,0:T(8,128)(2,1)S(1)}, bf16[27,32,256]{2,1,0:T(8,128)(2,1)S(1)}, u32[]{:S(2)}, u32[]{:S(2)}) collective-permute-start(bf16[27,32,256]{2,1,0:T(8,128)(2,1)S(1)} %collective-permute-done.18.refs_1_), channel_id=1, source_target_pairs={{0,8},{1,9},{2,10},{3,11},{4,12},{5,13},{6,14},{7,15},{8,0},{9,1},... | collective-permute-start | bytes 1327112 | tf_op jit(solution)/shard_map/ppermute | solution.py:40
  117.4 1.8 %copy-done.1 = bf16[27,256,256]{2,1,0:T(8,128)(2,1)S(1)} copy-done((bf16[27,256,256]{2,1,0:T(8,128)(2,1)S(1)}, bf16[27,256,256]{2,1,0:T(8,128)(2,1)}, u32[]{:S(2)}) %copy-start.1) | copy-done | bytes 3538968
  119.2 5.3 %shard_map.60 = bf16[1024,256]{1,0:T(8,128)(2,1)} custom-call(bf16[3,10,128,256]{3,2,1,0:T(8,128)(2,1)S(1)} %pad_maximum_fusion.1.views, bf16[9,3,256,256]{3,2,1,0:T(8,128)(2,1)S(1)} %bitcast.46, f32[1024,1]{1,0:T(8,128)S(1)} %convert_element_type.124.mask), custom_call_target="tpu_custom_call" | custom-call | flops 3623878656 | bytes 6000000 | tf_op jit(solution)/shard_map/pallas_call | solution.py:187
  124.5 3.7 %shard_map.61 = f32[27,256,256]{2,1,0:T(8,128)} custom-call(s32[3]{0:T(128)S(1)} %pad_add_fusion.at_ref, bf16[27,32,256]{2,1,0:T(8,128)(2,1)S(1)} %add_convert_fusion.refs_0_, bf16[27,32,256]{2,1,0:T(8,128)(2,1)S(1)} %collective-permute-done.18.refs_1_, bf16[27,32,256]{2,1,0:T(8,128)(2,1)S(1)} %collective-permute-done.19.refs_2_, ...), custom_call_target="tpu_custom_call" | custom-call | bytes 11000000 | tf_op jit(solution)/shard_map/pallas_call | solution.py:199
  (56 shorter events, 11.8 us)
Async XLA Ops:
  3.3 5.7 %collective-permute-start = (bf16[8,1,8,256]{3,2,1,0:T(8,128)(2,1)S(1)}, bf16[8,1,8,256]{3,2,1,0:T(8,128)(2,1)S(1)}, u32[]{:S(2)}, u32[]{:S(2)}) collective-permute-start(bf16[8,1,8,256]{3,2,1,0:T(8,128)(2,1)S(1)} %get-tuple-element.25), channel_id=1, source_target_pairs={{0,1},{1,2},{2,3},{3,4},{4,5},{5,6},{6,7},{8,9},{9,10},{10,11},{11... | collective-permute-start | bytes 98312 | tf_op jit(solution)/shard_map/ppermute | solution.py:60
  7.7 4.8 %collective-permute-start.1 = (bf16[8,1,8,256]{3,2,1,0:T(8,128)(2,1)S(1)}, bf16[8,1,8,256]{3,2,1,0:T(8,128)(2,1)S(1)}, u32[]{:S(2)}, u32[]{:S(2)}) collective-permute-start(bf16[8,1,8,256]{3,2,1,0:T(8,128)(2,1)S(1)} %get-tuple-element.26), channel_id=1, source_target_pairs={{1,0},{2,1},{3,2},{4,3},{5,4},{6,5},{7,6},{9,8},{10,9},{11,10},{12... | collective-permute-start | bytes 98312 | tf_op jit(solution)/shard_map/ppermute | solution.py:62
  12.6 6.9 %collective-permute-start.2 = (bf16[1,18,8,256]{3,2,1,0:T(8,128)(2,1)S(1)}, bf16[1,18,8,256]{3,2,1,0:T(8,128)(2,1)S(1)}, u32[]{:S(2)}, u32[]{:S(2)}) collective-permute-start(bf16[1,18,8,256]{3,2,1,0:T(8,128)(2,1)S(1)} %get-tuple-element.21), channel_id=1, source_target_pairs={{0,8},{8,16},{16,24},{24,32},{32,40},{40,48},{48,56},{56,64},{64,7... | collective-permute-start | bytes 221192 | tf_op jit(solution)/shard_map/ppermute | solution.py:60
  17.5 5.7 %collective-permute-start.3 = (bf16[1,18,8,256]{3,2,1,0:T(8,128)(2,1)S(1)}, bf16[1,18,8,256]{3,2,1,0:T(8,128)(2,1)S(1)}, u32[]{:S(2)}, u32[]{:S(2)}) collective-permute-start(bf16[1,18,8,256]{3,2,1,0:T(8,128)(2,1)S(1)} %get-tuple-element.22), channel_id=1, source_target_pairs={{8,0},{16,8},{24,16},{32,24},{40,32},{48,40},{56,48},{64,56},{72,6... | collective-permute-start | bytes 221192 | tf_op jit(solution)/shard_map/ppermute | solution.py:62
  23.5 2.0 %copy-start = (bf16[27,256,256]{2,1,0:T(8,128)(2,1)S(1)}, bf16[27,256,256]{2,1,0:T(8,128)(2,1)}, u32[]{:S(2)}) copy-start(bf16[27,256,256]{2,1,0:T(8,128)(2,1)} %param.6) | copy-start | bytes 10616836
  38.1 3.8 %collective-permute-start.8 = (bf16[4,27,32,256]{3,2,1,0:T(8,128)(2,1)S(1)}, bf16[4,27,32,256]{3,2,1,0:T(8,128)(2,1)S(1)}, u32[]{:S(2)}, u32[]{:S(2)}) collective-permute-start(bf16[4,27,32,256]{3,2,1,0:T(8,128)(2,1)S(1)} %get-tuple-element.7), channel_id=1, source_target_pairs={{0,8},{1,9},{2,10},{3,11},{4,12},{5,13},{6,14},{7,15},{8,0},{9,1},... | collective-permute-start | bytes 5308424 | tf_op jit(solution)/shard_map/ppermute | solution.py:40
  42.9 10.9 %collective-permute-start.9 = (bf16[27,32,256]{2,1,0:T(8,128)(2,1)S(1)}, bf16[27,32,256]{2,1,0:T(8,128)(2,1)S(1)}, u32[]{:S(2)}, u32[]{:S(2)}) collective-permute-start(bf16[27,32,256]{2,1,0:T(8,128)(2,1)S(1)} %get-tuple-element.10), channel_id=1, source_target_pairs={{0,16},{1,17},{2,18},{3,19},{4,20},{5,21},{6,22},{7,23},{8,12},{9,... | collective-permute-start | bytes 1327112 | tf_op jit(solution)/shard_map/ppermute | solution.py:40
  44.3 13.6 %collective-permute-start.11 = (bf16[27,32,256]{2,1,0:T(8,128)(2,1)S(1)}, bf16[27,32,256]{2,1,0:T(8,128)(2,1)S(1)}, u32[]{:S(2)}, u32[]{:S(2)}) collective-permute-start(bf16[27,32,256]{2,1,0:T(8,128)(2,1)S(1)} %get-tuple-element.11), channel_id=1, source_target_pairs={{0,48},{1,49},{2,50},{3,51},{4,52},{5,53},{6,54},{7,55},{8,76},{9,... | collective-permute-start | bytes 1327112 | tf_op jit(solution)/shard_map/ppermute | solution.py:40
  47.9 11.8 %collective-permute-start.10 = (bf16[27,32,256]{2,1,0:T(8,128)(2,1)S(1)}, bf16[27,32,256]{2,1,0:T(8,128)(2,1)S(1)}, u32[]{:S(2)}, u32[]{:S(2)}) collective-permute-start(bf16[27,32,256]{2,1,0:T(8,128)(2,1)S(1)} %get-tuple-element.12), channel_id=1, source_target_pairs={{0,32},{1,33},{2,34},{3,35},{4,36},{5,37},{6,38},{7,39},{8,72},{9,... | collective-permute-start | bytes 1327112 | tf_op jit(solution)/shard_map/ppermute | solution.py:40
  60.0 13.0 %collective-permute-start.14 = (bf16[27,32,256]{2,1,0:T(8,128)(2,1)S(1)}, bf16[27,32,256]{2,1,0:T(8,128)(2,1)S(1)}, u32[]{:S(2)}, u32[]{:S(2)}) collective-permute-start(bf16[27,32,256]{2,1,0:T(8,128)(2,1)S(1)} %fusion.3), channel_id=1, source_target_pairs={{0,68},{1,69},{2,70},{3,71},{4,0},{5,1},{6,2},{7,3},{8,11},{9,8},{... | collective-permute-start | bytes 1327112 | tf_op jit(solution)/shard_map/ppermute | solution.py:40
  63.1 13.4 %collective-permute-start.13 = (bf16[27,32,256]{2,1,0:T(8,128)(2,1)S(1)}, bf16[27,32,256]{2,1,0:T(8,128)(2,1)S(1)}, u32[]{:S(2)}, u32[]{:S(2)}) collective-permute-start(bf16[27,32,256]{2,1,0:T(8,128)(2,1)S(1)} %fusion.3), channel_id=1, source_target_pairs={{0,4},{1,5},{2,6},{3,7},{4,64},{5,65},{6,66},{7,67},{8,9},{9,10},{... | collective-permute-start | bytes 1327112 | tf_op jit(solution)/shard_map/ppermute | solution.py:40
  63.1 13.4 %collective-permute-start.12 = (bf16[27,32,256]{2,1,0:T(8,128)(2,1)S(1)}, bf16[27,32,256]{2,1,0:T(8,128)(2,1)S(1)}, u32[]{:S(2)}, u32[]{:S(2)}) collective-permute-start(bf16[27,32,256]{2,1,0:T(8,128)(2,1)S(1)} %fusion.3), channel_id=1, source_target_pairs={{0,64},{1,65},{2,66},{3,67},{4,68},{5,69},{6,70},{7,71},{8,10},{9,... | collective-permute-start | bytes 1327112 | tf_op jit(solution)/shard_map/ppermute | solution.py:40
  76.8 22.9 %collective-permute-start.17 = (bf16[27,32,256]{2,1,0:T(8,128)(2,1)S(1)}, bf16[27,32,256]{2,1,0:T(8,128)(2,1)S(1)}, u32[]{:S(2)}, u32[]{:S(2)}) collective-permute-start(bf16[27,32,256]{2,1,0:T(8,128)(2,1)S(1)} %add_convert_fusion.1), channel_id=1, source_target_pairs={{0,3},{1,0},{2,1},{3,2},{4,7},{5,4},{6,5},{7,6},{8,56},{9,57},{10,... | collective-permute-start | bytes 1327112 | tf_op jit(solution)/shard_map/ppermute | solution.py:40
  81.9 17.7 %collective-permute-start.16 = (bf16[27,32,256]{2,1,0:T(8,128)(2,1)S(1)}, bf16[27,32,256]{2,1,0:T(8,128)(2,1)S(1)}, u32[]{:S(2)}, u32[]{:S(2)}) collective-permute-start(bf16[27,32,256]{2,1,0:T(8,128)(2,1)S(1)} %add_convert_fusion.1), channel_id=1, source_target_pairs={{0,1},{1,2},{2,3},{3,0},{4,5},{5,6},{6,7},{7,4},{8,24},{9,25},{10,... | collective-permute-start | bytes 1327112 | tf_op jit(solution)/shard_map/ppermute | solution.py:40
  81.9 17.7 %collective-permute-start.15 = (bf16[27,32,256]{2,1,0:T(8,128)(2,1)S(1)}, bf16[27,32,256]{2,1,0:T(8,128)(2,1)S(1)}, u32[]{:S(2)}, u32[]{:S(2)}) collective-permute-start(bf16[27,32,256]{2,1,0:T(8,128)(2,1)S(1)} %add_convert_fusion.1), channel_id=1, source_target_pairs={{0,2},{1,3},{2,0},{3,1},{4,6},{5,7},{6,4},{7,5},{8,40},{9,41},{10,... | collective-permute-start | bytes 1327112 | tf_op jit(solution)/shard_map/ppermute | solution.py:40
  83.2 2.6 %collective-permute-start.4 = (bf16[8,1,8,256]{3,2,1,0:T(8,128)(2,1)S(1)}, bf16[8,1,8,256]{3,2,1,0:T(8,128)(2,1)S(1)}, u32[]{:S(2)}, u32[]{:S(2)}) collective-permute-start(bf16[8,1,8,256]{3,2,1,0:T(8,128)(2,1)S(1)} %get-tuple-element.23), channel_id=1, source_target_pairs={{0,1},{1,2},{2,3},{3,4},{4,5},{5,6},{6,7},{8,9},{9,10},{10,11},{11... | collective-permute-start | bytes 98312 | tf_op jit(solution)/shard_map/ppermute | solution.py:60
  84.5 5.3 %collective-permute-start.5 = (bf16[8,1,8,256]{3,2,1,0:T(8,128)(2,1)S(1)}, bf16[8,1,8,256]{3,2,1,0:T(8,128)(2,1)S(1)}, u32[]{:S(2)}, u32[]{:S(2)}) collective-permute-start(bf16[8,1,8,256]{3,2,1,0:T(8,128)(2,1)S(1)} %get-tuple-element.24), channel_id=1, source_target_pairs={{1,0},{2,1},{3,2},{4,3},{5,4},{6,5},{7,6},{9,8},{10,9},{11,10},{12... | collective-permute-start | bytes 98312 | tf_op jit(solution)/shard_map/ppermute | solution.py:62
  89.8 13.6 %collective-permute-start.6 = (bf16[1,18,8,256]{3,2,1,0:T(8,128)(2,1)S(1)}, bf16[1,18,8,256]{3,2,1,0:T(8,128)(2,1)S(1)}, u32[]{:S(2)}, u32[]{:S(2)}) collective-permute-start(bf16[1,18,8,256]{3,2,1,0:T(8,128)(2,1)S(1)} %get-tuple-element.19), channel_id=1, source_target_pairs={{0,8},{8,16},{16,24},{24,32},{32,40},{40,48},{48,56},{56,64},{64,7... | collective-permute-start | bytes 221192 | tf_op jit(solution)/shard_map/ppermute | solution.py:60
  97.7 5.7 %collective-permute-start.7 = (bf16[1,18,8,256]{3,2,1,0:T(8,128)(2,1)S(1)}, bf16[1,18,8,256]{3,2,1,0:T(8,128)(2,1)S(1)}, u32[]{:S(2)}, u32[]{:S(2)}) collective-permute-start(bf16[1,18,8,256]{3,2,1,0:T(8,128)(2,1)S(1)} %get-tuple-element.20), channel_id=1, source_target_pairs={{8,0},{16,8},{24,16},{32,24},{40,32},{48,40},{56,48},{64,56},{72,6... | collective-permute-start | bytes 221192 | tf_op jit(solution)/shard_map/ppermute | solution.py:62
  100.0 7.5 %collective-permute-start.20 = (bf16[27,32,256]{2,1,0:T(8,128)(2,1)S(1)}, bf16[27,32,256]{2,1,0:T(8,128)(2,1)S(1)}, u32[]{:S(2)}, u32[]{:S(2)}) collective-permute-start(bf16[27,32,256]{2,1,0:T(8,128)(2,1)S(1)} %add_convert_fusion.refs_0_), channel_id=1, source_target_pairs={{0,48},{1,49},{2,50},{3,51},{4,52},{5,53},{6,54},{7,55},{8,76},{9,... | collective-permute-start | bytes 1327112 | tf_op jit(solution)/shard_map/ppermute | solution.py:40
  101.2 12.1 %collective-permute-start.19 = (bf16[27,32,256]{2,1,0:T(8,128)(2,1)S(1)}, bf16[27,32,256]{2,1,0:T(8,128)(2,1)S(1)}, u32[]{:S(2)}, u32[]{:S(2)}) collective-permute-start(bf16[27,32,256]{2,1,0:T(8,128)(2,1)S(1)} %add_convert_fusion.refs_0_), channel_id=1, source_target_pairs={{0,32},{1,33},{2,34},{3,35},{4,36},{5,37},{6,38},{7,39},{8,72},{9,... | collective-permute-start | bytes 1327112 | tf_op jit(solution)/shard_map/ppermute | solution.py:40
  102.1 12.7 %collective-permute-start.18 = (bf16[27,32,256]{2,1,0:T(8,128)(2,1)S(1)}, bf16[27,32,256]{2,1,0:T(8,128)(2,1)S(1)}, u32[]{:S(2)}, u32[]{:S(2)}) collective-permute-start(bf16[27,32,256]{2,1,0:T(8,128)(2,1)S(1)} %add_convert_fusion.refs_0_), channel_id=1, source_target_pairs={{0,16},{1,17},{2,18},{3,19},{4,20},{5,21},{6,22},{7,23},{8,12},{9,... | collective-permute-start | bytes 1327112 | tf_op jit(solution)/shard_map/ppermute | solution.py:40
  103.7 20.7 %collective-permute-start.21 = (bf16[27,32,256]{2,1,0:T(8,128)(2,1)S(1)}, bf16[27,32,256]{2,1,0:T(8,128)(2,1)S(1)}, u32[]{:S(2)}, u32[]{:S(2)}) collective-permute-start(bf16[27,32,256]{2,1,0:T(8,128)(2,1)S(1)} %add_convert_fusion.refs_0_), channel_id=1, source_target_pairs={{0,8},{1,9},{2,10},{3,11},{4,12},{5,13},{6,14},{7,15},{8,0},{9,1},... | collective-permute-start | bytes 1327112 | tf_op jit(solution)/shard_map/ppermute | solution.py:40
  107.5 17.0 %collective-permute-start.24 = (bf16[27,32,256]{2,1,0:T(8,128)(2,1)S(1)}, bf16[27,32,256]{2,1,0:T(8,128)(2,1)S(1)}, u32[]{:S(2)}, u32[]{:S(2)}) collective-permute-start(bf16[27,32,256]{2,1,0:T(8,128)(2,1)S(1)} %collective-permute-done.20.refs_3_), channel_id=1, source_target_pairs={{0,8},{1,9},{2,10},{3,11},{4,12},{5,13},{6,14},{7,15},{8,0},{9,1},... | collective-permute-start | bytes 1327112 | tf_op jit(solution)/shard_map/ppermute | solution.py:40
  113.2 11.3 %collective-permute-start.23 = (bf16[27,32,256]{2,1,0:T(8,128)(2,1)S(1)}, bf16[27,32,256]{2,1,0:T(8,128)(2,1)S(1)}, u32[]{:S(2)}, u32[]{:S(2)}) collective-permute-start(bf16[27,32,256]{2,1,0:T(8,128)(2,1)S(1)} %collective-permute-done.19.refs_2_), channel_id=1, source_target_pairs={{0,8},{1,9},{2,10},{3,11},{4,12},{5,13},{6,14},{7,15},{8,0},{9,1},... | collective-permute-start | bytes 1327112 | tf_op jit(solution)/shard_map/ppermute | solution.py:40
  114.8 9.6 %collective-permute-start.22 = (bf16[27,32,256]{2,1,0:T(8,128)(2,1)S(1)}, bf16[27,32,256]{2,1,0:T(8,128)(2,1)S(1)}, u32[]{:S(2)}, u32[]{:S(2)}) collective-permute-start(bf16[27,32,256]{2,1,0:T(8,128)(2,1)S(1)} %collective-permute-done.18.refs_1_), channel_id=1, source_target_pairs={{0,8},{1,9},{2,10},{3,11},{4,12},{5,13},{6,14},{7,15},{8,0},{9,1},... | collective-permute-start | bytes 1327112 | tf_op jit(solution)/shard_map/ppermute | solution.py:40
  117.2 2.0 %copy-start.1 = (bf16[27,256,256]{2,1,0:T(8,128)(2,1)S(1)}, bf16[27,256,256]{2,1,0:T(8,128)(2,1)}, u32[]{:S(2)}) copy-start(bf16[27,256,256]{2,1,0:T(8,128)(2,1)} %param.6) | copy-start | bytes 10616836

commit v2 on v0

v2 whole, which is shorter than its diff:
```python
import functools

import jax
import jax.numpy as jnp
from jax import lax
from jax.experimental import pallas as pl
from jax.experimental.pallas import tpu as pltpu
from jax.sharding import PartitionSpec as P

AXES = ("gx", "gy")
F32, BF16 = jnp.float32, jnp.bfloat16
COUNT = 128
ORDERS = tuple(
    tuple(tuple((first + step) % 6 for step in range(6)) for first in firsts) for firsts in ((0, 1), (3, 4))
)
GROUPS = (5, 4)


def place(index):
    gx, gy = index // 8, index % 8
    return (gx // 2) % 4, (gx // 8) * 2 + gy // 4, gy % 4, gx % 2


def index_of(x, y, z, core):
    return ((y // 2) * 8 + x * 2 + core) * 8 + (y % 2) * 4 + z


def step_pairs(chain, step):
    pairs = []
    for i in range(COUNT):
        *at, core = place(i)
        dim = ORDERS[chain][core][step]
        at[dim % 3] = at[dim % 3] ^ 1 if dim < 3 else 3 - at[dim % 3]
        pairs.append((i, index_of(*at, core)))
    return pairs


def core_pairs():
    return [(i, index_of(*place(i)[:3], 1 - place(i)[3])) for i in range(COUNT)]


def send(array, pairs):
    return lax.ppermute(array, AXES, pairs)


def where_am_i():
    gx, gy = lax.axis_index("gx"), lax.axis_index("gy")
    core = gx % 2
    at = [(gx // 2) % 4, (gx // 8) * 2 + gy // 4, gy % 4]
    side = [(v % 2) ^ (v // 2) for v in at] + [v // 2 for v in at]
    found = [core]
    for chain in range(2):
        quarters = [side[order[0]] * 2 + side[order[1]] for order in ORDERS[chain]]
        found.append(jnp.where(core == 0, quarters[0], quarters[1]))
        found.append(jnp.where(core == 0, quarters[1], quarters[0]))
    return jnp.stack(found).astype(jnp.int32)


def pair_swap(axis, first, array):
    count = lax.axis_size(axis)
    pairs = [(i, i + 1) for i in range(first, count - 1, 2)]
    return lax.ppermute(array, axis, pairs + [(b, a) for a, b in pairs])


def neighbours(axis, head, tail):
    even = lax.axis_index(axis) % 2 == 0
    one = pair_swap(axis, 0, jnp.where(even, tail, head))
    two = pair_swap(axis, 1, jnp.where(even, head, tail))
    return jnp.where(even, two, one), jnp.where(even, one, two)


def slabs(masked, mgrad, before, after):
    beside = [(b, a) for b, a in zip(before.reshape(3, 8, 8, 256), after.reshape(3, 8, 8, 256))]
    found = []
    for near, next_one in ((0, 1), (7, 6)):
        parts = []
        for line in (near, next_one):
            at = slice(line * 128, line * 128 + 128)
            parts += [beside[1][0][line], beside[0][0][line], masked[at], beside[0][1][line], beside[1][1][line]]
        at = slice(near * 128, near * 128 + 128)
        parts += [beside[2][0][near], mgrad[at], beside[2][1][near]]
        found.append(jnp.concatenate(parts))
    return found


def roll_cells(field, step):
    cells, chan = field.shape
    tall = field.reshape(cells // 8, 8, chan)
    level = lax.broadcasted_iota(jnp.int32, tall.shape, 1)
    moved = pltpu.roll(tall, step % 8, 1)
    kept = jnp.where((level >= step) & (level < 8 + step), moved, 0.0)
    return kept.reshape(cells, chan)


def dsilu(pre):
    sig = jax.nn.sigmoid(pre)
    return sig * (1.0 + pre * (1.0 - sig))


def brick_mask(occupied, bx, by):
    level = lax.broadcasted_iota(jnp.int32, (8, 256), 0)
    return jnp.where(level < 4, occupied[bx, 0, by], occupied[bx, 1, by]).astype(F32)


def line_mask(occupied, bx):
    return jnp.concatenate([brick_mask(occupied, bx, by) for by in range(4) for _ in range(4)], axis=0)


def mask_kernel(occupied, features_hbm, grad_out_hbm, masked, mgrad, head, tail, features, grad_out, arrived):
    copies = [
        pltpu.make_async_copy(features_hbm, features, arrived.at[0]),
        pltpu.make_async_copy(grad_out_hbm, grad_out, arrived.at[1]),
    ]
    for copy in copies:
        copy.start()
    masks = [line_mask(occupied, bx) for bx in range(2)]
    for copy in copies:
        copy.wait()
    for bx in range(2):
        mask = masks[bx]
        for pair in range(2):
            heads, tails = [], []
            for line in (bx * 4 + pair * 2, bx * 4 + pair * 2 + 1):
                here = slice(line * 128, line * 128 + 128)
                value = features[here, :].astype(F32) * mask
                masked[here, :] = value.astype(BF16)
                grad = grad_out[here, :].astype(F32) * mask
                mgrad[here, :] = grad.astype(BF16)
                heads.append((value[:8], value[8:16], grad[:8]))
                tails.append((value[120:], value[112:120], grad[120:]))
            for kind in range(3):
                two = slice(kind * 64 + bx * 32 + pair * 16, kind * 64 + bx * 32 + pair * 16 + 16)
                head[two, :] = jnp.concatenate([h[kind] for h in heads], axis=0).astype(BF16)
                tail[two, :] = jnp.concatenate([t[kind] for t in tails], axis=0).astype(BF16)


def levels(left, weights, oy_list, ox_list):
    pre = None
    for oz in range(3):
        right = jnp.concatenate([weights[ox * 3 + oy, oz] for ox in ox_list for oy in oy_list], axis=0)
        part = jnp.dot(left, right, preferred_element_type=F32)
        part = part if oz == 1 else roll_cells(part, 1 - oz)
        pre = part if pre is None else pre + part
    return pre


def middle_kernel(masked, weights, pre, turned, held, padded, copied):
    copy = pltpu.make_async_copy(weights, held, copied)
    copy.start()
    padded[0] = jnp.zeros((128, 256), BF16)
    padded[9] = jnp.zeros((128, 256), BF16)
    for line in range(8):
        here = slice(line * 128, line * 128 + 128)
        value = masked[here, :]
        padded[1 + line] = value
        turned[:, here] = value.T

    @pl.loop(0, 4)
    def _(step):
        pieces = [padded[pl.ds(step * 2 + ox, 2)].reshape(256, 256) for ox in range(3)]
        here = pl.ds(pl.multiple_of(step * 256, 256), 256)
        pre[here, :] = levels(jnp.concatenate(pieces, axis=1), weights, (1,), (0, 1, 2))

    copy.wait()


def sides_kernel(masked, before, after, weights, pre_in, pre, turned, held, padded, copied):
    copy = pltpu.make_async_copy(weights, held, copied)
    copy.start()
    for side in range(2):
        padded[side, 0] = jnp.zeros((128, 256), BF16)
        padded[side, 9] = jnp.zeros((128, 256), BF16)
    for pair in range(4):
        left = before[pair * 16 : pair * 16 + 16, :].astype(F32)
        right = after[pair * 16 : pair * 16 + 16, :].astype(F32)
        for i in range(2):
            line = pair * 2 + i
            here = slice(line * 128, line * 128 + 128)
            value = masked[here, :].astype(F32)
            low = jnp.concatenate([left[i * 8 : i * 8 + 8], value[:120]], axis=0).astype(BF16)
            high = jnp.concatenate([value[8:], right[i * 8 : i * 8 + 8]], axis=0).astype(BF16)
            padded[0, 1 + line] = low
            padded[1, 1 + line] = high
            turned[0, :, here] = low.T
            turned[1, :, here] = high.T

    @pl.loop(0, 4)
    def _(step):
        pieces = [padded[side, pl.ds(step * 2 + ox, 2)].reshape(256, 256) for ox in range(3) for side in range(2)]
        here = pl.ds(pl.multiple_of(step * 256, 256), 256)
        pre[here, :] = pre_in[here, :] + levels(jnp.concatenate(pieces, axis=1), weights, (0, 2), (0, 1, 2))

    copy.wait()


def chain_grads(at_ref, middle, sides, ends, shifted, away, keep, chain):
    chan = 256
    core, mine, other = at_ref[0], at_ref[1 + 2 * chain], at_ref[2 + 2 * chain]
    first = sum(GROUPS[:chain])
    for group in range(GROUPS[chain]):
        ox, oy = (first + group) // 3, (first + group) % 3
        rows = []
        for half, quarter in ((core, mine), (1 - core, other)):
            for slot in range(4):
                here = pl.ds(pl.multiple_of(half * 128 + (quarter ^ slot) * 32, 32), 32)
                cells = (lambda a, b: middle[here, a:b]) if oy == 1 else (lambda a, b: sides[oy // 2, here, a:b])
                if ox == 0:
                    row = jnp.concatenate([ends[0, oy, here, :], cells(0, 896)], axis=1)
                elif ox == 1:
                    row = cells(0, 1024)
                else:
                    row = jnp.concatenate([cells(128, 1024), ends[1, oy, here, :]], axis=1)
                rows.append(row)
        left = jnp.concatenate(rows, axis=0)
        for oz in range(3):
            part = jnp.dot(left, shifted[:, oz * chan : (oz + 1) * chan], preferred_element_type=F32)
            keep[:, :, group * 3 + oz] = part[:128].reshape(2, 2, 32, chan)
            away[:, :, group * 3 + oz] = part[128:].reshape(2, 2, 32, chan).astype(BF16)


def grads_kernel(at_ref, first, last, weights, pre, mgrad, middle, sides, dpre, shifted, ends, away, keep):
    chan = 256
    lines = []
    for end, slab in ((0, first), (1, last)):
        line = slab[0:160, :].astype(F32)
        lines.append([line[8 + oy * 8 : 136 + oy * 8].astype(BF16) for oy in range(3)])
        for oy in range(3):
            ends[end, oy] = lines[end][oy].T
    for line in range(8):
        here = slice(line * 128, line * 128 + 128)
        value = pre[here, :]
        if line in (0, 7):
            end, ox = (0, 0) if line == 0 else (1, 2)
            value = value + levels(jnp.concatenate(lines[end], axis=1), weights, (0, 1, 2), (ox,))
        value = (mgrad[here, :].astype(F32) * dsilu(value)).astype(BF16)
        dpre[here, :] = value
        wide = value.astype(F32)
        shifted[here, 0:chan] = roll_cells(wide, -1).astype(BF16)
        shifted[here, chan : 2 * chan] = value
        shifted[here, 2 * chan : 3 * chan] = roll_cells(wide, 1).astype(BF16)
    chain_grads(at_ref, middle, sides, ends, shifted, away, keep, 0)


def more_kernel(at_ref, middle, sides, ends, shifted, away, keep):
    chain_grads(at_ref, middle, sides, ends, shifted, away, keep, 1)


def border_kernel(masked, before, after, first, last, weights, border, left):
    def cells(ref, start, stop):
        return ref[start:stop, :].astype(F32)

    def wide(line):
        near, at = slice(line * 8, line * 8 + 8), slice(line * 128, line * 128 + 128)
        return jnp.concatenate(
            [sides[0][1][near], sides[0][0][near], masked[at, :].astype(F32), sides[1][0][near], sides[1][1][near]], axis=0
        )

    sides = [[cells(ref, kind * 64, kind * 64 + 64) for kind in range(2)] for ref in (before, after)]
    ends = [[cells(ref, 0, 160), cells(ref, 160, 320)] for ref in (first, last)]
    edges = [[masked[x * 128 + y * 112 : x * 128 + y * 112 + 16, :].astype(F32) for x in range(8)] for y in range(2)]
    edge = [
        jnp.concatenate([v[:8] for v in edges[0]], axis=0),
        jnp.concatenate([v[8:] for v in edges[1]], axis=0),
    ]

    def column(index, body):
        at = slice(index * 8, index * 8 + 8)
        return jnp.concatenate([ends[0][0][at], body, ends[1][0][at]], axis=0)

    above = (ends[0][1], ends[0][0], wide(0))
    below = (wide(7), ends[1][0], ends[1][1])
    low = (column(0, sides[0][1]), column(1, sides[0][0]), column(2, edge[0]))
    high = (column(17, edge[1]), column(18, sides[1][0]), column(19, sides[1][1]))
    for ox in range(3):
        for oy in range(3):
            parts = [above[ox][oy * 8 : oy * 8 + 144], below[ox][oy * 8 : oy * 8 + 144]]
            parts += [low[oy][ox * 8 : ox * 8 + 64], high[oy][ox * 8 : ox * 8 + 64]]
            k = (ox * 3 + oy) * 256
            left[:, k : k + 256] = jnp.concatenate(parts, axis=0).astype(BF16)
    pre = None
    for oz in range(3):
        part = jnp.dot(left[...], weights[:, oz].reshape(2304, 256), preferred_element_type=F32)
        part = part if oz == 1 else roll_cells(part, 1 - oz)
        pre = part if pre is None else pre + part
    grad = [cells(first, 320, 464), cells(last, 320, 464), cells(before, 128, 192), cells(after, 128, 192)]
    border[...] = (jnp.concatenate(grad, axis=0) * dsilu(pre)).astype(BF16)


def input_kernel(occupied, dpre, border, weights, out, views):
    tile, chan = 256, 256
    lines = tile // 128

    for line, start in ((0, 0), (9, 144)):
        value = border[start : start + 144, :].astype(F32)
        for side in range(3):
            views[side, line] = value[side * 8 : side * 8 + 128].astype(BF16)
    for pair in range(4):
        low = border[288 + pair * 16 : 304 + pair * 16, :].astype(F32)
        high = border[352 + pair * 16 : 368 + pair * 16, :].astype(F32)
        for i in range(2):
            line = pair * 2 + i
            value = dpre[line * 128 : line * 128 + 128, :]
            views[1, 1 + line] = value
            value = value.astype(F32)
            views[0, 1 + line] = jnp.concatenate([low[i * 8 : i * 8 + 8], value[:120]], axis=0).astype(BF16)
            views[2, 1 + line] = jnp.concatenate([value[8:], high[i * 8 : i * 8 + 8]], axis=0).astype(BF16)

    @pl.loop(0, 8 // lines)
    def _(step):
        first = step * lines
        pieces = []
        for ox in range(3):
            for oy in range(3):
                pieces.append(views[2 - oy, pl.ds(first + 2 - ox, lines)].reshape(tile, chan))
        left = jnp.concatenate(pieces, axis=1)
        total = None
        for oz in range(3):
            right = jnp.concatenate([weights[k, oz] for k in range(9)], axis=1)
            part = lax.dot_general(left, right, (((1,), (1,)), ((), ())), preferred_element_type=F32)
            part = part if oz == 1 else roll_cells(part, oz - 1)
            total = part if total is None else total + part
        mask = line_mask(occupied, step // 2)
        here = pl.ds(pl.multiple_of(first * 128, tile), tile)
        out[here, :] = (total * jnp.concatenate([mask, mask], axis=0)).astype(BF16)


def place_kernel(far, sides, at_ref, *refs):
    pieces, out, built, done = refs[: 2 * len(sides)], refs[-3], refs[-2], refs[-1]
    copies = []
    for chain in range(2):
        for side in sides:
            half = at_ref[0] if side == 0 else 1 - at_ref[0]
            quarter = at_ref[1 + 2 * chain + side]
            pair = (quarter // 2) ^ far
            row = pl.multiple_of(half * 128 + pair * 64, 64)
            for group in range(GROUPS[chain]):
                first = 3 * (sum(GROUPS[:chain]) + group)
                here = slice(first, first + 3)
                for slot in range(2):
                    start = pl.multiple_of(((quarter % 2) ^ slot) * 32, 32)
                    value = pieces[chain * len(sides) + side - sides[0]][slot, group * 3 : group * 3 + 3]
                    built[side - sides[0], here, pl.ds(start, 32), :] = value.astype(F32)
                copy = pltpu.make_async_copy(
                    built.at[side - sides[0], here], out.at[here, pl.ds(row, 64), :], done.at[len(copies)]
                )
                copy.start()
                copies.append(copy)
    for copy in copies:
        copy.wait()


VMEM = pl.BlockSpec(memory_space=pltpu.VMEM)
SMEM = pl.BlockSpec(memory_space=pltpu.SMEM)
HBM = pl.BlockSpec(memory_space=pltpu.HBM)


def shape(*dims, dtype=BF16):
    return jax.ShapeDtypeStruct(dims, dtype)


def chain_shapes(chain):
    dims = (2, 2, 3 * GROUPS[chain], 32, 256)
    return shape(*dims), shape(*dims, dtype=F32)


def kernel(body, outs, specs, args, flops, scratch=(), out_specs=None, aliases=None, nbytes=6_000_000, room=20):
    return pl.pallas_call(
        body,
        out_shape=outs,
        in_specs=specs,
        out_specs=out_specs if out_specs is not None else jax.tree.map(lambda _: VMEM, outs),
        scratch_shapes=scratch,
        input_output_aliases=aliases or {},
        compiler_params=pltpu.CompilerParams(vmem_limit_bytes=room * 2**20),
        cost_estimate=pl.CostEstimate(flops=flops, bytes_accessed=nbytes, transcendentals=0),
    )(*args)


def put_in_place(far, sides, at, pieces, out=None):
    more = () if out is None else (out,)
    return kernel(
        functools.partial(place_kernel, far, sides),
        shape(27, 256, 256, dtype=F32),
        [SMEM] + [VMEM] * len(pieces) + [HBM] * len(more),
        (at, *pieces, *more),
        0,
        [pltpu.VMEM((len(sides), 27, 64, 256), F32), pltpu.SemaphoreType.DMA((9 * len(sides),))],
        HBM,
        {1 + len(pieces): 0} if more else {},
        nbytes=10_000_000,
    )


def halved(chain, total):
    for step in range(2):
        total = total[0] + send(total[1].astype(BF16), step_pairs(chain, step)).astype(F32)
    return total.astype(BF16)


def summed(chain, own, step):
    return (own.astype(F32) + send(own, step_pairs(chain, step)).astype(F32)).astype(BF16)


def gathered(chain, own):
    near = jnp.stack([own, send(own, step_pairs(chain, 1))])
    return near, send(near, step_pairs(chain, 0))


CONV = 3_623_878_656


def local(features, grad_out, weights, occupied):
    at = where_am_i()
    cells, chan = 1024, 256
    packed = weights.reshape(9, 3, chan, chan)
    occupied = jnp.transpose(occupied, (0, 2, 1))
    masked, mgrad, head, tail = kernel(
        mask_kernel,
        (shape(cells, chan), shape(cells, chan), shape(192, chan), shape(192, chan)),
        [SMEM, HBM, HBM],
        (occupied, features.reshape(cells, chan), grad_out.reshape(cells, chan)),
        0,
        [pltpu.VMEM((cells, chan), BF16), pltpu.VMEM((cells, chan), BF16), pltpu.SemaphoreType.DMA((2,))],
        nbytes=2_000_000,
    )
    before, after = neighbours("gy", head, tail)
    held = shape(9, 3, chan, chan)
    pre, middle, kept = kernel(
        middle_kernel,
        (shape(cells, chan, dtype=F32), shape(chan, cells), held),
        [VMEM, VMEM],
        (masked, packed),
        CONV // 3,
        [pltpu.VMEM((10, 128, chan), BF16), pltpu.SemaphoreType.DMA],
    )
    before, after, pre = lax.optimization_barrier((before, after, pre))
    first, last = neighbours("gx", *slabs(masked, mgrad, before, after))
    pre, sides, kept = kernel(
        sides_kernel,
        (shape(cells, chan, dtype=F32), shape(2, chan, cells), held),
        [VMEM] * 5,
        (masked, before, after, kept, pre),
        2 * CONV // 3,
        [pltpu.VMEM((2, 10, 128, chan), BF16), pltpu.SemaphoreType.DMA],
    )
    dpre, shifted, ends, away, keep = kernel(
        grads_kernel,
        (shape(cells, chan), shape(cells, 3 * chan), shape(2, 3, chan, 128), *chain_shapes(0)),
        [SMEM] + [VMEM] * 7,
        (at, first, last, kept, pre, mgrad, middle, sides),
        2 * CONV // 3,
    )
    got = send(away, core_pairs())
    away, more_keep = kernel(
        more_kernel, chain_shapes(1), [SMEM] + [VMEM] * 4, (at, middle, sides, ends, shifted), CONV // 2
    )
    away, got = lax.optimization_barrier((away, got))
    more_got = send(away, core_pairs())
    sums = [halved(0, keep + got.astype(F32)), halved(1, more_keep + more_got.astype(F32))]
    border = kernel(
        border_kernel,
        shape(416, chan),
        [VMEM] * 6,
        (masked, before, after, first, last, packed),
        CONV // 2,
        [pltpu.VMEM((416, 9 * chan), BF16)],
    )
    for step in range(2, 6):
        sums = [summed(chain, own, step) for chain, own in enumerate(sums)]
        if step == 3:
            sums, border = lax.optimization_barrier((sums, border))
            grad_features = kernel(
                input_kernel,
                shape(cells, chan),
                [SMEM, VMEM, VMEM, VMEM],
                (occupied, dpre, border, packed),
                CONV,
                [pltpu.VMEM((3, 10, 128, chan), BF16)],
            )
        if step == 4:
            sums, grad_features = lax.optimization_barrier((sums, grad_features))
    nears, fars = zip(*(gathered(chain, own) for chain, own in enumerate(sums)))
    pieces = [p for near in nears for p in (near, send(near, core_pairs()))]
    out = put_in_place(0, (0, 1), at, pieces)
    fars, out = lax.optimization_barrier((fars, out))
    others = [send(far, core_pairs()) for far in fars]
    out = put_in_place(1, (0,), at, fars, out)
    out = put_in_place(1, (1,), at, others, out)
    return grad_features.reshape(features.shape), out


def solution(mesh):
    return jax.shard_map(
        local,
        mesh=mesh,
        in_specs=(P("gx", "gy", None, None), P("gx", "gy", None, None), P(), P("gx", "gy", None)),
        out_specs=(P("gx", "gy", None, None), P()),
        check_vma=False,
    )
```

time: 265 us -> 109 us (0.41); the launches traced: 261 us -> 109 us
  waiting for transfers between devices: 146 us -> 26.5 us
  matrix products: 45.1 us -> 0 us
  Pallas kernels: 0 us -> 27.1 us
  starting transfers between devices: 25 us -> 42.5 us
  local copies, waits for them, and re-layouts: 23.5 us -> 8.88 us
  between operations: 15.4 us -> 1.42 us
  other arithmetic: 6.5 us -> 2.52 us
    psum x1 -> x0, waiting for transfers between devices: 143 us -> none  [reduce_grads(): return lax.psum(local_grads, ('gx', 'gy'))]
    dot_general x81 -> x0, matrix products: 45.1 us -> none  [the longest x27 28.3 us: kernel_grads(): lax.dot_general(block, flat, (((0,), (0,)), ((), ())), preferred_element_...]
    pallas_call x0 -> x10, Pallas kernels: none -> 27.1 us  [kernel(): pl.pallas_call(body, out_shape=outs, in_specs=specs, out_specs=out_specs...]
    ppermute x8 -> x26, waiting for transfers between devices: 3.26 us -> 26.5 us  [the longest x22 26.5 us: send(): return lax.ppermute(array, AXES, pairs)]
    ppermute x8 -> x26, starting transfers between devices: 24.9 us -> 42.5 us  [the longest x22 35.3 us: send(): return lax.ppermute(array, AXES, pairs)]
    slice x59 -> x0, local copies, waits for them, and re-layouts: 15.1 us -> none  [the longest x29 7.59 us: input_grads(): dextended[1 - ox:1 - ox + sx, 1 - oy:1 - oy + sy, 1 - oz:1 - oz + sz]]
    unnamed x7 -> x28, local copies, waits for them, and re-layouts: 7.56 us -> 8.62 us
  transfers between devices with their start and end apart: 9 -> 26, of which waited for: 4 -> 14; matrix products, arithmetic and copies ran while one was open for 18% -> 2% of each run, Pallas kernels for 0% -> 19%
where the time goes in v2:
time: 109 us
  starting transfers between devices  42.5 us (39%)
  Pallas kernels  27.1 us (25%)
  waiting for transfers between devices  26.5 us (24%)
  local copies, waits for them, and re-layouts  8.88 us (8%)
  other arithmetic  2.52 us (2%)
  between operations  1.42 us (1%)
    ppermute x22, starting transfers between devices, send(): return lax.ppermute(array, AXES, pairs)  35.3 us
    pallas_call x10, Pallas kernels, kernel(): pl.pallas_call(body, out_shape=outs, in_specs=specs, out_specs=out_specs...  27.1 us
    ppermute x22, waiting for transfers between devices, send(): return lax.ppermute(array, AXES, pairs)  26.5 us
    unnamed x28, local copies, waits for them, and re-layouts  8.62 us
    ppermute x4, starting transfers between devices, pair_swap(): return lax.ppermute(array, axis, pairs + [(b, a) for a, b in pairs])  7.15 us
  transfers between devices with their start and end apart: 26, of which 14 were waited for; matrix products, arithmetic and copies ran while one was open for 2% of the time, Pallas kernels for 19%

profile of v2, /device:TPU:1, one launch (start us, length us, event | category | flops | bytes accessed | tf_op | source)
XLA Modules:
  0.0 108.9 jit_solution(14558507488664431902)
XLA Ops:
  1.7 1.0 copy-done.1
  4.3 2.5 %collective-permute-start.1 = (bf16[192,256]{1,0:T(8,128)(2,1)S(1)}, bf16[192,256]{1,0:T(8,128)(2,1)S(1)}, u32[]{:S(2)}, u32[]{:S(2)}) collective-permute-start(bf16[192,256]{1,0:T(8,128)(2,1)S(1)} %get-tuple-element.76), channel_id=1, source_target_pairs={{0,1},{2,3},{4,5},{6,7},{1,0},{3,2},{5,4},{7,6},{8,9},{10,11},{12,... | collective-permute-start | bytes 294920 | tf_op jit(solution)/shard_map/ppermute | solution.py:62
  7.5 2.0 %copy-done.4 = bf16[27,256,256]{2,1,0:T(8,128)(2,1)S(1)} copy-done((bf16[27,256,256]{2,1,0:T(8,128)(2,1)S(1)}, bf16[27,256,256]{2,1,0:T(8,128)(2,1)}, u32[]{:S(2)}) %copy-start.4) | copy-done | bytes 3538968
  9.5 2.6 %shard_map.60 = (f32[1024,256]{1,0:T(8,128)S(1)}, bf16[256,1024]{1,0:T(8,128)(2,1)S(1)}, bf16[9,3,256,256]{3,2,1,0:T(8,128)(2,1)S(1)}) custom-call(bf16[1024,256]{1,0:T(8,128)(2,1)S(1)} %get-tuple-element.35.masked, bf16[9,3,256,256]{3,2,1,0:T(8,128)(2,1)S(1)} %bitcast.46), custom_call_target="tpu_custom_call" | custom-call | flops 1207959552 | bytes 6000000 | tf_op jit(solution)/shard_map/pallas_call | solution.py:367
  12.1 1.8 %copy-done.6 = bf16[9,3,256,256]{3,2,1,0:T(8,128)(2,1)} copy-done((bf16[9,3,256,256]{3,2,1,0:T(8,128)(2,1)}, bf16[9,3,256,256]{3,2,1,0:T(8,128)(2,1)S(1)}, u32[]{:S(2)}) %copy-start.6) | copy-done | bytes 3538968
  15.8 3.0 %collective-permute-start.2 = (bf16[464,256]{1,0:T(8,128)(2,1)S(1)}, bf16[464,256]{1,0:T(8,128)(2,1)S(1)}, u32[]{:S(2)}, u32[]{:S(2)}) collective-permute-start(bf16[464,256]{1,0:T(8,128)(2,1)S(1)} %get-tuple-element.73), channel_id=1, source_target_pairs={{8,16},{24,32},{40,48},{56,64},{72,80},{88,96},{104,112},{16,8},{3... | collective-permute-start | bytes 712712 | tf_op jit(solution)/shard_map/ppermute | solution.py:62
  19.0 2.0 %copy-done.7 = bf16[9,3,256,256]{3,2,1,0:T(8,128)(2,1)S(1)} copy-done((bf16[9,3,256,256]{3,2,1,0:T(8,128)(2,1)S(1)}, bf16[9,3,256,256]{3,2,1,0:T(8,128)(2,1)}, u32[]{:S(2)}) %copy-start.7) | copy-done | bytes 3538968
  21.0 3.9 %shard_map.61 = (f32[1024,256]{1,0:T(8,128)S(1)}, bf16[2,256,1024]{2,1,0:T(8,128)(2,1)S(1)}, bf16[9,3,256,256]{3,2,1,0:T(8,128)(2,1)S(1)}) custom-call(bf16[1024,256]{1,0:T(8,128)(2,1)S(1)} %get-tuple-element.35.masked, bf16[192,256]{1,0:T(8,128)(2,1)S(1)} %get-tuple-element.37.before, bf16[192,256]{1,0:T(8,128)(2,1)S(1)} %get-tuple-element.38.after, ...), custom_call_target="tpu_custom_call" | custom-call | flops 2415919104 | bytes 6000000 | tf_op jit(solution)/shard_map/pallas_call | solution.py:367
  25.0 3.6 %shard_map.62 = (bf16[1024,256]{1,0:T(8,128)(2,1)S(1)}, bf16[1024,768]{1,0:T(8,128)(2,1)S(1)}, bf16[2,3,256,128]{3,2,1,0:T(8,128)(2,1)S(1)}, bf16[2,2,15,32,256]...) custom-call(s32[5]{0:T(128)S(1)} %stack.41.at_ref, bf16[464,256]{1,0:T(8,128)(2,1)S(1)} %get-tuple-element.71.first, ...), custom_call_target="tpu_custom_call" | custom-call | flops 2415919104 | bytes 6000000 | tf_op jit(solution)/shard_map/pallas_call | solution.py:367
  28.7 2.4 %shard_map.63 = (bf16[2,2,12,32,256]{4,3,2,1,0:T(8,128)(2,1)S(1)}, f32[2,2,12,32,256]{4,3,2,1,0:T(8,128)S(1)}) custom-call(s32[5]{0:T(128)S(1)} %stack.41.at_ref, bf16[256,1024]{1,0:T(8,128)(2,1)S(1)} %get-tuple-element.44.middle, bf16[2,256,1024]{2,1,0:T(8,128)(2,1)S(1)} %get-tuple-element.45.sides, bf16[2,3,256,128]{3,2,1,0:T(8,128)(2,1)S(1)} %get-tuple-element.47.ends, ...), custom_call_target="tpu_custom_call" | custom-call | flops 1811939328 | bytes 6000000 | tf_op jit(solution)/shard_map/pallas_call | solution.py:367
  32.1 5.0 %collective-permute-start.5 = (bf16[2,15,32,256]{3,2,1,0:T(8,128)(2,1)S(1)}, bf16[2,15,32,256]{3,2,1,0:T(8,128)(2,1)S(1)}, u32[]{:S(2)}, u32[]{:S(2)}) collective-permute-start(bf16[2,15,32,256]{3,2,1,0:T(8,128)(2,1)S(1)} %fusion.2), channel_id=1, source_target_pairs={{0,16},{1,17},{2,18},{3,19},{4,20},{5,21},{6,22},{7,23},{8,12},{9,... | collective-permute-start | bytes 1474568 | tf_op jit(solution)/shard_map/ppermute | solution.py:43
  37.5 5.1 %collective-permute-start.10 = (bf16[2,12,32,256]{3,2,1,0:T(8,128)(2,1)S(1)}, bf16[2,12,32,256]{3,2,1,0:T(8,128)(2,1)S(1)}, u32[]{:S(2)}, u32[]{:S(2)}) collective-permute-start(bf16[2,12,32,256]{3,2,1,0:T(8,128)(2,1)S(1)} %fusion.5), channel_id=1, source_target_pairs={{0,48},{1,49},{2,50},{3,51},{4,52},{5,53},{6,54},{7,55},{8,76},{9,... | collective-permute-start | bytes 1179656 | tf_op jit(solution)/shard_map/ppermute | solution.py:43
  42.6 1.1 collective-permute-done.5
  43.9 1.1 %collective-permute-start.6 = (bf16[15,32,256]{2,1,0:T(8,128)(2,1)S(1)}, bf16[15,32,256]{2,1,0:T(8,128)(2,1)S(1)}, u32[]{:S(2)}, u32[]{:S(2)}) collective-permute-start(bf16[15,32,256]{2,1,0:T(8,128)(2,1)S(1)} %fusion.8), channel_id=1, source_target_pairs={{0,4},{1,5},{2,6},{3,7},{4,0},{5,1},{6,2},{7,3},{8,9},{9,8},{10,11... | collective-permute-start | bytes 737288 | tf_op jit(solution)/shard_map/ppermute | solution.py:43
  45.0 2.8 %collective-permute-done.10 = bf16[2,12,32,256]{3,2,1,0:T(8,128)(2,1)S(1)} collective-permute-done((bf16[2,12,32,256]{3,2,1,0:T(8,128)(2,1)S(1)}, bf16[2,12,32,256]{3,2,1,0:T(8,128)(2,1)S(1)}, u32[]{:S(2)}, u32[]{:S(2)}) %collective-permute-start.10) | collective-permute-done | bytes 393248 | tf_op jit(solution)/shard_map/ppermute | solution.py:43
  48.0 1.3 %collective-permute-done.6 = bf16[15,32,256]{2,1,0:T(8,128)(2,1)S(1)} collective-permute-done((bf16[15,32,256]{2,1,0:T(8,128)(2,1)S(1)}, bf16[15,32,256]{2,1,0:T(8,128)(2,1)S(1)}, u32[]{:S(2)}, u32[]{:S(2)}) %collective-permute-start.6) | collective-permute-done | bytes 245792 | tf_op jit(solution)/shard_map/ppermute | solution.py:43
  49.4 4.1 %collective-permute-start.7 = (bf16[15,32,256]{2,1,0:T(8,128)(2,1)S(1)}, bf16[15,32,256]{2,1,0:T(8,128)(2,1)S(1)}, u32[]{:S(2)}, u32[]{:S(2)}) collective-permute-start(bf16[15,32,256]{2,1,0:T(8,128)(2,1)S(1)} %fusion.4), channel_id=1, source_target_pairs={{0,1},{1,0},{2,3},{3,2},{4,5},{5,4},{6,7},{7,6},{8,56},{9,57},{10,... | collective-permute-start | bytes 737288 | tf_op jit(solution)/shard_map/ppermute | solution.py:43
  54.2 2.9 %collective-permute-done.7 = bf16[15,32,256]{2,1,0:T(8,128)(2,1)S(1)} collective-permute-done((bf16[15,32,256]{2,1,0:T(8,128)(2,1)S(1)}, bf16[15,32,256]{2,1,0:T(8,128)(2,1)S(1)}, u32[]{:S(2)}, u32[]{:S(2)}) %collective-permute-start.7) | collective-permute-done | bytes 245792 | tf_op jit(solution)/shard_map/ppermute | solution.py:43
  57.1 3.9 %collective-permute-start.8 = (bf16[15,32,256]{2,1,0:T(8,128)(2,1)S(1)}, bf16[15,32,256]{2,1,0:T(8,128)(2,1)S(1)}, u32[]{:S(2)}, u32[]{:S(2)}) collective-permute-start(bf16[15,32,256]{2,1,0:T(8,128)(2,1)S(1)} %add_convert_fusion.3), channel_id=1, source_target_pairs={{0,48},{1,49},{2,50},{3,51},{4,52},{5,53},{6,54},{7,55},{8,76},{9,... | collective-permute-start | bytes 737288 | tf_op jit(solution)/shard_map/ppermute | solution.py:43
  61.0 1.7 %shard_map.64.border = bf16[416,256]{1,0:T(8,128)(2,1)S(1)} custom-call(bf16[1024,256]{1,0:T(8,128)(2,1)S(1)} %get-tuple-element.35.masked, bf16[192,256]{1,0:T(8,128)(2,1)S(1)} %get-tuple-element.37.before, bf16[192,256]{1,0:T(8,128)(2,1)S(1)} %get-tuple-element.38.after, bf16[464,256]{1,0:T(8,128)(2,1)S(1)} %get-tuple-element.71.first, ...), custom_call_target="tpu_custom_call" | custom-call | flops 1811939328 | bytes 6000000 | tf_op jit(solution)/shard_map/pallas_call | solution.py:367
  62.9 2.0 %collective-permute-done.8 = bf16[15,32,256]{2,1,0:T(8,128)(2,1)S(1)} collective-permute-done((bf16[15,32,256]{2,1,0:T(8,128)(2,1)S(1)}, bf16[15,32,256]{2,1,0:T(8,128)(2,1)S(1)}, u32[]{:S(2)}, u32[]{:S(2)}) %collective-permute-start.8) | collective-permute-done | bytes 245792 | tf_op jit(solution)/shard_map/ppermute | solution.py:43
  65.0 2.8 %collective-permute-done.13 = bf16[12,32,256]{2,1,0:T(8,128)(2,1)S(1)} collective-permute-done((bf16[12,32,256]{2,1,0:T(8,128)(2,1)S(1)}, bf16[12,32,256]{2,1,0:T(8,128)(2,1)S(1)}, u32[]{:S(2)}, u32[]{:S(2)}) %collective-permute-start.13) | collective-permute-done | bytes 196640 | tf_op jit(solution)/shard_map/ppermute | solution.py:43
  68.8 6.0 %shard_map.65 = bf16[1024,256]{1,0:T(8,128)(2,1)} custom-call(s32[2,2,4]{2,1,0:T(2,128)S(1)} %bitcast.45, bf16[1024,256]{1,0:T(8,128)(2,1)S(1)} %get-tuple-element.56.dpre, bf16[416,256]{1,0:T(8,128)(2,1)S(1)} %shard_map.64.border, bf16[9,3,256,256]{3,2,1,0:T(8,128)(2,1)S(1)} %bitcast.48), custom_call_target="tpu_custom_call" | custom-call | flops 3623878656 | bytes 6000000 | tf_op jit(solution)/shard_map/pallas_call | solution.py:367
  75.4 4.8 %collective-permute-done.16 = bf16[15,32,256]{2,1,0:T(8,128)(2,1)S(1)} collective-permute-done((bf16[15,32,256]{2,1,0:T(8,128)(2,1)S(1)}, bf16[15,32,256]{2,1,0:T(8,128)(2,1)S(1)}, u32[]{:S(2)}, u32[]{:S(2)}) %collective-permute-start.16) | collective-permute-done | bytes 245792 | tf_op jit(solution)/shard_map/ppermute | solution.py:43
  81.1 2.6 %collective-permute-start.20 = (bf16[12,32,256]{2,1,0:T(8,128)(2,1)S(1)}, bf16[12,32,256]{2,1,0:T(8,128)(2,1)S(1)}, u32[]{:S(2)}, u32[]{:S(2)}) collective-permute-start(bf16[12,32,256]{2,1,0:T(8,128)(2,1)S(1)} %add_convert_fusion.4), channel_id=1, source_target_pairs={{0,68},{1,69},{2,70},{3,71},{4,64},{5,65},{6,66},{7,67},{8,11},{9,... | collective-permute-start | bytes 589832 | tf_op jit(solution)/shard_map/ppermute | solution.py:43
  83.6 4.1 %collective-permute-done.17 = bf16[15,32,256]{2,1,0:T(8,128)(2,1)S(1)} collective-permute-done((bf16[15,32,256]{2,1,0:T(8,128)(2,1)S(1)}, bf16[15,32,256]{2,1,0:T(8,128)(2,1)S(1)}, u32[]{:S(2)}, u32[]{:S(2)}) %collective-permute-start.17) | collective-permute-done | bytes 245792 | tf_op jit(solution)/shard_map/ppermute | solution.py:43
  87.8 7.0 %collective-permute-start.22 = (bf16[2,15,32,256]{3,2,1,0:T(8,128)(2,1)S(1)}, bf16[2,15,32,256]{3,2,1,0:T(8,128)(2,1)S(1)}, u32[]{:S(2)}, u32[]{:S(2)}) collective-permute-start(bf16[2,15,32,256]{3,2,1,0:T(8,128)(2,1)S(1)} %pad_maximum_fusion.refs_0_), channel_id=1, source_target_pairs={{0,8},{1,9},{2,10},{3,11},{4,12},{5,13},{6,14},{7,15},{8,0},{9,1},... | collective-permute-start | bytes 1474568 | tf_op jit(solution)/shard_map/ppermute | solution.py:43
  95.8 2.0 %collective-permute-start.21 = (bf16[2,12,32,256]{3,2,1,0:T(8,128)(2,1)S(1)}, bf16[2,12,32,256]{3,2,1,0:T(8,128)(2,1)S(1)}, u32[]{:S(2)}, u32[]{:S(2)}) collective-permute-start(bf16[2,12,32,256]{3,2,1,0:T(8,128)(2,1)S(1)} %pad_maximum_fusion.1.refs_2_), channel_id=1, source_target_pairs={{0,48},{1,49},{2,50},{3,51},{4,52},{5,53},{6,54},{7,55},{8,76},{9,... | collective-permute-start | bytes 1179656 | tf_op jit(solution)/shard_map/ppermute | solution.py:43
  97.8 2.5 %shard_map.66.refs_2_ = f32[27,256,256]{2,1,0:T(8,128)} custom-call(s32[5]{0:T(128)S(1)} %stack.41.at_ref, bf16[2,15,32,256]{3,2,1,0:T(8,128)(2,1)S(1)} %pad_maximum_fusion.refs_0_, bf16[2,15,32,256]{3,2,1,0:T(8,128)(2,1)S(1)} %collective-permute-done.22.refs_1_, bf16[2,12,32,256]{3,2,1,0:T(8,128)(2,1)S(1)} %pad_maximum_fusion.1.refs_2_, ...), custom_call_target="tpu_custom_call" | custom-call | bytes 10000000 | tf_op jit(solution)/shard_map/pallas_call | solution.py:367
  100.3 3.6 %collective-permute-done.21.refs_1_ = bf16[2,12,32,256]{3,2,1,0:T(8,128)(2,1)S(1)} collective-permute-done((bf16[2,12,32,256]{3,2,1,0:T(8,128)(2,1)S(1)}, bf16[2,12,32,256]{3,2,1,0:T(8,128)(2,1)S(1)}, u32[]{:S(2)}, u32[]{:S(2)}) %collective-permute-start.21) | collective-permute-done | bytes 393248 | tf_op jit(solution)/shard_map/ppermute | solution.py:43
  104.9 1.8 %shard_map.67.refs_2_ = f32[27,256,256]{2,1,0:T(8,128)} custom-call(s32[5]{0:T(128)S(1)} %stack.41.at_ref, bf16[2,15,32,256]{3,2,1,0:T(8,128)(2,1)S(1)} %collective-permute-done.18.refs_0_, bf16[2,12,32,256]{3,2,1,0:T(8,128)(2,1)S(1)} %collective-permute-done.21.refs_1_, f32[27,256,256]{2,1,0:T(8,128)} %shard_map.66.refs_2_), custom_call_target="tpu_custom_call", output_to_operand_aliasing={{}: (3, {})} | custom-call | bytes 10000000 | tf_op jit(solution)/shard_map/pallas_call | solution.py:367
  106.9 1.8 %shard_map.68 = f32[27,256,256]{2,1,0:T(8,128)} custom-call(s32[5]{0:T(128)S(1)} %stack.41.at_ref, bf16[2,15,32,256]{3,2,1,0:T(8,128)(2,1)S(1)} %collective-permute-done.24.refs_0_, bf16[2,12,32,256]{3,2,1,0:T(8,128)(2,1)S(1)} %collective-permute-done.25.refs_1_, f32[27,256,256]{2,1,0:T(8,128)} %shard_map.67.refs_2_), custom_call_target="tpu_custom_call", output_to_operand_aliasing={{}: (3, {})} | custom-call | bytes 10000000 | tf_op jit(solution)/shard_map/pallas_call | solution.py:367
  (84 shorter events, 12.9 us)
Async XLA Ops:
  0.6 1.0 copy-start
  4.3 9.6 %collective-permute-start.1 = (bf16[192,256]{1,0:T(8,128)(2,1)S(1)}, bf16[192,256]{1,0:T(8,128)(2,1)S(1)}, u32[]{:S(2)}, u32[]{:S(2)}) collective-permute-start(bf16[192,256]{1,0:T(8,128)(2,1)S(1)} %get-tuple-element.76), channel_id=1, source_target_pairs={{0,1},{2,3},{4,5},{6,7},{1,0},{3,2},{5,4},{7,6},{8,9},{10,11},{12,... | collective-permute-start | bytes 294920 | tf_op jit(solution)/shard_map/ppermute | solution.py:62
  6.8 7.0 %collective-permute-start = (bf16[192,256]{1,0:T(8,128)(2,1)S(1)}, bf16[192,256]{1,0:T(8,128)(2,1)S(1)}, u32[]{:S(2)}, u32[]{:S(2)}) collective-permute-start(bf16[192,256]{1,0:T(8,128)(2,1)S(1)} %get-tuple-element.77), channel_id=1, source_target_pairs={{1,2},{3,4},{5,6},{2,1},{4,3},{6,5},{9,10},{11,12},{13,14},{10,9},... | collective-permute-start | bytes 294920 | tf_op jit(solution)/shard_map/ppermute | solution.py:62
  7.5 2.0 %copy-start.4 = (bf16[27,256,256]{2,1,0:T(8,128)(2,1)S(1)}, bf16[27,256,256]{2,1,0:T(8,128)(2,1)}, u32[]{:S(2)}) copy-start(bf16[27,256,256]{2,1,0:T(8,128)(2,1)} %param.6) | copy-start | bytes 10616836
  12.1 1.8 %copy-start.6 = (bf16[9,3,256,256]{3,2,1,0:T(8,128)(2,1)}, bf16[9,3,256,256]{3,2,1,0:T(8,128)(2,1)S(1)}, u32[]{:S(2)}) copy-start(bf16[9,3,256,256]{3,2,1,0:T(8,128)(2,1)S(1)} %get-tuple-element.40.weights) | copy-start | bytes 10616836
  14.8 10.1 %collective-permute-start.3 = (bf16[464,256]{1,0:T(8,128)(2,1)}, bf16[464,256]{1,0:T(8,128)(2,1)S(1)}, u32[]{:S(2)}, u32[]{:S(2)}) collective-permute-start(bf16[464,256]{1,0:T(8,128)(2,1)} %get-tuple-element.72), channel_id=1, source_target_pairs={{0,8},{16,24},{32,40},{48,56},{64,72},{80,88},{96,104},{112,120},{... | collective-permute-start | bytes 712712 | tf_op jit(solution)/shard_map/ppermute | solution.py:62
  15.8 9.2 %collective-permute-start.2 = (bf16[464,256]{1,0:T(8,128)(2,1)S(1)}, bf16[464,256]{1,0:T(8,128)(2,1)S(1)}, u32[]{:S(2)}, u32[]{:S(2)}) collective-permute-start(bf16[464,256]{1,0:T(8,128)(2,1)S(1)} %get-tuple-element.73), channel_id=1, source_target_pairs={{8,16},{24,32},{40,48},{56,64},{72,80},{88,96},{104,112},{16,8},{3... | collective-permute-start | bytes 712712 | tf_op jit(solution)/shard_map/ppermute | solution.py:62
  19.0 2.0 %copy-start.7 = (bf16[9,3,256,256]{3,2,1,0:T(8,128)(2,1)S(1)}, bf16[9,3,256,256]{3,2,1,0:T(8,128)(2,1)}, u32[]{:S(2)}) copy-start(bf16[9,3,256,256]{3,2,1,0:T(8,128)(2,1)} %copy-done.6) | copy-start | bytes 10616836
  28.6 2.6 %collective-permute-start.4 = (bf16[2,2,15,32,256]{4,3,2,1,0:T(8,128)(2,1)S(1)}, bf16[2,2,15,32,256]{4,3,2,1,0:T(8,128)(2,1)S(1)}, u32[]{:S(2)}, u32[]{:S(2)}) collective-permute-start(bf16[2,2,15,32,256]{4,3,2,1,0:T(8,128)(2,1)S(1)} %get-tuple-element.50), channel_id=1, source_target_pairs={{0,8},{1,9},{2,10},{3,11},{4,12},{5,13},{6,14},{7,15},{8,0},{9,1},... | collective-permute-start | bytes 2949128 | tf_op jit(solution)/shard_map/ppermute | solution.py:43
  31.2 5.9 %collective-permute-start.9 = (bf16[2,2,12,32,256]{4,3,2,1,0:T(8,128)(2,1)S(1)}, bf16[2,2,12,32,256]{4,3,2,1,0:T(8,128)(2,1)S(1)}, u32[]{:S(2)}, u32[]{:S(2)}) collective-permute-start(bf16[2,2,12,32,256]{4,3,2,1,0:T(8,128)(2,1)S(1)} %get-tuple-element.53), channel_id=1, source_target_pairs={{0,8},{1,9},{2,10},{3,11},{4,12},{5,13},{6,14},{7,15},{8,0},{9,1},... | collective-permute-start | bytes 2359304 | tf_op jit(solution)/shard_map/ppermute | solution.py:43
  32.1 11.5 %collective-permute-start.5 = (bf16[2,15,32,256]{3,2,1,0:T(8,128)(2,1)S(1)}, bf16[2,15,32,256]{3,2,1,0:T(8,128)(2,1)S(1)}, u32[]{:S(2)}, u32[]{:S(2)}) collective-permute-start(bf16[2,15,32,256]{3,2,1,0:T(8,128)(2,1)S(1)} %fusion.2), channel_id=1, source_target_pairs={{0,16},{1,17},{2,18},{3,19},{4,20},{5,21},{6,22},{7,23},{8,12},{9,... | collective-permute-start | bytes 1474568 | tf_op jit(solution)/shard_map/ppermute | solution.py:43
  37.5 10.3 %collective-permute-start.10 = (bf16[2,12,32,256]{3,2,1,0:T(8,128)(2,1)S(1)}, bf16[2,12,32,256]{3,2,1,0:T(8,128)(2,1)S(1)}, u32[]{:S(2)}, u32[]{:S(2)}) collective-permute-start(bf16[2,12,32,256]{3,2,1,0:T(8,128)(2,1)S(1)} %fusion.5), channel_id=1, source_target_pairs={{0,48},{1,49},{2,50},{3,51},{4,52},{5,53},{6,54},{7,55},{8,76},{9,... | collective-permute-start | bytes 1179656 | tf_op jit(solution)/shard_map/ppermute | solution.py:43
  43.9 17.2 %copy-start.5 = (bf16[27,256,256]{2,1,0:T(8,128)(2,1)S(1)}, bf16[27,256,256]{2,1,0:T(8,128)(2,1)}, u32[]{:S(2)}) copy-start(bf16[27,256,256]{2,1,0:T(8,128)(2,1)} %param.6) | copy-start | bytes 10616836
  43.9 5.4 %collective-permute-start.6 = (bf16[15,32,256]{2,1,0:T(8,128)(2,1)S(1)}, bf16[15,32,256]{2,1,0:T(8,128)(2,1)S(1)}, u32[]{:S(2)}, u32[]{:S(2)}) collective-permute-start(bf16[15,32,256]{2,1,0:T(8,128)(2,1)S(1)} %fusion.8), channel_id=1, source_target_pairs={{0,4},{1,5},{2,6},{3,7},{4,0},{5,1},{6,2},{7,3},{8,9},{9,8},{10,11... | collective-permute-start | bytes 737288 | tf_op jit(solution)/shard_map/ppermute | solution.py:43
  47.9 6.1 %collective-permute-start.11 = (bf16[12,32,256]{2,1,0:T(8,128)(2,1)S(1)}, bf16[12,32,256]{2,1,0:T(8,128)(2,1)S(1)}, u32[]{:S(2)}, u32[]{:S(2)}) collective-permute-start(bf16[12,32,256]{2,1,0:T(8,128)(2,1)S(1)} %fusion.9), channel_id=1, source_target_pairs={{0,68},{1,69},{2,70},{3,71},{4,64},{5,65},{6,66},{7,67},{8,11},{9,... | collective-permute-start | bytes 589832 | tf_op jit(solution)/shard_map/ppermute | solution.py:43
  49.4 7.7 %collective-permute-start.7 = (bf16[15,32,256]{2,1,0:T(8,128)(2,1)S(1)}, bf16[15,32,256]{2,1,0:T(8,128)(2,1)S(1)}, u32[]{:S(2)}, u32[]{:S(2)}) collective-permute-start(bf16[15,32,256]{2,1,0:T(8,128)(2,1)S(1)} %fusion.4), channel_id=1, source_target_pairs={{0,1},{1,0},{2,3},{3,2},{4,5},{5,4},{6,7},{7,6},{8,56},{9,57},{10,... | collective-permute-start | bytes 737288 | tf_op jit(solution)/shard_map/ppermute | solution.py:43
  54.1 8.7 %collective-permute-start.12 = (bf16[12,32,256]{2,1,0:T(8,128)(2,1)S(1)}, bf16[12,32,256]{2,1,0:T(8,128)(2,1)S(1)}, u32[]{:S(2)}, u32[]{:S(2)}) collective-permute-start(bf16[12,32,256]{2,1,0:T(8,128)(2,1)S(1)} %fusion.7), channel_id=1, source_target_pairs={{0,3},{1,2},{2,1},{3,0},{4,7},{5,6},{6,5},{7,4},{8,24},{9,25},{10,... | collective-permute-start | bytes 589832 | tf_op jit(solution)/shard_map/ppermute | solution.py:43
  57.1 11.7 %copy-start.3 = (s32[2,4,2]{1,2,0:T(2,128)S(1)}, s32[2,4,2]{1,2,0:T(2,128)}, u32[]{:S(2)}) copy-start(s32[2,4,2]{1,2,0:T(2,128)} %param.7) | copy-start | bytes 196
  57.1 7.8 %collective-permute-start.8 = (bf16[15,32,256]{2,1,0:T(8,128)(2,1)S(1)}, bf16[15,32,256]{2,1,0:T(8,128)(2,1)S(1)}, u32[]{:S(2)}, u32[]{:S(2)}) collective-permute-start(bf16[15,32,256]{2,1,0:T(8,128)(2,1)S(1)} %add_convert_fusion.3), channel_id=1, source_target_pairs={{0,48},{1,49},{2,50},{3,51},{4,52},{5,53},{6,54},{7,55},{8,76},{9,... | collective-permute-start | bytes 737288 | tf_op jit(solution)/shard_map/ppermute | solution.py:43
  62.9 4.9 %collective-permute-start.13 = (bf16[12,32,256]{2,1,0:T(8,128)(2,1)S(1)}, bf16[12,32,256]{2,1,0:T(8,128)(2,1)S(1)}, u32[]{:S(2)}, u32[]{:S(2)}) collective-permute-start(bf16[12,32,256]{2,1,0:T(8,128)(2,1)S(1)} %add_convert_fusion.7), channel_id=1, source_target_pairs={{0,16},{1,17},{2,18},{3,19},{4,20},{5,21},{6,22},{7,23},{8,12},{9,... | collective-permute-start | bytes 589832 | tf_op jit(solution)/shard_map/ppermute | solution.py:43
  67.8 7.0 %collective-permute-start.15 = (bf16[12,32,256]{2,1,0:T(8,128)(2,1)S(1)}, bf16[12,32,256]{2,1,0:T(8,128)(2,1)S(1)}, u32[]{:S(2)}, u32[]{:S(2)}) collective-permute-start(bf16[12,32,256]{2,1,0:T(8,128)(2,1)S(1)} %add_convert_fusion.6), channel_id=1, source_target_pairs={{0,4},{1,5},{2,6},{3,7},{4,0},{5,1},{6,2},{7,3},{8,9},{9,8},{10,11... | collective-permute-start | bytes 589832 | tf_op jit(solution)/shard_map/ppermute | solution.py:43
  68.7 6.3 %collective-permute-start.14 = (bf16[15,32,256]{2,1,0:T(8,128)(2,1)S(1)}, bf16[15,32,256]{2,1,0:T(8,128)(2,1)S(1)}, u32[]{:S(2)}, u32[]{:S(2)}) collective-permute-start(bf16[15,32,256]{2,1,0:T(8,128)(2,1)S(1)} %add_convert_fusion.2), channel_id=1, source_target_pairs={{0,68},{1,69},{2,70},{3,71},{4,64},{5,65},{6,66},{7,67},{8,11},{9,... | collective-permute-start | bytes 737288 | tf_op jit(solution)/shard_map/ppermute | solution.py:43
  75.1 5.1 %collective-permute-start.16 = (bf16[15,32,256]{2,1,0:T(8,128)(2,1)S(1)}, bf16[15,32,256]{2,1,0:T(8,128)(2,1)S(1)}, u32[]{:S(2)}, u32[]{:S(2)}) collective-permute-start(bf16[15,32,256]{2,1,0:T(8,128)(2,1)S(1)} %add_convert_fusion.1), channel_id=1, source_target_pairs={{0,3},{1,2},{2,1},{3,0},{4,7},{5,6},{6,5},{7,4},{8,24},{9,25},{10,... | collective-permute-start | bytes 737288 | tf_op jit(solution)/shard_map/ppermute | solution.py:43
  75.2 5.8 %collective-permute-start.19 = (bf16[12,32,256]{2,1,0:T(8,128)(2,1)S(1)}, bf16[12,32,256]{2,1,0:T(8,128)(2,1)S(1)}, u32[]{:S(2)}, u32[]{:S(2)}) collective-permute-start(bf16[12,32,256]{2,1,0:T(8,128)(2,1)S(1)} %add_convert_fusion.5), channel_id=1, source_target_pairs={{0,1},{1,0},{2,3},{3,2},{4,5},{5,4},{6,7},{7,6},{8,56},{9,57},{10,... | collective-permute-start | bytes 589832 | tf_op jit(solution)/shard_map/ppermute | solution.py:43
  80.3 7.4 %collective-permute-start.17 = (bf16[15,32,256]{2,1,0:T(8,128)(2,1)S(1)}, bf16[15,32,256]{2,1,0:T(8,128)(2,1)S(1)}, u32[]{:S(2)}, u32[]{:S(2)}) collective-permute-start(bf16[15,32,256]{2,1,0:T(8,128)(2,1)S(1)} %add_convert_fusion), channel_id=1, source_target_pairs={{0,4},{1,5},{2,6},{3,7},{4,0},{5,1},{6,2},{7,3},{8,9},{9,8},{10,11... | collective-permute-start | bytes 737288 | tf_op jit(solution)/shard_map/ppermute | solution.py:43
  81.1 13.7 %collective-permute-start.20 = (bf16[12,32,256]{2,1,0:T(8,128)(2,1)S(1)}, bf16[12,32,256]{2,1,0:T(8,128)(2,1)S(1)}, u32[]{:S(2)}, u32[]{:S(2)}) collective-permute-start(bf16[12,32,256]{2,1,0:T(8,128)(2,1)S(1)} %add_convert_fusion.4), channel_id=1, source_target_pairs={{0,68},{1,69},{2,70},{3,71},{4,64},{5,65},{6,66},{7,67},{8,11},{9,... | collective-permute-start | bytes 589832 | tf_op jit(solution)/shard_map/ppermute | solution.py:43
  87.8 10.1 %collective-permute-start.22 = (bf16[2,15,32,256]{3,2,1,0:T(8,128)(2,1)S(1)}, bf16[2,15,32,256]{3,2,1,0:T(8,128)(2,1)S(1)}, u32[]{:S(2)}, u32[]{:S(2)}) collective-permute-start(bf16[2,15,32,256]{3,2,1,0:T(8,128)(2,1)S(1)} %pad_maximum_fusion.refs_0_), channel_id=1, source_target_pairs={{0,8},{1,9},{2,10},{3,11},{4,12},{5,13},{6,14},{7,15},{8,0},{9,1},... | collective-permute-start | bytes 1474568 | tf_op jit(solution)/shard_map/ppermute | solution.py:43
  94.7 9.2 %collective-permute-start.18 = (bf16[2,15,32,256]{3,2,1,0:T(8,128)(2,1)S(1)}, bf16[2,15,32,256]{3,2,1,0:T(8,128)(2,1)S(1)}, u32[]{:S(2)}, u32[]{:S(2)}) collective-permute-start(bf16[2,15,32,256]{3,2,1,0:T(8,128)(2,1)S(1)} %pad_maximum_fusion.refs_0_), channel_id=1, source_target_pairs={{0,16},{1,17},{2,18},{3,19},{4,20},{5,21},{6,22},{7,23},{8,12},{9,... | collective-permute-start | bytes 1474568 | tf_op jit(solution)/shard_map/ppermute | solution.py:43
  94.8 3.1 %collective-permute-start.23 = (bf16[2,12,32,256]{3,2,1,0:T(8,128)(2,1)S(1)}, bf16[2,12,32,256]{3,2,1,0:T(8,128)(2,1)S(1)}, u32[]{:S(2)}, u32[]{:S(2)}) collective-permute-start(bf16[2,12,32,256]{3,2,1,0:T(8,128)(2,1)S(1)} %pad_maximum_fusion.1.refs_2_), channel_id=1, source_target_pairs={{0,8},{1,9},{2,10},{3,11},{4,12},{5,13},{6,14},{7,15},{8,0},{9,1},... | collective-permute-start | bytes 1179656 | tf_op jit(solution)/shard_map/ppermute | solution.py:43
  95.8 8.1 %collective-permute-start.21 = (bf16[2,12,32,256]{3,2,1,0:T(8,128)(2,1)S(1)}, bf16[2,12,32,256]{3,2,1,0:T(8,128)(2,1)S(1)}, u32[]{:S(2)}, u32[]{:S(2)}) collective-permute-start(bf16[2,12,32,256]{3,2,1,0:T(8,128)(2,1)S(1)} %pad_maximum_fusion.1.refs_2_), channel_id=1, source_target_pairs={{0,48},{1,49},{2,50},{3,51},{4,52},{5,53},{6,54},{7,55},{8,76},{9,... | collective-permute-start | bytes 1179656 | tf_op jit(solution)/shard_map/ppermute | solution.py:43
  103.9 3.0 %collective-permute-start.24 = (bf16[2,15,32,256]{3,2,1,0:T(8,128)(2,1)S(1)}, bf16[2,15,32,256]{3,2,1,0:T(8,128)(2,1)S(1)}, u32[]{:S(2)}, u32[]{:S(2)}) collective-permute-start(bf16[2,15,32,256]{3,2,1,0:T(8,128)(2,1)S(1)} %collective-permute-done.18.refs_0_), channel_id=1, source_target_pairs={{0,8},{1,9},{2,10},{3,11},{4,12},{5,13},{6,14},{7,15},{8,0},{9,1},... | collective-permute-start | bytes 1474568 | tf_op jit(solution)/shard_map/ppermute | solution.py:43
  104.9 2.1 %collective-permute-start.25 = (bf16[2,12,32,256]{3,2,1,0:T(8,128)(2,1)S(1)}, bf16[2,12,32,256]{3,2,1,0:T(8,128)(2,1)S(1)}, u32[]{:S(2)}, u32[]{:S(2)}) collective-permute-start(bf16[2,12,32,256]{3,2,1,0:T(8,128)(2,1)S(1)} %collective-permute-done.21.refs_1_), channel_id=1, source_target_pairs={{0,8},{1,9},{2,10},{3,11},{4,12},{5,13},{6,14},{7,15},{8,0},{9,1},... | collective-permute-start | bytes 1179656 | tf_op jit(solution)/shard_map/ppermute | solution.py:43
  (2 other events, 1.7 us)

commit v3 on v2

v3 whole, which is shorter than its diff:
```python
import functools

import jax
import jax.numpy as jnp
from jax import lax
from jax.experimental import pallas as pl
from jax.experimental.pallas import tpu as pltpu
from jax.sharding import PartitionSpec as P

AXES = ("gx", "gy")
F32, BF16 = jnp.float32, jnp.bfloat16
COUNT = 128
FIRSTS = ((0, 1), (3, 4))
ORDERS = tuple(
    tuple(tuple((first + step) % 6 for step in range(6)) for first in firsts) for firsts in FIRSTS
)
GROUPS = (5, 4)
CHAINS = len(GROUPS)


def place(index):
    gx, gy = index // 8, index % 8
    return (gx // 2) % 4, (gx // 8) * 2 + gy // 4, gy % 4, gx % 2


def index_of(x, y, z, core):
    return ((y // 2) * 8 + x * 2 + core) * 8 + (y % 2) * 4 + z


def step_pairs(chain, step):
    pairs = []
    for i in range(COUNT):
        *at, core = place(i)
        dim = ORDERS[chain][core][step]
        at[dim % 3] = at[dim % 3] ^ 1 if dim < 3 else 3 - at[dim % 3]
        pairs.append((i, index_of(*at, core)))
    return pairs


def core_pairs():
    return [(i, index_of(*place(i)[:3], 1 - place(i)[3])) for i in range(COUNT)]


def send(array, pairs):
    return lax.ppermute(array, AXES, pairs)


def where_am_i():
    gx, gy = lax.axis_index("gx"), lax.axis_index("gy")
    core = gx % 2
    at = [(gx // 2) % 4, (gx // 8) * 2 + gy // 4, gy % 4]
    side = [(v % 2) ^ (v // 2) for v in at] + [v // 2 for v in at]
    found = [core]
    for chain in range(CHAINS):
        quarters = [side[order[0]] * 2 + side[order[1]] for order in ORDERS[chain]]
        found.append(jnp.where(core == 0, quarters[0], quarters[1]))
        found.append(jnp.where(core == 0, quarters[1], quarters[0]))
    return jnp.stack(found).astype(jnp.int32)


def pair_swap(axis, first, array):
    count = lax.axis_size(axis)
    pairs = [(i, i + 1) for i in range(first, count - 1, 2)]
    return lax.ppermute(array, axis, pairs + [(b, a) for a, b in pairs])


def neighbours(axis, head, tail):
    even = lax.axis_index(axis) % 2 == 0
    one = pair_swap(axis, 0, jnp.where(even, tail, head))
    two = pair_swap(axis, 1, jnp.where(even, head, tail))
    return jnp.where(even, two, one), jnp.where(even, one, two)


def slabs(masked, mgrad, before, after):
    beside = [(b, a) for b, a in zip(before.reshape(3, 8, 8, 256), after.reshape(3, 8, 8, 256))]
    found = []
    for near, next_one in ((0, 1), (7, 6)):
        parts = []
        for line in (near, next_one):
            at = slice(line * 128, line * 128 + 128)
            parts += [beside[1][0][line], beside[0][0][line], masked[at], beside[0][1][line], beside[1][1][line]]
        at = slice(near * 128, near * 128 + 128)
        parts += [beside[2][0][near], mgrad[at], beside[2][1][near]]
        found.append(jnp.concatenate(parts))
    return found


def roll_cells(field, step):
    cells, chan = field.shape
    tall = field.reshape(cells // 8, 8, chan)
    level = lax.broadcasted_iota(jnp.int32, tall.shape, 1)
    moved = pltpu.roll(tall, step % 8, 1)
    kept = jnp.where((level >= step) & (level < 8 + step), moved, 0.0)
    return kept.reshape(cells, chan)


def dsilu(pre):
    sig = jax.nn.sigmoid(pre)
    return sig * (1.0 + pre * (1.0 - sig))


def brick_mask(occupied, bx, by):
    level = lax.broadcasted_iota(jnp.int32, (8, 256), 0)
    return jnp.where(level < 4, occupied[bx, 0, by], occupied[bx, 1, by]).astype(F32)


def line_mask(occupied, bx):
    return jnp.concatenate([brick_mask(occupied, bx, by) for by in range(4) for _ in range(4)], axis=0)


def mask_kernel(occupied, mask):
    for bx in range(2):
        lines = line_mask(occupied, bx).astype(BF16)
        for line in range(bx * 4, bx * 4 + 4):
            mask[line * 128 : line * 128 + 128, :] = lines


def levels(left, weights, oy_list, ox_list):
    pre = None
    for oz in range(3):
        right = jnp.concatenate([weights[ox * 3 + oy, oz] for ox in ox_list for oy in oy_list], axis=0)
        part = jnp.dot(left, right, preferred_element_type=F32)
        part = part if oz == 1 else roll_cells(part, 1 - oz)
        pre = part if pre is None else pre + part
    return pre


def inner_kernel(masked, before, after, weights, pre, turned, held, padded, copied):
    copy = pltpu.make_async_copy(weights, held, copied)
    copy.start()
    for side in range(3):
        padded[side, 0] = jnp.zeros((128, 256), BF16)
        padded[side, 9] = jnp.zeros((128, 256), BF16)
    for pair in range(4):
        left = before[pair * 16 : pair * 16 + 16, :].astype(F32)
        right = after[pair * 16 : pair * 16 + 16, :].astype(F32)
        for i in range(2):
            line = pair * 2 + i
            here = slice(line * 128, line * 128 + 128)
            value = masked[here, :]
            wide = value.astype(F32)
            low = jnp.concatenate([left[i * 8 : i * 8 + 8], wide[:120]], axis=0).astype(BF16)
            high = jnp.concatenate([wide[8:], right[i * 8 : i * 8 + 8]], axis=0).astype(BF16)
            for side, field in enumerate((low, value, high)):
                padded[side, 1 + line] = field
                turned[side, :, here] = field.T

    @pl.loop(0, 2)
    def _(step):
        pieces = [padded[oy, pl.ds(step * 4 + ox, 4)].reshape(512, 256) for ox in range(3) for oy in range(3)]
        here = pl.ds(pl.multiple_of(step * 512, 512), 512)
        pre[here, :] = levels(jnp.concatenate(pieces, axis=1), weights, (0, 1, 2), (0, 1, 2))

    copy.wait()


def chain_grads(at_ref, turned, ends, shifted, away, keep, chain):
    chan = 256
    core, mine, other = at_ref[0], at_ref[1 + 2 * chain], at_ref[2 + 2 * chain]
    for group in range(GROUPS[chain]):
        ox, oy = divmod(sum(GROUPS[:chain]) + group, 3)
        rows = []
        for half, quarter in ((core, mine), (1 - core, other)):
            for slot in range(4):
                here = pl.ds(pl.multiple_of(half * 128 + (quarter ^ slot) * 32, 32), 32)
                if ox == 0:
                    row = jnp.concatenate([ends[0, oy, here, :], turned[oy, here, 0:896]], axis=1)
                elif ox == 1:
                    row = turned[oy, here, :]
                else:
                    row = jnp.concatenate([turned[oy, here, 128:1024], ends[1, oy, here, :]], axis=1)
                rows.append(row)
        left = jnp.concatenate(rows, axis=0)
        for oz in range(3):
            part = jnp.dot(left, shifted[:, oz * chan : (oz + 1) * chan], preferred_element_type=F32)
            keep[:, :, group * 3 + oz] = part[:128].reshape(2, 2, 32, chan)
            away[:, :, group * 3 + oz] = part[128:].reshape(2, 2, 32, chan).astype(BF16)


def grads_kernel(at_ref, first, last, weights, pre, mgrad, turned, dpre, shifted, ends, away, keep):
    chan = 256
    lines = []
    for end, slab in ((0, first), (1, last)):
        line = slab[0:160, :].astype(F32)
        lines.append([line[8 + oy * 8 : 136 + oy * 8].astype(BF16) for oy in range(3)])
        for oy in range(3):
            ends[end, oy] = lines[end][oy].T
    for line in range(8):
        here = slice(line * 128, line * 128 + 128)
        value = pre[here, :]
        if line in (0, 7):
            end, ox = (0, 0) if line == 0 else (1, 2)
            value = value + levels(jnp.concatenate(lines[end], axis=1), weights, (0, 1, 2), (ox,))
        value = (mgrad[here, :].astype(F32) * dsilu(value)).astype(BF16)
        dpre[here, :] = value
        wide = value.astype(F32)
        shifted[here, 0:chan] = roll_cells(wide, -1).astype(BF16)
        shifted[here, chan : 2 * chan] = value
        shifted[here, 2 * chan : 3 * chan] = roll_cells(wide, 1).astype(BF16)
    chain_grads(at_ref, turned, ends, shifted, away, keep, 0)


def more_kernel(chain, at_ref, turned, ends, shifted, away, keep):
    chain_grads(at_ref, turned, ends, shifted, away, keep, chain)


def border_kernel(masked, before, after, first, last, weights, border, left):
    def cells(ref, start, stop):
        return ref[start:stop, :].astype(F32)

    def wide(line):
        near, at = slice(line * 8, line * 8 + 8), slice(line * 128, line * 128 + 128)
        return jnp.concatenate(
            [sides[0][1][near], sides[0][0][near], masked[at, :].astype(F32), sides[1][0][near], sides[1][1][near]], axis=0
        )

    sides = [[cells(ref, kind * 64, kind * 64 + 64) for kind in range(2)] for ref in (before, after)]
    ends = [[cells(ref, 0, 160), cells(ref, 160, 320)] for ref in (first, last)]
    edges = [[masked[x * 128 + y * 112 : x * 128 + y * 112 + 16, :].astype(F32) for x in range(8)] for y in range(2)]
    edge = [
        jnp.concatenate([v[:8] for v in edges[0]], axis=0),
        jnp.concatenate([v[8:] for v in edges[1]], axis=0),
    ]

    def column(index, body):
        at = slice(index * 8, index * 8 + 8)
        return jnp.concatenate([ends[0][0][at], body, ends[1][0][at]], axis=0)

    above = (ends[0][1], ends[0][0], wide(0))
    below = (wide(7), ends[1][0], ends[1][1])
    low = (column(0, sides[0][1]), column(1, sides[0][0]), column(2, edge[0]))
    high = (column(17, edge[1]), column(18, sides[1][0]), column(19, sides[1][1]))
    for ox in range(3):
        for oy in range(3):
            parts = [above[ox][oy * 8 : oy * 8 + 144], below[ox][oy * 8 : oy * 8 + 144]]
            parts += [low[oy][ox * 8 : ox * 8 + 64], high[oy][ox * 8 : ox * 8 + 64]]
            k = (ox * 3 + oy) * 256
            left[:, k : k + 256] = jnp.concatenate(parts, axis=0).astype(BF16)
    pre = None
    for oz in range(3):
        part = jnp.dot(left[...], weights[:, oz].reshape(2304, 256), preferred_element_type=F32)
        part = part if oz == 1 else roll_cells(part, 1 - oz)
        pre = part if pre is None else pre + part
    grad = [cells(first, 320, 464), cells(last, 320, 464), cells(before, 128, 192), cells(after, 128, 192)]
    border[...] = (jnp.concatenate(grad, axis=0) * dsilu(pre)).astype(BF16)


def input_kernel(part, occupied, dpre, border, weights, out, views):
    tile, chan = 512, 256
    lines = tile // 128

    line, start = ((0, 0), (5, 144))[part]
    value = border[start : start + 144, :].astype(F32)
    for side in range(3):
        views[side, line] = value[side * 8 : side * 8 + 128].astype(BF16)
    for pair in range(part, part + 3):
        low = border[288 + pair * 16 : 304 + pair * 16, :].astype(F32)
        high = border[352 + pair * 16 : 368 + pair * 16, :].astype(F32)
        for i in range(2):
            line = pair * 2 + i
            slot = line + 1 - part * 4
            if not 0 <= slot <= 5:
                continue
            value = dpre[line * 128 : line * 128 + 128, :]
            views[1, slot] = value
            value = value.astype(F32)
            views[0, slot] = jnp.concatenate([low[i * 8 : i * 8 + 8], value[:120]], axis=0).astype(BF16)
            views[2, slot] = jnp.concatenate([value[8:], high[i * 8 : i * 8 + 8]], axis=0).astype(BF16)

    pieces = []
    for ox in range(3):
        for oy in range(3):
            pieces.append(views[2 - oy, 2 - ox : 6 - ox].reshape(tile, chan))
    left = jnp.concatenate(pieces, axis=1)
    total = None
    for oz in range(3):
        right = jnp.concatenate([weights[k, oz] for k in range(9)], axis=1)
        field = lax.dot_general(left, right, (((1,), (1,)), ((), ())), preferred_element_type=F32)
        field = field if oz == 1 else roll_cells(field, oz - 1)
        total = field if total is None else total + field
    out[...] = (total * jnp.concatenate([line_mask(occupied, part)] * lines, axis=0)).astype(BF16)


def place_kernel(parts, at_ref, *refs):
    pieces, out, built, done = refs[: CHAINS * len(parts)], refs[-3], refs[-2], refs[-1]
    copies = []
    for index, (far, side) in enumerate(parts):
        half = at_ref[0] if side == 0 else 1 - at_ref[0]
        for chain in range(CHAINS):
            quarter = at_ref[1 + 2 * chain + side]
            row = pl.multiple_of(half * 128 + ((quarter // 2) ^ far) * 64, 64)
            for group in range(GROUPS[chain]):
                first = 3 * (sum(GROUPS[:chain]) + group)
                here = slice(first, first + 3)
                for slot in range(2):
                    start = pl.multiple_of(((quarter % 2) ^ slot) * 32, 32)
                    value = pieces[index * CHAINS + chain][slot, group * 3 : group * 3 + 3]
                    built[index, here, pl.ds(start, 32), :] = value.astype(F32)
                copy = pltpu.make_async_copy(
                    built.at[index, here], out.at[here, pl.ds(row, 64), :], done.at[len(copies)]
                )
                copy.start()
                copies.append(copy)
    for copy in copies:
        copy.wait()


VMEM = pl.BlockSpec(memory_space=pltpu.VMEM)
SMEM = pl.BlockSpec(memory_space=pltpu.SMEM)
HBM = pl.BlockSpec(memory_space=pltpu.HBM)


def shape(*dims, dtype=BF16):
    return jax.ShapeDtypeStruct(dims, dtype)


def chain_shapes(chain):
    dims = (2, 2, 3 * GROUPS[chain], 32, 256)
    return shape(*dims), shape(*dims, dtype=F32)


def kernel(body, outs, specs, args, flops, scratch=(), out_specs=None, aliases=None, nbytes=6_000_000, room=20):
    return pl.pallas_call(
        body,
        out_shape=outs,
        in_specs=specs,
        out_specs=out_specs if out_specs is not None else jax.tree.map(lambda _: VMEM, outs),
        scratch_shapes=scratch,
        input_output_aliases=aliases or {},
        compiler_params=pltpu.CompilerParams(vmem_limit_bytes=room * 2**20),
        cost_estimate=pl.CostEstimate(flops=flops, bytes_accessed=nbytes, transcendentals=0),
    )(*args)


def put_in_place(parts, at, pieces, out=None):
    more = () if out is None else (out,)
    return kernel(
        functools.partial(place_kernel, parts),
        shape(27, 256, 256, dtype=F32),
        [SMEM] + [VMEM] * len(pieces) + [HBM] * len(more),
        (at, *pieces, *more),
        0,
        [pltpu.VMEM((len(parts), 27, 64, 256), F32), pltpu.SemaphoreType.DMA((9 * len(parts),))],
        HBM,
        {1 + len(pieces): 0} if more else {},
        nbytes=10_000_000,
    )


CONV = 3_623_878_656


def local(features, grad_out, weights, occupied):
    at = where_am_i()
    cells, chan = 1024, 256
    packed = weights.reshape(9, 3, chan, chan)
    occupied = jnp.transpose(occupied, (0, 2, 1))
    mask = kernel(mask_kernel, shape(cells, chan), [SMEM], (occupied,), 0, nbytes=500_000).reshape(features.shape)
    masked, mgrad = features * mask, grad_out * mask
    head, tail = (
        jnp.concatenate([v.reshape(64, chan) for v in (masked[:, a], masked[:, b], mgrad[:, a])]) for a, b in ((0, 1), (15, 14))
    )
    masked, mgrad = masked.reshape(cells, chan), mgrad.reshape(cells, chan)
    before, after = neighbours("gy", head, tail)
    first, last_line = neighbours("gx", *slabs(masked, mgrad, before, after))
    pre, turned, held = kernel(
        inner_kernel,
        (shape(cells, chan, dtype=F32), shape(3, chan, cells), shape(9, 3, chan, chan)),
        [VMEM] * 4,
        (masked, before, after, packed),
        CONV,
        [pltpu.VMEM((3, 10, 128, chan), BF16), pltpu.SemaphoreType.DMA],
    )
    dpre, shifted, ends, away, keep = kernel(
        grads_kernel,
        (shape(cells, chan), shape(cells, 3 * chan), shape(2, 3, chan, 128), *chain_shapes(0)),
        [SMEM] + [VMEM] * 6,
        (at, first, last_line, held, pre, mgrad, turned),
        CONV // 2,
    )
    got, keeps, tie = [], [keep], lax.optimization_barrier
    for chain in range(CHAINS):
        got.append(send(away, core_pairs()))
        if chain < CHAINS - 1:
            away, keep = kernel(
                functools.partial(more_kernel, chain + 1),
                chain_shapes(chain + 1),
                [SMEM] + [VMEM] * 3,
                (at, turned, ends, shifted),
                CONV // 3,
            )
            keeps.append(keep)
            away, got[chain] = tie((away, got[chain]))
    halves = []
    sums = [keep + g.astype(F32) for keep, g in zip(keeps, got)]
    for step in range(6):
        for chain in range(CHAINS):
            give = sums[chain][1].astype(BF16) if step < 2 else sums[chain]
            got[chain] = send(give, step_pairs(chain, step))
        if step == 3:
            border = kernel(
                border_kernel,
                shape(416, chan),
                [VMEM] * 6,
                (masked, before, after, first, last_line, packed),
                CONV // 2,
                [pltpu.VMEM((416, 9 * chan), BF16)],
            )
            got[0], border = tie((got[0], border))
        if step > 3:
            half = kernel(
                functools.partial(input_kernel, step - 4),
                shape(cells // 2, chan),
                [SMEM, VMEM, VMEM, VMEM],
                (occupied, dpre, border, packed),
                CONV // 2,
                [pltpu.VMEM((3, 6, 128, chan), BF16)],
            )
            got[0], half = tie((got[0], half))
            halves.append(half)
        for chain in range(CHAINS):
            if chain == 0 and step:
                got[0], sums[-1] = tie((got[0], sums[-1]))
            own = sums[chain][0] if step < 2 else sums[chain]
            total = own.astype(F32) + got[chain].astype(F32)
            sums[chain] = total if step < 1 else total.astype(BF16)
    for chain in range(CHAINS):
        got[chain] = send(sums[chain], step_pairs(chain, 1))
    grad_features = jnp.concatenate(halves)
    got[0], sums[-1], grad_features = tie((got[0], sums[-1], grad_features))
    nears, fars = [], []
    for chain in range(CHAINS):
        nears.append(jnp.stack([sums[chain], got[chain]]))
        fars.append(send(nears[chain], step_pairs(chain, 0)))
    out = put_in_place(((0, 0),), at, nears)
    fars[0], out, *nears = tie((fars[0], out, *nears))
    other_nears = [send(near, core_pairs()) for near in nears]
    others = [send(far, core_pairs()) for far in fars]
    out = put_in_place(((1, 0), (0, 1)), at, fars + other_nears, out)
    out = put_in_place(((1, 1),), at, others, out)
    return grad_features.reshape(features.shape), out


def solution(mesh):
    return jax.shard_map(
        local,
        mesh=mesh,
        in_specs=(P("gx", "gy", None, None), P("gx", "gy", None, None), P(), P("gx", "gy", None)),
        out_specs=(P("gx", "gy", None, None), P()),
        check_vma=False,
    )
```

time: 109 us -> 105 us (0.963)
  local copies, waits for them, and re-layouts: 8.88 us -> 3.02 us
  starting transfers between devices: 42.5 us -> 47.9 us
  Pallas kernels: 27.1 us -> 24.6 us
  waiting for transfers between devices: 26.5 us -> 24.3 us
  other arithmetic: 2.52 us -> 3.99 us
    unnamed x28 -> x20, local copies, waits for them, and re-layouts: 8.62 us -> 2.75 us
    ppermute x22, waiting for transfers between devices: 26.5 us -> 22.3 us  [send(): return lax.ppermute(array, AXES, pairs)]
    ppermute x4, starting transfers between devices: 7.15 us -> 11 us  [pair_swap(): return lax.ppermute(array, axis, pairs + [(b, a) for a, b in pairs])]
    pallas_call x10, Pallas kernels: 27.1 us -> 24.6 us  [kernel(): pl.pallas_call(body, out_shape=outs, in_specs=specs, out_specs=out_specs...]
    ppermute x4, waiting for transfers between devices: 0.01 us -> 1.93 us  [pair_swap(): return lax.ppermute(array, axis, pairs + [(b, a) for a, b in pairs])]
    ppermute x22, starting transfers between devices: 35.3 us -> 36.9 us  [send(): return lax.ppermute(array, AXES, pairs)]
    mul x0 -> x1, other arithmetic: none -> 1.3 us  [local(): masked, mgrad = (features * mask, grad_out * mask)]
  transfers between devices with their start and end apart: 26 -> 26, of which waited for: 14 -> 12; matrix products, arithmetic and copies ran while one was open for 2% -> 3% of each run, Pallas kernels for 19% -> 18%
where the time goes in v3:
time: 105 us
  starting transfers between devices  47.9 us (46%)
  Pallas kernels  24.6 us (23%)
  waiting for transfers between devices  24.3 us (23%)
  other arithmetic  3.99 us (4%)
  local copies, waits for them, and re-layouts  3.02 us (3%)
  between operations  1.31 us (1%)
    ppermute x22, starting transfers between devices, send(): return lax.ppermute(array, AXES, pairs)  36.9 us
    pallas_call x10, Pallas kernels, kernel(): pl.pallas_call(body, out_shape=outs, in_specs=specs, out_specs=out_specs...  24.6 us
    ppermute x22, waiting for transfers between devices, send(): return lax.ppermute(array, AXES, pairs)  22.3 us
    ppermute x4, starting transfers between devices, pair_swap(): return lax.ppermute(array, axis, pairs + [(b, a) for a, b in pairs])  11 us
    unnamed x20, local copies, waits for them, and re-layouts  2.75 us
  transfers between devices with their start and end apart: 26, of which 12 were waited for; matrix products, arithmetic and copies ran while one was open for 3% of the time, Pallas kernels for 18%

profile of v3, /device:TPU:1, one launch (start us, length us, event | category | flops | bytes accessed | tf_op | source)
XLA Modules:
  0.0 105.1 jit_solution(10085793161169034786)
XLA Ops:
  1.9 1.3 %fusion.15 = (bf16[8,16,8,256]{3,2,1,0:T(8,128)(2,1)S(1)}, bf16[8,16,8,256]{3,2,1,0:T(8,128)(2,1)S(1)}) fusion(bf16[8,16,8,256]{3,2,1,0:T(8,128)(2,1)} %param.4, bf16[8,16,8,256]{3,2,1,0:T(8,128)(2,1)S(1)} %bitcast.78, bf16[8,16,8,256]{3,2,1,0:T(8,128)(2,1)} %param.5), kind=kLoop, calls=%fused_computation.78 | loop fusion | flops 524288 | bytes 2621440 | tf_op jit(solution)/shard_map/mul | solution.py:359
  4.0 5.4 %collective-permute-start.1 = (bf16[192,256]{1,0:T(8,128)(2,1)S(1)}, bf16[192,256]{1,0:T(8,128)(2,1)S(1)}, u32[]{:S(2)}, u32[]{:S(2)}) collective-permute-start(bf16[192,256]{1,0:T(8,128)(2,1)S(1)} %get-tuple-element.92), channel_id=1, source_target_pairs={{0,1},{2,3},{4,5},{6,7},{1,0},{3,2},{5,4},{7,6},{8,9},{10,11},{12,... | collective-permute-start | bytes 294920 | tf_op jit(solution)/shard_map/ppermute | solution.py:64
  9.5 1.9 %collective-permute-done.1 = bf16[192,256]{1,0:T(8,128)(2,1)S(1)} collective-permute-done((bf16[192,256]{1,0:T(8,128)(2,1)S(1)}, bf16[192,256]{1,0:T(8,128)(2,1)S(1)}, u32[]{:S(2)}, u32[]{:S(2)}) %collective-permute-start.1) | collective-permute-done | bytes 98336 | tf_op jit(solution)/shard_map/ppermute | solution.py:64
  11.7 4.8 %collective-permute-start.2 = (bf16[464,256]{1,0:T(8,128)(2,1)S(1)}, bf16[464,256]{1,0:T(8,128)(2,1)S(1)}, u32[]{:S(2)}, u32[]{:S(2)}) collective-permute-start(bf16[464,256]{1,0:T(8,128)(2,1)S(1)} %get-tuple-element.89), channel_id=1, source_target_pairs={{8,16},{24,32},{40,48},{56,64},{72,80},{88,96},{104,112},{16,8},{3... | collective-permute-start | bytes 712712 | tf_op jit(solution)/shard_map/ppermute | solution.py:64
  16.6 2.0 %copy-done.2 = bf16[27,256,256]{2,1,0:T(8,128)(2,1)S(1)} copy-done((bf16[27,256,256]{2,1,0:T(8,128)(2,1)S(1)}, bf16[27,256,256]{2,1,0:T(8,128)(2,1)}, u32[]{:S(2)}) %copy-start.2) | copy-done | bytes 3538968
  18.6 5.0 %shard_map.60 = (f32[1024,256]{1,0:T(8,128)S(1)}, bf16[3,256,1024]{2,1,0:T(8,128)(2,1)S(1)}, bf16[9,3,256,256]{3,2,1,0:T(8,128)(2,1)S(1)}) custom-call(bf16[1024,256]{1,0:T(8,128)(2,1)S(1)} %bitcast.79, bf16[192,256]{1,0:T(8,128)(2,1)S(1)} %get-tuple-element.91.before, bf16[192,256]{1,0:T(8,128)(2,1)S(1)} %get-tuple-element.90.after, ...), custom_call_target="tpu_custom_call" | custom-call | flops 3623878656 | bytes 6000000 | tf_op jit(solution)/shard_map/pallas_call | solution.py:323
  23.7 3.5 %shard_map.61 = (bf16[1024,256]{1,0:T(8,128)(2,1)S(1)}, bf16[1024,768]{1,0:T(8,128)(2,1)S(1)}, bf16[2,3,256,128]{3,2,1,0:T(8,128)(2,1)S(1)}, bf16[2,2,15,32,256]...) custom-call(s32[5]{0:T(128)S(1)} %stack.41.at_ref, bf16[464,256]{1,0:T(8,128)(2,1)S(1)} %get-tuple-element.87.first, ...), custom_call_target="tpu_custom_call" | custom-call | flops 1811939328 | bytes 6000000 | tf_op jit(solution)/shard_map/pallas_call | solution.py:323
  27.8 2.4 %shard_map.62 = (bf16[2,2,12,32,256]{4,3,2,1,0:T(8,128)(2,1)S(1)}, f32[2,2,12,32,256]{4,3,2,1,0:T(8,128)S(1)}) custom-call(s32[5]{0:T(128)S(1)} %stack.41.at_ref, bf16[3,256,1024]{2,1,0:T(8,128)(2,1)S(1)} %get-tuple-element.39.turned, bf16[2,3,256,128]{3,2,1,0:T(8,128)(2,1)S(1)} %get-tuple-element.41.ends, bf16[1024,768]{1,0:T(8,128)(2,1)S(1)} %get-tuple-element.42.shifted), custom_call_target="tpu_custom_call" | custom-call | flops 1207959552 | bytes 6000000 | tf_op jit(solution)/shard_map/pallas_call | solution.py:323
  30.9 3.5 %collective-permute-start.5 = (bf16[2,15,32,256]{3,2,1,0:T(8,128)(2,1)S(1)}, bf16[2,15,32,256]{3,2,1,0:T(8,128)(2,1)S(1)}, u32[]{:S(2)}, u32[]{:S(2)}) collective-permute-start(bf16[2,15,32,256]{3,2,1,0:T(8,128)(2,1)S(1)} %fusion.2), channel_id=1, source_target_pairs={{0,16},{1,17},{2,18},{3,19},{4,20},{5,21},{6,22},{7,23},{8,12},{9,... | collective-permute-start | bytes 1474568 | tf_op jit(solution)/shard_map/ppermute | solution.py:45
  34.7 3.8 %collective-permute-start.8 = (bf16[2,12,32,256]{3,2,1,0:T(8,128)(2,1)S(1)}, bf16[2,12,32,256]{3,2,1,0:T(8,128)(2,1)S(1)}, u32[]{:S(2)}, u32[]{:S(2)}) collective-permute-start(bf16[2,12,32,256]{3,2,1,0:T(8,128)(2,1)S(1)} %fusion.5), channel_id=1, source_target_pairs={{0,48},{1,49},{2,50},{3,51},{4,52},{5,53},{6,54},{7,55},{8,76},{9,... | collective-permute-start | bytes 1179656 | tf_op jit(solution)/shard_map/ppermute | solution.py:45
  38.5 2.4 %collective-permute-done.5 = bf16[2,15,32,256]{3,2,1,0:T(8,128)(2,1)S(1)} collective-permute-done((bf16[2,15,32,256]{3,2,1,0:T(8,128)(2,1)S(1)}, bf16[2,15,32,256]{3,2,1,0:T(8,128)(2,1)S(1)}, u32[]{:S(2)}, u32[]{:S(2)}) %collective-permute-start.5) | collective-permute-done | bytes 491552 | tf_op jit(solution)/shard_map/ppermute | solution.py:45
  41.2 2.5 %collective-permute-done.8 = bf16[2,12,32,256]{3,2,1,0:T(8,128)(2,1)S(1)} collective-permute-done((bf16[2,12,32,256]{3,2,1,0:T(8,128)(2,1)S(1)}, bf16[2,12,32,256]{3,2,1,0:T(8,128)(2,1)S(1)}, u32[]{:S(2)}, u32[]{:S(2)}) %collective-permute-start.8) | collective-permute-done | bytes 393248 | tf_op jit(solution)/shard_map/ppermute | solution.py:45
  43.8 1.4 %collective-permute-start.10 = (bf16[12,32,256]{2,1,0:T(8,128)(2,1)S(1)}, bf16[12,32,256]{2,1,0:T(8,128)(2,1)S(1)}, u32[]{:S(2)}, u32[]{:S(2)}) collective-permute-start(bf16[12,32,256]{2,1,0:T(8,128)(2,1)S(1)} %fusion.8), channel_id=1, source_target_pairs={{0,68},{1,69},{2,70},{3,71},{4,64},{5,65},{6,66},{7,67},{8,11},{9,... | collective-permute-start | bytes 589832 | tf_op jit(solution)/shard_map/ppermute | solution.py:45
  46.6 3.6 %collective-permute-start.9 = (bf16[15,32,256]{2,1,0:T(8,128)(2,1)S(1)}, bf16[15,32,256]{2,1,0:T(8,128)(2,1)S(1)}, u32[]{:S(2)}, u32[]{:S(2)}) collective-permute-start(bf16[15,32,256]{2,1,0:T(8,128)(2,1)S(1)} %fusion.4), channel_id=1, source_target_pairs={{0,1},{1,0},{2,3},{3,2},{4,5},{5,4},{6,7},{7,6},{8,56},{9,57},{10,... | collective-permute-start | bytes 737288 | tf_op jit(solution)/shard_map/ppermute | solution.py:45
  50.8 2.9 %collective-permute-done.9 = bf16[15,32,256]{2,1,0:T(8,128)(2,1)S(1)} collective-permute-done((bf16[15,32,256]{2,1,0:T(8,128)(2,1)S(1)}, bf16[15,32,256]{2,1,0:T(8,128)(2,1)S(1)}, u32[]{:S(2)}, u32[]{:S(2)}) %collective-permute-start.9) | collective-permute-done | bytes 245792 | tf_op jit(solution)/shard_map/ppermute | solution.py:45
  53.8 3.1 %collective-permute-start.11 = (bf16[15,32,256]{2,1,0:T(8,128)(2,1)S(1)}, bf16[15,32,256]{2,1,0:T(8,128)(2,1)S(1)}, u32[]{:S(2)}, u32[]{:S(2)}) collective-permute-start(bf16[15,32,256]{2,1,0:T(8,128)(2,1)S(1)} %add_convert_fusion.3), channel_id=1, source_target_pairs={{0,48},{1,49},{2,50},{3,51},{4,52},{5,53},{6,54},{7,55},{8,76},{9,... | collective-permute-start | bytes 737288 | tf_op jit(solution)/shard_map/ppermute | solution.py:45
  56.9 1.7 %shard_map.63.border = bf16[416,256]{1,0:T(8,128)(2,1)S(1)} custom-call(bf16[1024,256]{1,0:T(8,128)(2,1)S(1)} %bitcast.80, bf16[192,256]{1,0:T(8,128)(2,1)S(1)} %get-tuple-element.91.before, bf16[192,256]{1,0:T(8,128)(2,1)S(1)} %get-tuple-element.90.after, bf16[464,256]{1,0:T(8,128)(2,1)S(1)} %get-tuple-element.87.first, ...), custom_call_target="tpu_custom_call" | custom-call | flops 1811939328 | bytes 6000000 | tf_op jit(solution)/shard_map/pallas_call | solution.py:323
  58.8 2.0 %collective-permute-done.11 = bf16[15,32,256]{2,1,0:T(8,128)(2,1)S(1)} collective-permute-done((bf16[15,32,256]{2,1,0:T(8,128)(2,1)S(1)}, bf16[15,32,256]{2,1,0:T(8,128)(2,1)S(1)}, u32[]{:S(2)}, u32[]{:S(2)}) %collective-permute-start.11) | collective-permute-done | bytes 245792 | tf_op jit(solution)/shard_map/ppermute | solution.py:45
  60.9 2.6 %collective-permute-start.13 = (bf16[15,32,256]{2,1,0:T(8,128)(2,1)S(1)}, bf16[15,32,256]{2,1,0:T(8,128)(2,1)S(1)}, u32[]{:S(2)}, u32[]{:S(2)}) collective-permute-start(bf16[15,32,256]{2,1,0:T(8,128)(2,1)S(1)} %add_convert_fusion.2), channel_id=1, source_target_pairs={{0,68},{1,69},{2,70},{3,71},{4,64},{5,65},{6,66},{7,67},{8,11},{9,... | collective-permute-start | bytes 737288 | tf_op jit(solution)/shard_map/ppermute | solution.py:45
  63.4 2.6 %shard_map.64 = bf16[512,256]{1,0:T(8,128)(2,1)S(1)} custom-call(s32[2,2,4]{2,1,0:T(2,128)S(1)} %bitcast.82, bf16[1024,256]{1,0:T(8,128)(2,1)S(1)} %get-tuple-element.54.dpre, bf16[416,256]{1,0:T(8,128)(2,1)S(1)} %shard_map.63.border, bf16[9,3,256,256]{3,2,1,0:T(8,128)(2,1)S(1)} %bitcast.86), custom_call_target="tpu_custom_call" | custom-call | flops 1811939328 | bytes 6000000 | tf_op jit(solution)/shard_map/pallas_call | solution.py:323
  67.4 2.6 %shard_map.65 = bf16[512,256]{1,0:T(8,128)(2,1)S(1)} custom-call(s32[2,2,4]{2,1,0:T(2,128)S(1)} %bitcast.83, bf16[1024,256]{1,0:T(8,128)(2,1)S(1)} %get-tuple-element.54.dpre, bf16[416,256]{1,0:T(8,128)(2,1)S(1)} %shard_map.63.border, bf16[9,3,256,256]{3,2,1,0:T(8,128)(2,1)S(1)} %bitcast.87), custom_call_target="tpu_custom_call" | custom-call | flops 1811939328 | bytes 6000000 | tf_op jit(solution)/shard_map/pallas_call | solution.py:323
  70.8 3.0 %collective-permute-start.18 = (bf16[12,32,256]{2,1,0:T(8,128)(2,1)S(1)}, bf16[12,32,256]{2,1,0:T(8,128)(2,1)S(1)}, u32[]{:S(2)}, u32[]{:S(2)}) collective-permute-start(bf16[12,32,256]{2,1,0:T(8,128)(2,1)S(1)} %add_convert_fusion.5), channel_id=1, source_target_pairs={{0,1},{1,0},{2,3},{3,2},{4,5},{5,4},{6,7},{7,6},{8,56},{9,57},{10,... | collective-permute-start | bytes 589832 | tf_op jit(solution)/shard_map/ppermute | solution.py:45
  74.8 2.3 %collective-permute-done.18 = bf16[12,32,256]{2,1,0:T(8,128)(2,1)S(1)} collective-permute-done((bf16[12,32,256]{2,1,0:T(8,128)(2,1)S(1)}, bf16[12,32,256]{2,1,0:T(8,128)(2,1)S(1)}, u32[]{:S(2)}, u32[]{:S(2)}) %collective-permute-start.18) | collective-permute-done | bytes 196640 | tf_op jit(solution)/shard_map/ppermute | solution.py:45
  77.2 1.5 %collective-permute-start.20 = (bf16[12,32,256]{2,1,0:T(8,128)(2,1)S(1)}, bf16[12,32,256]{2,1,0:T(8,128)(2,1)S(1)}, u32[]{:S(2)}, u32[]{:S(2)}) collective-permute-start(bf16[12,32,256]{2,1,0:T(8,128)(2,1)S(1)} %add_convert_fusion.4), channel_id=1, source_target_pairs={{0,68},{1,69},{2,70},{3,71},{4,64},{5,65},{6,66},{7,67},{8,11},{9,... | collective-permute-start | bytes 589832 | tf_op jit(solution)/shard_map/ppermute | solution.py:45
  79.2 3.9 %collective-permute-done.20 = bf16[12,32,256]{2,1,0:T(8,128)(2,1)S(1)} collective-permute-done((bf16[12,32,256]{2,1,0:T(8,128)(2,1)S(1)}, bf16[12,32,256]{2,1,0:T(8,128)(2,1)S(1)}, u32[]{:S(2)}, u32[]{:S(2)}) %collective-permute-start.20) | collective-permute-done | bytes 196640 | tf_op jit(solution)/shard_map/ppermute | solution.py:45
  83.1 1.7 %collective-permute-start.22 = (bf16[2,12,32,256]{3,2,1,0:T(8,128)(2,1)S(1)}, bf16[2,12,32,256]{3,2,1,0:T(8,128)(2,1)S(1)}, u32[]{:S(2)}, u32[]{:S(2)}) collective-permute-start(bf16[2,12,32,256]{3,2,1,0:T(8,128)(2,1)S(1)} %pad_maximum_fusion.2.refs_1_), channel_id=1, source_target_pairs={{0,48},{1,49},{2,50},{3,51},{4,52},{5,53},{6,54},{7,55},{8,76},{9,... | collective-permute-start | bytes 1179656 | tf_op jit(solution)/shard_map/ppermute | solution.py:45
  84.8 1.8 %shard_map.66.refs_4_ = f32[27,256,256]{2,1,0:T(8,128)} custom-call(s32[5]{0:T(128)S(1)} %stack.41.at_ref, bf16[2,15,32,256]{3,2,1,0:T(8,128)(2,1)S(1)} %pad_maximum_fusion.1.refs_0_, bf16[2,12,32,256]{3,2,1,0:T(8,128)(2,1)S(1)} %pad_maximum_fusion.2.refs_1_), custom_call_target="tpu_custom_call" | custom-call | bytes 10000000 | tf_op jit(solution)/shard_map/pallas_call | solution.py:323
  86.7 3.1 %collective-permute-done.19.refs_0_ = bf16[2,15,32,256]{3,2,1,0:T(8,128)(2,1)S(1)} collective-permute-done((bf16[2,15,32,256]{3,2,1,0:T(8,128)(2,1)S(1)}, bf16[2,15,32,256]{3,2,1,0:T(8,128)(2,1)S(1)}, u32[]{:S(2)}, u32[]{:S(2)}) %collective-permute-start.19) | collective-permute-done | bytes 491552 | tf_op jit(solution)/shard_map/ppermute | solution.py:45
  89.8 7.0 %collective-permute-start.24 = (bf16[2,15,32,256]{3,2,1,0:T(8,128)(2,1)S(1)}, bf16[2,15,32,256]{3,2,1,0:T(8,128)(2,1)S(1)}, u32[]{:S(2)}, u32[]{:S(2)}) collective-permute-start(bf16[2,15,32,256]{3,2,1,0:T(8,128)(2,1)S(1)} %pad_maximum_fusion.1.refs_0_), channel_id=1, source_target_pairs={{0,8},{1,9},{2,10},{3,11},{4,12},{5,13},{6,14},{7,15},{8,0},{9,1},... | collective-permute-start | bytes 1474568 | tf_op jit(solution)/shard_map/ppermute | solution.py:45
  97.3 3.3 %collective-permute-start.23 = (bf16[2,12,32,256]{3,2,1,0:T(8,128)(2,1)S(1)}, bf16[2,12,32,256]{3,2,1,0:T(8,128)(2,1)S(1)}, u32[]{:S(2)}, u32[]{:S(2)}) collective-permute-start(bf16[2,12,32,256]{3,2,1,0:T(8,128)(2,1)S(1)} %collective-permute-done.22.refs_1_), channel_id=1, source_target_pairs={{0,8},{1,9},{2,10},{3,11},{4,12},{5,13},{6,14},{7,15},{8,0},{9,1},... | collective-permute-start | bytes 1179656 | tf_op jit(solution)/shard_map/ppermute | solution.py:45
  100.6 2.5 %shard_map.67.refs_2_ = f32[27,256,256]{2,1,0:T(8,128)} custom-call(s32[5]{0:T(128)S(1)} %stack.41.at_ref, bf16[2,15,32,256]{3,2,1,0:T(8,128)(2,1)S(1)} %collective-permute-done.19.refs_0_, bf16[2,12,32,256]{3,2,1,0:T(8,128)(2,1)S(1)} %collective-permute-done.22.refs_1_, ...), custom_call_target="tpu_custom_call", output_to_operand_aliasing={{}: (5, {})} | custom-call | bytes 10000000 | tf_op jit(solution)/shard_map/pallas_call | solution.py:323
  103.1 1.8 %shard_map.68 = f32[27,256,256]{2,1,0:T(8,128)} custom-call(s32[5]{0:T(128)S(1)} %stack.41.at_ref, bf16[2,15,32,256]{3,2,1,0:T(8,128)(2,1)S(1)} %collective-permute-done.21.refs_0_, bf16[2,12,32,256]{3,2,1,0:T(8,128)(2,1)S(1)} %collective-permute-done.23.refs_1_, f32[27,256,256]{2,1,0:T(8,128)} %shard_map.67.refs_2_), custom_call_target="tpu_custom_call", output_to_operand_aliasing={{}: (3, {})} | custom-call | bytes 10000000 | tf_op jit(solution)/shard_map/pallas_call | solution.py:323
  (79 shorter events, 10.8 us)
Async XLA Ops:
  0.6 0.7 copy-start
  3.3 6.2 %collective-permute-start = (bf16[192,256]{1,0:T(8,128)(2,1)S(1)}, bf16[192,256]{1,0:T(8,128)(2,1)S(1)}, u32[]{:S(2)}, u32[]{:S(2)}) collective-permute-start(bf16[192,256]{1,0:T(8,128)(2,1)S(1)} %get-tuple-element.93), channel_id=1, source_target_pairs={{1,2},{3,4},{5,6},{2,1},{4,3},{6,5},{9,10},{11,12},{13,14},{10,9},... | collective-permute-start | bytes 294920 | tf_op jit(solution)/shard_map/ppermute | solution.py:64
  4.0 7.4 %collective-permute-start.1 = (bf16[192,256]{1,0:T(8,128)(2,1)S(1)}, bf16[192,256]{1,0:T(8,128)(2,1)S(1)}, u32[]{:S(2)}, u32[]{:S(2)}) collective-permute-start(bf16[192,256]{1,0:T(8,128)(2,1)S(1)} %get-tuple-element.92), channel_id=1, source_target_pairs={{0,1},{2,3},{4,5},{6,7},{1,0},{3,2},{5,4},{7,6},{8,9},{10,11},{12,... | collective-permute-start | bytes 294920 | tf_op jit(solution)/shard_map/ppermute | solution.py:64
  11.7 11.9 %collective-permute-start.2 = (bf16[464,256]{1,0:T(8,128)(2,1)S(1)}, bf16[464,256]{1,0:T(8,128)(2,1)S(1)}, u32[]{:S(2)}, u32[]{:S(2)}) collective-permute-start(bf16[464,256]{1,0:T(8,128)(2,1)S(1)} %get-tuple-element.89), channel_id=1, source_target_pairs={{8,16},{24,32},{40,48},{56,64},{72,80},{88,96},{104,112},{16,8},{3... | collective-permute-start | bytes 712712 | tf_op jit(solution)/shard_map/ppermute | solution.py:64
  16.5 7.1 %collective-permute-start.3 = (bf16[464,256]{1,0:T(8,128)(2,1)S(1)}, bf16[464,256]{1,0:T(8,128)(2,1)S(1)}, u32[]{:S(2)}, u32[]{:S(2)}) collective-permute-start(bf16[464,256]{1,0:T(8,128)(2,1)S(1)} %get-tuple-element.88), channel_id=1, source_target_pairs={{0,8},{16,24},{32,40},{48,56},{64,72},{80,88},{96,104},{112,120},{... | collective-permute-start | bytes 712712 | tf_op jit(solution)/shard_map/ppermute | solution.py:64
  16.6 2.0 %copy-start.2 = (bf16[27,256,256]{2,1,0:T(8,128)(2,1)S(1)}, bf16[27,256,256]{2,1,0:T(8,128)(2,1)}, u32[]{:S(2)}) copy-start(bf16[27,256,256]{2,1,0:T(8,128)(2,1)} %param.6) | copy-start | bytes 10616836
  27.2 2.9 %collective-permute-start.4 = (bf16[2,2,15,32,256]{4,3,2,1,0:T(8,128)(2,1)S(1)}, bf16[2,2,15,32,256]{4,3,2,1,0:T(8,128)(2,1)S(1)}, u32[]{:S(2)}, u32[]{:S(2)}) collective-permute-start(bf16[2,2,15,32,256]{4,3,2,1,0:T(8,128)(2,1)S(1)} %get-tuple-element.44), channel_id=1, source_target_pairs={{0,8},{1,9},{2,10},{3,11},{4,12},{5,13},{6,14},{7,15},{8,0},{9,1},... | collective-permute-start | bytes 2949128 | tf_op jit(solution)/shard_map/ppermute | solution.py:45
  30.2 4.2 %collective-permute-start.7 = (bf16[2,2,12,32,256]{4,3,2,1,0:T(8,128)(2,1)S(1)}, bf16[2,2,12,32,256]{4,3,2,1,0:T(8,128)(2,1)S(1)}, u32[]{:S(2)}, u32[]{:S(2)}) collective-permute-start(bf16[2,2,12,32,256]{4,3,2,1,0:T(8,128)(2,1)S(1)} %get-tuple-element.47), channel_id=1, source_target_pairs={{0,8},{1,9},{2,10},{3,11},{4,12},{5,13},{6,14},{7,15},{8,0},{9,1},... | collective-permute-start | bytes 2359304 | tf_op jit(solution)/shard_map/ppermute | solution.py:45
  30.9 10.0 %collective-permute-start.5 = (bf16[2,15,32,256]{3,2,1,0:T(8,128)(2,1)S(1)}, bf16[2,15,32,256]{3,2,1,0:T(8,128)(2,1)S(1)}, u32[]{:S(2)}, u32[]{:S(2)}) collective-permute-start(bf16[2,15,32,256]{3,2,1,0:T(8,128)(2,1)S(1)} %fusion.2), channel_id=1, source_target_pairs={{0,16},{1,17},{2,18},{3,19},{4,20},{5,21},{6,22},{7,23},{8,12},{9,... | collective-permute-start | bytes 1474568 | tf_op jit(solution)/shard_map/ppermute | solution.py:45
  34.7 9.0 %collective-permute-start.8 = (bf16[2,12,32,256]{3,2,1,0:T(8,128)(2,1)S(1)}, bf16[2,12,32,256]{3,2,1,0:T(8,128)(2,1)S(1)}, u32[]{:S(2)}, u32[]{:S(2)}) collective-permute-start(bf16[2,12,32,256]{3,2,1,0:T(8,128)(2,1)S(1)} %fusion.5), channel_id=1, source_target_pairs={{0,48},{1,49},{2,50},{3,51},{4,52},{5,53},{6,54},{7,55},{8,76},{9,... | collective-permute-start | bytes 1179656 | tf_op jit(solution)/shard_map/ppermute | solution.py:45
  41.1 15.8 %copy-start.3 = (bf16[27,256,256]{2,1,0:T(8,128)(2,1)S(1)}, bf16[27,256,256]{2,1,0:T(8,128)(2,1)}, u32[]{:S(2)}) copy-start(bf16[27,256,256]{2,1,0:T(8,128)(2,1)} %param.6) | copy-start | bytes 10616836
  41.1 5.4 %collective-permute-start.6 = (bf16[15,32,256]{2,1,0:T(8,128)(2,1)S(1)}, bf16[15,32,256]{2,1,0:T(8,128)(2,1)S(1)}, u32[]{:S(2)}, u32[]{:S(2)}) collective-permute-start(bf16[15,32,256]{2,1,0:T(8,128)(2,1)S(1)} %fusion.7), channel_id=1, source_target_pairs={{0,4},{1,5},{2,6},{3,7},{4,0},{5,1},{6,2},{7,3},{8,9},{9,8},{10,11... | collective-permute-start | bytes 737288 | tf_op jit(solution)/shard_map/ppermute | solution.py:45
  43.8 6.4 %collective-permute-start.10 = (bf16[12,32,256]{2,1,0:T(8,128)(2,1)S(1)}, bf16[12,32,256]{2,1,0:T(8,128)(2,1)S(1)}, u32[]{:S(2)}, u32[]{:S(2)}) collective-permute-start(bf16[12,32,256]{2,1,0:T(8,128)(2,1)S(1)} %fusion.8), channel_id=1, source_target_pairs={{0,68},{1,69},{2,70},{3,71},{4,64},{5,65},{6,66},{7,67},{8,11},{9,... | collective-permute-start | bytes 589832 | tf_op jit(solution)/shard_map/ppermute | solution.py:45
  46.6 7.2 %collective-permute-start.9 = (bf16[15,32,256]{2,1,0:T(8,128)(2,1)S(1)}, bf16[15,32,256]{2,1,0:T(8,128)(2,1)S(1)}, u32[]{:S(2)}, u32[]{:S(2)}) collective-permute-start(bf16[15,32,256]{2,1,0:T(8,128)(2,1)S(1)} %fusion.4), channel_id=1, source_target_pairs={{0,1},{1,0},{2,3},{3,2},{4,5},{5,4},{6,7},{7,6},{8,56},{9,57},{10,... | collective-permute-start | bytes 737288 | tf_op jit(solution)/shard_map/ppermute | solution.py:45
  50.2 8.4 %collective-permute-start.12 = (bf16[12,32,256]{2,1,0:T(8,128)(2,1)S(1)}, bf16[12,32,256]{2,1,0:T(8,128)(2,1)S(1)}, u32[]{:S(2)}, u32[]{:S(2)}) collective-permute-start(bf16[12,32,256]{2,1,0:T(8,128)(2,1)S(1)} %fusion.6), channel_id=1, source_target_pairs={{0,3},{1,2},{2,1},{3,0},{4,7},{5,6},{6,5},{7,4},{8,24},{9,25},{10,... | collective-permute-start | bytes 589832 | tf_op jit(solution)/shard_map/ppermute | solution.py:45
  53.8 9.6 %copy-start.1 = (s32[2,4,2]{1,2,0:T(2,128)S(1)}, s32[2,4,2]{1,2,0:T(2,128)}, u32[]{:S(2)}) copy-start(s32[2,4,2]{1,2,0:T(2,128)} %param.7) | copy-start | bytes 196
  53.8 6.9 %collective-permute-start.11 = (bf16[15,32,256]{2,1,0:T(8,128)(2,1)S(1)}, bf16[15,32,256]{2,1,0:T(8,128)(2,1)S(1)}, u32[]{:S(2)}, u32[]{:S(2)}) collective-permute-start(bf16[15,32,256]{2,1,0:T(8,128)(2,1)S(1)} %add_convert_fusion.3), channel_id=1, source_target_pairs={{0,48},{1,49},{2,50},{3,51},{4,52},{5,53},{6,54},{7,55},{8,76},{9,... | collective-permute-start | bytes 737288 | tf_op jit(solution)/shard_map/ppermute | solution.py:45
  58.7 7.3 %collective-permute-start.14 = (bf16[12,32,256]{2,1,0:T(8,128)(2,1)S(1)}, bf16[12,32,256]{2,1,0:T(8,128)(2,1)S(1)}, u32[]{:S(2)}, u32[]{:S(2)}) collective-permute-start(bf16[12,32,256]{2,1,0:T(8,128)(2,1)S(1)} %add_convert_fusion.7), channel_id=1, source_target_pairs={{0,16},{1,17},{2,18},{3,19},{4,20},{5,21},{6,22},{7,23},{8,12},{9,... | collective-permute-start | bytes 589832 | tf_op jit(solution)/shard_map/ppermute | solution.py:45
  60.9 6.3 %collective-permute-start.13 = (bf16[15,32,256]{2,1,0:T(8,128)(2,1)S(1)}, bf16[15,32,256]{2,1,0:T(8,128)(2,1)S(1)}, u32[]{:S(2)}, u32[]{:S(2)}) collective-permute-start(bf16[15,32,256]{2,1,0:T(8,128)(2,1)S(1)} %add_convert_fusion.2), channel_id=1, source_target_pairs={{0,68},{1,69},{2,70},{3,71},{4,64},{5,65},{6,66},{7,67},{8,11},{9,... | collective-permute-start | bytes 737288 | tf_op jit(solution)/shard_map/ppermute | solution.py:45
  66.1 4.6 %collective-permute-start.16 = (bf16[12,32,256]{2,1,0:T(8,128)(2,1)S(1)}, bf16[12,32,256]{2,1,0:T(8,128)(2,1)S(1)}, u32[]{:S(2)}, u32[]{:S(2)}) collective-permute-start(bf16[12,32,256]{2,1,0:T(8,128)(2,1)S(1)} %add_convert_fusion.6), channel_id=1, source_target_pairs={{0,4},{1,5},{2,6},{3,7},{4,0},{5,1},{6,2},{7,3},{8,9},{9,8},{10,11... | collective-permute-start | bytes 589832 | tf_op jit(solution)/shard_map/ppermute | solution.py:45
  67.3 6.5 %collective-permute-start.15 = (bf16[15,32,256]{2,1,0:T(8,128)(2,1)S(1)}, bf16[15,32,256]{2,1,0:T(8,128)(2,1)S(1)}, u32[]{:S(2)}, u32[]{:S(2)}) collective-permute-start(bf16[15,32,256]{2,1,0:T(8,128)(2,1)S(1)} %add_convert_fusion.1), channel_id=1, source_target_pairs={{0,3},{1,2},{2,1},{3,0},{4,7},{5,6},{6,5},{7,4},{8,24},{9,25},{10,... | collective-permute-start | bytes 737288 | tf_op jit(solution)/shard_map/ppermute | solution.py:45
  70.8 6.4 %collective-permute-start.18 = (bf16[12,32,256]{2,1,0:T(8,128)(2,1)S(1)}, bf16[12,32,256]{2,1,0:T(8,128)(2,1)S(1)}, u32[]{:S(2)}, u32[]{:S(2)}) collective-permute-start(bf16[12,32,256]{2,1,0:T(8,128)(2,1)S(1)} %add_convert_fusion.5), channel_id=1, source_target_pairs={{0,1},{1,0},{2,3},{3,2},{4,5},{5,4},{6,7},{7,6},{8,56},{9,57},{10,... | collective-permute-start | bytes 589832 | tf_op jit(solution)/shard_map/ppermute | solution.py:45
  73.9 5.1 %collective-permute-start.17 = (bf16[15,32,256]{2,1,0:T(8,128)(2,1)S(1)}, bf16[15,32,256]{2,1,0:T(8,128)(2,1)S(1)}, u32[]{:S(2)}, u32[]{:S(2)}) collective-permute-start(bf16[15,32,256]{2,1,0:T(8,128)(2,1)S(1)} %add_convert_fusion), channel_id=1, source_target_pairs={{0,4},{1,5},{2,6},{3,7},{4,0},{5,1},{6,2},{7,3},{8,9},{9,8},{10,11... | collective-permute-start | bytes 737288 | tf_op jit(solution)/shard_map/ppermute | solution.py:45
  77.2 5.8 %collective-permute-start.20 = (bf16[12,32,256]{2,1,0:T(8,128)(2,1)S(1)}, bf16[12,32,256]{2,1,0:T(8,128)(2,1)S(1)}, u32[]{:S(2)}, u32[]{:S(2)}) collective-permute-start(bf16[12,32,256]{2,1,0:T(8,128)(2,1)S(1)} %add_convert_fusion.4), channel_id=1, source_target_pairs={{0,68},{1,69},{2,70},{3,71},{4,64},{5,65},{6,66},{7,67},{8,11},{9,... | collective-permute-start | bytes 589832 | tf_op jit(solution)/shard_map/ppermute | solution.py:45
  79.1 10.7 %collective-permute-start.19 = (bf16[2,15,32,256]{3,2,1,0:T(8,128)(2,1)S(1)}, bf16[2,15,32,256]{3,2,1,0:T(8,128)(2,1)S(1)}, u32[]{:S(2)}, u32[]{:S(2)}) collective-permute-start(bf16[2,15,32,256]{3,2,1,0:T(8,128)(2,1)S(1)} %pad_maximum_fusion.1.refs_0_), channel_id=1, source_target_pairs={{0,16},{1,17},{2,18},{3,19},{4,20},{5,21},{6,22},{7,23},{8,12},{9,... | collective-permute-start | bytes 1474568 | tf_op jit(solution)/shard_map/ppermute | solution.py:45
  83.1 14.2 %collective-permute-start.22 = (bf16[2,12,32,256]{3,2,1,0:T(8,128)(2,1)S(1)}, bf16[2,12,32,256]{3,2,1,0:T(8,128)(2,1)S(1)}, u32[]{:S(2)}, u32[]{:S(2)}) collective-permute-start(bf16[2,12,32,256]{3,2,1,0:T(8,128)(2,1)S(1)} %pad_maximum_fusion.2.refs_1_), channel_id=1, source_target_pairs={{0,48},{1,49},{2,50},{3,51},{4,52},{5,53},{6,54},{7,55},{8,76},{9,... | collective-permute-start | bytes 1179656 | tf_op jit(solution)/shard_map/ppermute | solution.py:45
  89.8 10.8 %collective-permute-start.24 = (bf16[2,15,32,256]{3,2,1,0:T(8,128)(2,1)S(1)}, bf16[2,15,32,256]{3,2,1,0:T(8,128)(2,1)S(1)}, u32[]{:S(2)}, u32[]{:S(2)}) collective-permute-start(bf16[2,15,32,256]{3,2,1,0:T(8,128)(2,1)S(1)} %pad_maximum_fusion.1.refs_0_), channel_id=1, source_target_pairs={{0,8},{1,9},{2,10},{3,11},{4,12},{5,13},{6,14},{7,15},{8,0},{9,1},... | collective-permute-start | bytes 1474568 | tf_op jit(solution)/shard_map/ppermute | solution.py:45
  96.7 6.3 %collective-permute-start.21 = (bf16[2,15,32,256]{3,2,1,0:T(8,128)(2,1)S(1)}, bf16[2,15,32,256]{3,2,1,0:T(8,128)(2,1)S(1)}, u32[]{:S(2)}, u32[]{:S(2)}) collective-permute-start(bf16[2,15,32,256]{3,2,1,0:T(8,128)(2,1)S(1)} %collective-permute-done.19.refs_0_), channel_id=1, source_target_pairs={{0,8},{1,9},{2,10},{3,11},{4,12},{5,13},{6,14},{7,15},{8,0},{9,1},... | collective-permute-start | bytes 1474568 | tf_op jit(solution)/shard_map/ppermute | solution.py:45
  96.8 3.7 %collective-permute-start.25 = (bf16[2,12,32,256]{3,2,1,0:T(8,128)(2,1)S(1)}, bf16[2,12,32,256]{3,2,1,0:T(8,128)(2,1)S(1)}, u32[]{:S(2)}, u32[]{:S(2)}) collective-permute-start(bf16[2,12,32,256]{3,2,1,0:T(8,128)(2,1)S(1)} %pad_maximum_fusion.2.refs_1_), channel_id=1, source_target_pairs={{0,8},{1,9},{2,10},{3,11},{4,12},{5,13},{6,14},{7,15},{8,0},{9,1},... | collective-permute-start | bytes 1179656 | tf_op jit(solution)/shard_map/ppermute | solution.py:45
  97.3 5.8 %collective-permute-start.23 = (bf16[2,12,32,256]{3,2,1,0:T(8,128)(2,1)S(1)}, bf16[2,12,32,256]{3,2,1,0:T(8,128)(2,1)S(1)}, u32[]{:S(2)}, u32[]{:S(2)}) collective-permute-start(bf16[2,12,32,256]{3,2,1,0:T(8,128)(2,1)S(1)} %collective-permute-done.22.refs_1_), channel_id=1, source_target_pairs={{0,8},{1,9},{2,10},{3,11},{4,12},{5,13},{6,14},{7,15},{8,0},{9,1},... | collective-permute-start | bytes 1179656 | tf_op jit(solution)/shard_map/ppermute | solution.py:45

commit v4 on v3

--- a/solution.py
+++ b/solution.py
@@ -10,7 +10,7 @@
 AXES = ("gx", "gy")
 F32, BF16 = jnp.float32, jnp.bfloat16
 COUNT = 128
-FIRSTS = ((0, 1), (3, 4))
+FIRSTS = ((0, 2), (3, 5))
 ORDERS = tuple(
     tuple(tuple((first + step) % 6 for step in range(6)) for first in firsts) for firsts in FIRSTS
 )

time: 105 us -> 103 us (0.981)
  waiting for transfers between devices: 24.3 us -> 22.6 us
    ppermute x22, waiting for transfers between devices: 22.3 us -> 20.7 us  [send(): return lax.ppermute(array, AXES, pairs)]
  transfers between devices with their start and end apart: 26 -> 26, of which waited for: 12 -> 10; matrix products, arithmetic and copies ran while one was open for 3% -> 3% of each run, Pallas kernels for 18% -> 18%
where the time goes in v4:
time: 103 us
  starting transfers between devices  47.6 us (46%)
  Pallas kernels  24.6 us (24%)
  waiting for transfers between devices  22.6 us (22%)
  other arithmetic  3.99 us (4%)
  local copies, waits for them, and re-layouts  3.02 us (3%)
  between operations  1.32 us (1%)
    ppermute x22, starting transfers between devices, send(): return lax.ppermute(array, AXES, pairs)  36.6 us
    pallas_call x10, Pallas kernels, kernel(): pl.pallas_call(body, out_shape=outs, in_specs=specs, out_specs=out_specs...  24.6 us
    ppermute x22, waiting for transfers between devices, send(): return lax.ppermute(array, AXES, pairs)  20.7 us
    ppermute x4, starting transfers between devices, pair_swap(): return lax.ppermute(array, axis, pairs + [(b, a) for a, b in pairs])  11 us
    unnamed x20, local copies, waits for them, and re-layouts  2.75 us
  transfers between devices with their start and end apart: 26, of which 10 were waited for; matrix products, arithmetic and copies ran while one was open for 3% of the time, Pallas kernels for 18%

profile of v4, /device:TPU:1, one launch (start us, length us, event | category | flops | bytes accessed | tf_op | source)
XLA Modules:
  0.0 103.1 jit_solution(4255916679965576922)
XLA Ops:
  1.9 1.3 %fusion.15 = (bf16[8,16,8,256]{3,2,1,0:T(8,128)(2,1)S(1)}, bf16[8,16,8,256]{3,2,1,0:T(8,128)(2,1)S(1)}) fusion(bf16[8,16,8,256]{3,2,1,0:T(8,128)(2,1)} %param.4, bf16[8,16,8,256]{3,2,1,0:T(8,128)(2,1)S(1)} %bitcast.78, bf16[8,16,8,256]{3,2,1,0:T(8,128)(2,1)} %param.5), kind=kLoop, calls=%fused_computation.78 | loop fusion | flops 524288 | bytes 2621440 | tf_op jit(solution)/shard_map/mul | solution.py:359
  4.0 5.4 %collective-permute-start.1 = (bf16[192,256]{1,0:T(8,128)(2,1)S(1)}, bf16[192,256]{1,0:T(8,128)(2,1)S(1)}, u32[]{:S(2)}, u32[]{:S(2)}) collective-permute-start(bf16[192,256]{1,0:T(8,128)(2,1)S(1)} %get-tuple-element.92), channel_id=1, source_target_pairs={{0,1},{2,3},{4,5},{6,7},{1,0},{3,2},{5,4},{7,6},{8,9},{10,11},{12,... | collective-permute-start | bytes 294920 | tf_op jit(solution)/shard_map/ppermute | solution.py:64
  9.5 1.9 %collective-permute-done.1 = bf16[192,256]{1,0:T(8,128)(2,1)S(1)} collective-permute-done((bf16[192,256]{1,0:T(8,128)(2,1)S(1)}, bf16[192,256]{1,0:T(8,128)(2,1)S(1)}, u32[]{:S(2)}, u32[]{:S(2)}) %collective-permute-start.1) | collective-permute-done | bytes 98336 | tf_op jit(solution)/shard_map/ppermute | solution.py:64
  11.7 4.8 %collective-permute-start.2 = (bf16[464,256]{1,0:T(8,128)(2,1)S(1)}, bf16[464,256]{1,0:T(8,128)(2,1)S(1)}, u32[]{:S(2)}, u32[]{:S(2)}) collective-permute-start(bf16[464,256]{1,0:T(8,128)(2,1)S(1)} %get-tuple-element.89), channel_id=1, source_target_pairs={{8,16},{24,32},{40,48},{56,64},{72,80},{88,96},{104,112},{16,8},{3... | collective-permute-start | bytes 712712 | tf_op jit(solution)/shard_map/ppermute | solution.py:64
  16.6 2.0 %copy-done.2 = bf16[27,256,256]{2,1,0:T(8,128)(2,1)S(1)} copy-done((bf16[27,256,256]{2,1,0:T(8,128)(2,1)S(1)}, bf16[27,256,256]{2,1,0:T(8,128)(2,1)}, u32[]{:S(2)}) %copy-start.2) | copy-done | bytes 3538968
  18.6 5.0 %shard_map.60 = (f32[1024,256]{1,0:T(8,128)S(1)}, bf16[3,256,1024]{2,1,0:T(8,128)(2,1)S(1)}, bf16[9,3,256,256]{3,2,1,0:T(8,128)(2,1)S(1)}) custom-call(bf16[1024,256]{1,0:T(8,128)(2,1)S(1)} %bitcast.79, bf16[192,256]{1,0:T(8,128)(2,1)S(1)} %get-tuple-element.91.before, bf16[192,256]{1,0:T(8,128)(2,1)S(1)} %get-tuple-element.90.after, ...), custom_call_target="tpu_custom_call" | custom-call | flops 3623878656 | bytes 6000000 | tf_op jit(solution)/shard_map/pallas_call | solution.py:323
  23.7 3.5 %shard_map.61 = (bf16[1024,256]{1,0:T(8,128)(2,1)S(1)}, bf16[1024,768]{1,0:T(8,128)(2,1)S(1)}, bf16[2,3,256,128]{3,2,1,0:T(8,128)(2,1)S(1)}, bf16[2,2,15,32,256]...) custom-call(s32[5]{0:T(128)S(1)} %stack.41.at_ref, bf16[464,256]{1,0:T(8,128)(2,1)S(1)} %get-tuple-element.87.first, ...), custom_call_target="tpu_custom_call" | custom-call | flops 1811939328 | bytes 6000000 | tf_op jit(solution)/shard_map/pallas_call | solution.py:323
  27.8 2.4 %shard_map.62 = (bf16[2,2,12,32,256]{4,3,2,1,0:T(8,128)(2,1)S(1)}, f32[2,2,12,32,256]{4,3,2,1,0:T(8,128)S(1)}) custom-call(s32[5]{0:T(128)S(1)} %stack.41.at_ref, bf16[3,256,1024]{2,1,0:T(8,128)(2,1)S(1)} %get-tuple-element.39.turned, bf16[2,3,256,128]{3,2,1,0:T(8,128)(2,1)S(1)} %get-tuple-element.41.ends, bf16[1024,768]{1,0:T(8,128)(2,1)S(1)} %get-tuple-element.42.shifted), custom_call_target="tpu_custom_call" | custom-call | flops 1207959552 | bytes 6000000 | tf_op jit(solution)/shard_map/pallas_call | solution.py:323
  30.9 1.8 %collective-permute-start.5 = (bf16[2,15,32,256]{3,2,1,0:T(8,128)(2,1)S(1)}, bf16[2,15,32,256]{3,2,1,0:T(8,128)(2,1)S(1)}, u32[]{:S(2)}, u32[]{:S(2)}) collective-permute-start(bf16[2,15,32,256]{3,2,1,0:T(8,128)(2,1)S(1)} %fusion.2), channel_id=1, source_target_pairs={{0,16},{1,17},{2,18},{3,19},{4,20},{5,21},{6,22},{7,23},{8,9},{9,8... | collective-permute-start | bytes 1474568 | tf_op jit(solution)/shard_map/ppermute | solution.py:45
  33.0 3.9 %collective-permute-start.8 = (bf16[2,12,32,256]{3,2,1,0:T(8,128)(2,1)S(1)}, bf16[2,12,32,256]{3,2,1,0:T(8,128)(2,1)S(1)}, u32[]{:S(2)}, u32[]{:S(2)}) collective-permute-start(bf16[2,12,32,256]{3,2,1,0:T(8,128)(2,1)S(1)} %fusion.5), channel_id=1, source_target_pairs={{0,48},{1,49},{2,50},{3,51},{4,52},{5,53},{6,54},{7,55},{8,11},{9,... | collective-permute-start | bytes 1179656 | tf_op jit(solution)/shard_map/ppermute | solution.py:45
  36.9 2.3 %collective-permute-done.5 = bf16[2,15,32,256]{3,2,1,0:T(8,128)(2,1)S(1)} collective-permute-done((bf16[2,15,32,256]{3,2,1,0:T(8,128)(2,1)S(1)}, bf16[2,15,32,256]{3,2,1,0:T(8,128)(2,1)S(1)}, u32[]{:S(2)}, u32[]{:S(2)}) %collective-permute-start.5) | collective-permute-done | bytes 491552 | tf_op jit(solution)/shard_map/ppermute | solution.py:45
  39.4 4.2 %collective-permute-start.6 = (bf16[15,32,256]{2,1,0:T(8,128)(2,1)S(1)}, bf16[15,32,256]{2,1,0:T(8,128)(2,1)S(1)}, u32[]{:S(2)}, u32[]{:S(2)}) collective-permute-start(bf16[15,32,256]{2,1,0:T(8,128)(2,1)S(1)} %fusion.7), channel_id=1, source_target_pairs={{0,4},{1,5},{2,6},{3,7},{4,0},{5,1},{6,2},{7,3},{8,56},{9,57},{10,... | collective-permute-start | bytes 737288 | tf_op jit(solution)/shard_map/ppermute | solution.py:45
  43.8 3.4 %collective-permute-done.6 = bf16[15,32,256]{2,1,0:T(8,128)(2,1)S(1)} collective-permute-done((bf16[15,32,256]{2,1,0:T(8,128)(2,1)S(1)}, bf16[15,32,256]{2,1,0:T(8,128)(2,1)S(1)}, u32[]{:S(2)}, u32[]{:S(2)}) %collective-permute-start.6) | collective-permute-done | bytes 245792 | tf_op jit(solution)/shard_map/ppermute | solution.py:45
  47.3 3.9 %collective-permute-start.9 = (bf16[15,32,256]{2,1,0:T(8,128)(2,1)S(1)}, bf16[15,32,256]{2,1,0:T(8,128)(2,1)S(1)}, u32[]{:S(2)}, u32[]{:S(2)}) collective-permute-start(bf16[15,32,256]{2,1,0:T(8,128)(2,1)S(1)} %fusion.4), channel_id=1, source_target_pairs={{0,1},{1,0},{2,3},{3,2},{4,5},{5,4},{6,7},{7,6},{8,76},{9,77},{10,... | collective-permute-start | bytes 737288 | tf_op jit(solution)/shard_map/ppermute | solution.py:45
  51.4 3.4 %collective-permute-done.9 = bf16[15,32,256]{2,1,0:T(8,128)(2,1)S(1)} collective-permute-done((bf16[15,32,256]{2,1,0:T(8,128)(2,1)S(1)}, bf16[15,32,256]{2,1,0:T(8,128)(2,1)S(1)}, u32[]{:S(2)}, u32[]{:S(2)}) %collective-permute-start.9) | collective-permute-done | bytes 245792 | tf_op jit(solution)/shard_map/ppermute | solution.py:45
  54.9 2.7 %collective-permute-start.11 = (bf16[15,32,256]{2,1,0:T(8,128)(2,1)S(1)}, bf16[15,32,256]{2,1,0:T(8,128)(2,1)S(1)}, u32[]{:S(2)}, u32[]{:S(2)}) collective-permute-start(bf16[15,32,256]{2,1,0:T(8,128)(2,1)S(1)} %add_convert_fusion.3), channel_id=1, source_target_pairs={{0,48},{1,49},{2,50},{3,51},{4,52},{5,53},{6,54},{7,55},{8,11},{9,... | collective-permute-start | bytes 737288 | tf_op jit(solution)/shard_map/ppermute | solution.py:45
  57.6 1.7 %shard_map.63.border = bf16[416,256]{1,0:T(8,128)(2,1)S(1)} custom-call(bf16[1024,256]{1,0:T(8,128)(2,1)S(1)} %bitcast.80, bf16[192,256]{1,0:T(8,128)(2,1)S(1)} %get-tuple-element.91.before, bf16[192,256]{1,0:T(8,128)(2,1)S(1)} %get-tuple-element.90.after, bf16[464,256]{1,0:T(8,128)(2,1)S(1)} %get-tuple-element.87.first, ...), custom_call_target="tpu_custom_call" | custom-call | flops 1811939328 | bytes 6000000 | tf_op jit(solution)/shard_map/pallas_call | solution.py:323
  59.6 2.1 %collective-permute-done.11 = bf16[15,32,256]{2,1,0:T(8,128)(2,1)S(1)} collective-permute-done((bf16[15,32,256]{2,1,0:T(8,128)(2,1)S(1)}, bf16[15,32,256]{2,1,0:T(8,128)(2,1)S(1)}, u32[]{:S(2)}, u32[]{:S(2)}) %collective-permute-start.11) | collective-permute-done | bytes 245792 | tf_op jit(solution)/shard_map/ppermute | solution.py:45
  61.9 2.6 %shard_map.64 = bf16[512,256]{1,0:T(8,128)(2,1)S(1)} custom-call(s32[2,2,4]{2,1,0:T(2,128)S(1)} %bitcast.82, bf16[1024,256]{1,0:T(8,128)(2,1)S(1)} %get-tuple-element.54.dpre, bf16[416,256]{1,0:T(8,128)(2,1)S(1)} %shard_map.63.border, bf16[9,3,256,256]{3,2,1,0:T(8,128)(2,1)S(1)} %bitcast.86), custom_call_target="tpu_custom_call" | custom-call | flops 1811939328 | bytes 6000000 | tf_op jit(solution)/shard_map/pallas_call | solution.py:323
  64.6 2.7 %collective-permute-start.16 = (bf16[12,32,256]{2,1,0:T(8,128)(2,1)S(1)}, bf16[12,32,256]{2,1,0:T(8,128)(2,1)S(1)}, u32[]{:S(2)}, u32[]{:S(2)}) collective-permute-start(bf16[12,32,256]{2,1,0:T(8,128)(2,1)S(1)} %add_convert_fusion.6), channel_id=1, source_target_pairs={{0,4},{1,5},{2,6},{3,7},{4,0},{5,1},{6,2},{7,3},{8,56},{9,57},{10,... | collective-permute-start | bytes 589832 | tf_op jit(solution)/shard_map/ppermute | solution.py:45
  67.3 1.3 %collective-permute-done.13 = bf16[15,32,256]{2,1,0:T(8,128)(2,1)S(1)} collective-permute-done((bf16[15,32,256]{2,1,0:T(8,128)(2,1)S(1)}, bf16[15,32,256]{2,1,0:T(8,128)(2,1)S(1)}, u32[]{:S(2)}, u32[]{:S(2)}) %collective-permute-start.13) | collective-permute-done | bytes 245792 | tf_op jit(solution)/shard_map/ppermute | solution.py:45
  69.8 2.6 %shard_map.65 = bf16[512,256]{1,0:T(8,128)(2,1)S(1)} custom-call(s32[2,2,4]{2,1,0:T(2,128)S(1)} %bitcast.83, bf16[1024,256]{1,0:T(8,128)(2,1)S(1)} %get-tuple-element.54.dpre, bf16[416,256]{1,0:T(8,128)(2,1)S(1)} %shard_map.63.border, bf16[9,3,256,256]{3,2,1,0:T(8,128)(2,1)S(1)} %bitcast.87), custom_call_target="tpu_custom_call" | custom-call | flops 1811939328 | bytes 6000000 | tf_op jit(solution)/shard_map/pallas_call | solution.py:323
  73.8 1.8 %collective-permute-done.15 = bf16[15,32,256]{2,1,0:T(8,128)(2,1)S(1)} collective-permute-done((bf16[15,32,256]{2,1,0:T(8,128)(2,1)S(1)}, bf16[15,32,256]{2,1,0:T(8,128)(2,1)S(1)}, u32[]{:S(2)}, u32[]{:S(2)}) %collective-permute-start.15) | collective-permute-done | bytes 245792 | tf_op jit(solution)/shard_map/ppermute | solution.py:45
  75.6 2.0 %collective-permute-start.17 = (bf16[15,32,256]{2,1,0:T(8,128)(2,1)S(1)}, bf16[15,32,256]{2,1,0:T(8,128)(2,1)S(1)}, u32[]{:S(2)}, u32[]{:S(2)}) collective-permute-start(bf16[15,32,256]{2,1,0:T(8,128)(2,1)S(1)} %add_convert_fusion), channel_id=1, source_target_pairs={{0,4},{1,5},{2,6},{3,7},{4,0},{5,1},{6,2},{7,3},{8,56},{9,57},{10,... | collective-permute-start | bytes 737288 | tf_op jit(solution)/shard_map/ppermute | solution.py:45
  78.6 3.4 %collective-permute-done.17 = bf16[15,32,256]{2,1,0:T(8,128)(2,1)S(1)} collective-permute-done((bf16[15,32,256]{2,1,0:T(8,128)(2,1)S(1)}, bf16[15,32,256]{2,1,0:T(8,128)(2,1)S(1)}, u32[]{:S(2)}, u32[]{:S(2)}) %collective-permute-start.17) | collective-permute-done | bytes 245792 | tf_op jit(solution)/shard_map/ppermute | solution.py:45
  83.4 2.4 %collective-permute-start.22 = (bf16[2,12,32,256]{3,2,1,0:T(8,128)(2,1)S(1)}, bf16[2,12,32,256]{3,2,1,0:T(8,128)(2,1)S(1)}, u32[]{:S(2)}, u32[]{:S(2)}) collective-permute-start(bf16[2,12,32,256]{3,2,1,0:T(8,128)(2,1)S(1)} %pad_maximum_fusion.2.refs_1_), channel_id=1, source_target_pairs={{0,48},{1,49},{2,50},{3,51},{4,52},{5,53},{6,54},{7,55},{8,11},{9,... | collective-permute-start | bytes 1179656 | tf_op jit(solution)/shard_map/ppermute | solution.py:45
  85.8 1.8 %shard_map.66.refs_4_ = f32[27,256,256]{2,1,0:T(8,128)} custom-call(s32[5]{0:T(128)S(1)} %stack.41.at_ref, bf16[2,15,32,256]{3,2,1,0:T(8,128)(2,1)S(1)} %pad_maximum_fusion.1.refs_0_, bf16[2,12,32,256]{3,2,1,0:T(8,128)(2,1)S(1)} %pad_maximum_fusion.2.refs_1_), custom_call_target="tpu_custom_call" | custom-call | bytes 10000000 | tf_op jit(solution)/shard_map/pallas_call | solution.py:323
  87.7 2.4 %collective-permute-done.19.refs_0_ = bf16[2,15,32,256]{3,2,1,0:T(8,128)(2,1)S(1)} collective-permute-done((bf16[2,15,32,256]{3,2,1,0:T(8,128)(2,1)S(1)}, bf16[2,15,32,256]{3,2,1,0:T(8,128)(2,1)S(1)}, u32[]{:S(2)}, u32[]{:S(2)}) %collective-permute-start.19) | collective-permute-done | bytes 491552 | tf_op jit(solution)/shard_map/ppermute | solution.py:45
  90.0 4.6 %collective-permute-start.24 = (bf16[2,15,32,256]{3,2,1,0:T(8,128)(2,1)S(1)}, bf16[2,15,32,256]{3,2,1,0:T(8,128)(2,1)S(1)}, u32[]{:S(2)}, u32[]{:S(2)}) collective-permute-start(bf16[2,15,32,256]{3,2,1,0:T(8,128)(2,1)S(1)} %pad_maximum_fusion.1.refs_0_), channel_id=1, source_target_pairs={{0,8},{1,9},{2,10},{3,11},{4,12},{5,13},{6,14},{7,15},{8,0},{9,1},... | collective-permute-start | bytes 1474568 | tf_op jit(solution)/shard_map/ppermute | solution.py:45
  95.2 3.4 %collective-permute-start.23 = (bf16[2,12,32,256]{3,2,1,0:T(8,128)(2,1)S(1)}, bf16[2,12,32,256]{3,2,1,0:T(8,128)(2,1)S(1)}, u32[]{:S(2)}, u32[]{:S(2)}) collective-permute-start(bf16[2,12,32,256]{3,2,1,0:T(8,128)(2,1)S(1)} %collective-permute-done.22.refs_1_), channel_id=1, source_target_pairs={{0,8},{1,9},{2,10},{3,11},{4,12},{5,13},{6,14},{7,15},{8,0},{9,1},... | collective-permute-start | bytes 1179656 | tf_op jit(solution)/shard_map/ppermute | solution.py:45
  98.6 2.5 %shard_map.67.refs_2_ = f32[27,256,256]{2,1,0:T(8,128)} custom-call(s32[5]{0:T(128)S(1)} %stack.41.at_ref, bf16[2,15,32,256]{3,2,1,0:T(8,128)(2,1)S(1)} %collective-permute-done.19.refs_0_, bf16[2,12,32,256]{3,2,1,0:T(8,128)(2,1)S(1)} %collective-permute-done.22.refs_1_, ...), custom_call_target="tpu_custom_call", output_to_operand_aliasing={{}: (5, {})} | custom-call | bytes 10000000 | tf_op jit(solution)/shard_map/pallas_call | solution.py:323
  101.1 1.8 %shard_map.68 = f32[27,256,256]{2,1,0:T(8,128)} custom-call(s32[5]{0:T(128)S(1)} %stack.41.at_ref, bf16[2,15,32,256]{3,2,1,0:T(8,128)(2,1)S(1)} %collective-permute-done.21.refs_0_, bf16[2,12,32,256]{3,2,1,0:T(8,128)(2,1)S(1)} %collective-permute-done.23.refs_1_, f32[27,256,256]{2,1,0:T(8,128)} %shard_map.67.refs_2_), custom_call_target="tpu_custom_call", output_to_operand_aliasing={{}: (3, {})} | custom-call | bytes 10000000 | tf_op jit(solution)/shard_map/pallas_call | solution.py:323
  (79 shorter events, 10.6 us)
Async XLA Ops:
  0.6 0.7 copy-start
  3.3 6.2 %collective-permute-start = (bf16[192,256]{1,0:T(8,128)(2,1)S(1)}, bf16[192,256]{1,0:T(8,128)(2,1)S(1)}, u32[]{:S(2)}, u32[]{:S(2)}) collective-permute-start(bf16[192,256]{1,0:T(8,128)(2,1)S(1)} %get-tuple-element.93), channel_id=1, source_target_pairs={{1,2},{3,4},{5,6},{2,1},{4,3},{6,5},{9,10},{11,12},{13,14},{10,9},... | collective-permute-start | bytes 294920 | tf_op jit(solution)/shard_map/ppermute | solution.py:64
  4.0 7.4 %collective-permute-start.1 = (bf16[192,256]{1,0:T(8,128)(2,1)S(1)}, bf16[192,256]{1,0:T(8,128)(2,1)S(1)}, u32[]{:S(2)}, u32[]{:S(2)}) collective-permute-start(bf16[192,256]{1,0:T(8,128)(2,1)S(1)} %get-tuple-element.92), channel_id=1, source_target_pairs={{0,1},{2,3},{4,5},{6,7},{1,0},{3,2},{5,4},{7,6},{8,9},{10,11},{12,... | collective-permute-start | bytes 294920 | tf_op jit(solution)/shard_map/ppermute | solution.py:64
  11.7 11.9 %collective-permute-start.2 = (bf16[464,256]{1,0:T(8,128)(2,1)S(1)}, bf16[464,256]{1,0:T(8,128)(2,1)S(1)}, u32[]{:S(2)}, u32[]{:S(2)}) collective-permute-start(bf16[464,256]{1,0:T(8,128)(2,1)S(1)} %get-tuple-element.89), channel_id=1, source_target_pairs={{8,16},{24,32},{40,48},{56,64},{72,80},{88,96},{104,112},{16,8},{3... | collective-permute-start | bytes 712712 | tf_op jit(solution)/shard_map/ppermute | solution.py:64
  16.5 7.1 %collective-permute-start.3 = (bf16[464,256]{1,0:T(8,128)(2,1)S(1)}, bf16[464,256]{1,0:T(8,128)(2,1)S(1)}, u32[]{:S(2)}, u32[]{:S(2)}) collective-permute-start(bf16[464,256]{1,0:T(8,128)(2,1)S(1)} %get-tuple-element.88), channel_id=1, source_target_pairs={{0,8},{16,24},{32,40},{48,56},{64,72},{80,88},{96,104},{112,120},{... | collective-permute-start | bytes 712712 | tf_op jit(solution)/shard_map/ppermute | solution.py:64
  16.6 2.0 %copy-start.2 = (bf16[27,256,256]{2,1,0:T(8,128)(2,1)S(1)}, bf16[27,256,256]{2,1,0:T(8,128)(2,1)}, u32[]{:S(2)}) copy-start(bf16[27,256,256]{2,1,0:T(8,128)(2,1)} %param.6) | copy-start | bytes 10616836
  27.2 2.9 %collective-permute-start.4 = (bf16[2,2,15,32,256]{4,3,2,1,0:T(8,128)(2,1)S(1)}, bf16[2,2,15,32,256]{4,3,2,1,0:T(8,128)(2,1)S(1)}, u32[]{:S(2)}, u32[]{:S(2)}) collective-permute-start(bf16[2,2,15,32,256]{4,3,2,1,0:T(8,128)(2,1)S(1)} %get-tuple-element.44), channel_id=1, source_target_pairs={{0,8},{1,9},{2,10},{3,11},{4,12},{5,13},{6,14},{7,15},{8,0},{9,1},... | collective-permute-start | bytes 2949128 | tf_op jit(solution)/shard_map/ppermute | solution.py:45
  30.2 2.5 %collective-permute-start.7 = (bf16[2,2,12,32,256]{4,3,2,1,0:T(8,128)(2,1)S(1)}, bf16[2,2,12,32,256]{4,3,2,1,0:T(8,128)(2,1)S(1)}, u32[]{:S(2)}, u32[]{:S(2)}) collective-permute-start(bf16[2,2,12,32,256]{4,3,2,1,0:T(8,128)(2,1)S(1)} %get-tuple-element.47), channel_id=1, source_target_pairs={{0,8},{1,9},{2,10},{3,11},{4,12},{5,13},{6,14},{7,15},{8,0},{9,1},... | collective-permute-start | bytes 2359304 | tf_op jit(solution)/shard_map/ppermute | solution.py:45
  30.9 8.3 %collective-permute-start.5 = (bf16[2,15,32,256]{3,2,1,0:T(8,128)(2,1)S(1)}, bf16[2,15,32,256]{3,2,1,0:T(8,128)(2,1)S(1)}, u32[]{:S(2)}, u32[]{:S(2)}) collective-permute-start(bf16[2,15,32,256]{3,2,1,0:T(8,128)(2,1)S(1)} %fusion.2), channel_id=1, source_target_pairs={{0,16},{1,17},{2,18},{3,19},{4,20},{5,21},{6,22},{7,23},{8,9},{9,8... | collective-permute-start | bytes 1474568 | tf_op jit(solution)/shard_map/ppermute | solution.py:45
  33.0 10.6 %collective-permute-start.8 = (bf16[2,12,32,256]{3,2,1,0:T(8,128)(2,1)S(1)}, bf16[2,12,32,256]{3,2,1,0:T(8,128)(2,1)S(1)}, u32[]{:S(2)}, u32[]{:S(2)}) collective-permute-start(bf16[2,12,32,256]{3,2,1,0:T(8,128)(2,1)S(1)} %fusion.5), channel_id=1, source_target_pairs={{0,48},{1,49},{2,50},{3,51},{4,52},{5,53},{6,54},{7,55},{8,11},{9,... | collective-permute-start | bytes 1179656 | tf_op jit(solution)/shard_map/ppermute | solution.py:45
  39.4 18.2 %copy-start.3 = (bf16[27,256,256]{2,1,0:T(8,128)(2,1)S(1)}, bf16[27,256,256]{2,1,0:T(8,128)(2,1)}, u32[]{:S(2)}) copy-start(bf16[27,256,256]{2,1,0:T(8,128)(2,1)} %param.6) | copy-start | bytes 10616836
  39.4 7.8 %collective-permute-start.6 = (bf16[15,32,256]{2,1,0:T(8,128)(2,1)S(1)}, bf16[15,32,256]{2,1,0:T(8,128)(2,1)S(1)}, u32[]{:S(2)}, u32[]{:S(2)}) collective-permute-start(bf16[15,32,256]{2,1,0:T(8,128)(2,1)S(1)} %fusion.7), channel_id=1, source_target_pairs={{0,4},{1,5},{2,6},{3,7},{4,0},{5,1},{6,2},{7,3},{8,56},{9,57},{10,... | collective-permute-start | bytes 737288 | tf_op jit(solution)/shard_map/ppermute | solution.py:45
  43.7 7.5 %collective-permute-start.10 = (bf16[12,32,256]{2,1,0:T(8,128)(2,1)S(1)}, bf16[12,32,256]{2,1,0:T(8,128)(2,1)S(1)}, u32[]{:S(2)}, u32[]{:S(2)}) collective-permute-start(bf16[12,32,256]{2,1,0:T(8,128)(2,1)S(1)} %fusion.8), channel_id=1, source_target_pairs={{0,68},{1,69},{2,70},{3,71},{4,64},{5,65},{6,66},{7,67},{8,24},{9,... | collective-permute-start | bytes 589832 | tf_op jit(solution)/shard_map/ppermute | solution.py:45
  47.3 7.5 %collective-permute-start.9 = (bf16[15,32,256]{2,1,0:T(8,128)(2,1)S(1)}, bf16[15,32,256]{2,1,0:T(8,128)(2,1)S(1)}, u32[]{:S(2)}, u32[]{:S(2)}) collective-permute-start(bf16[15,32,256]{2,1,0:T(8,128)(2,1)S(1)} %fusion.4), channel_id=1, source_target_pairs={{0,1},{1,0},{2,3},{3,2},{4,5},{5,4},{6,7},{7,6},{8,76},{9,77},{10,... | collective-permute-start | bytes 737288 | tf_op jit(solution)/shard_map/ppermute | solution.py:45
  51.3 8.1 %collective-permute-start.12 = (bf16[12,32,256]{2,1,0:T(8,128)(2,1)S(1)}, bf16[12,32,256]{2,1,0:T(8,128)(2,1)S(1)}, u32[]{:S(2)}, u32[]{:S(2)}) collective-permute-start(bf16[12,32,256]{2,1,0:T(8,128)(2,1)S(1)} %fusion.6), channel_id=1, source_target_pairs={{0,3},{1,2},{2,1},{3,0},{4,7},{5,6},{6,5},{7,4},{8,12},{9,13},{10,... | collective-permute-start | bytes 589832 | tf_op jit(solution)/shard_map/ppermute | solution.py:45
  54.9 7.0 %copy-start.1 = (s32[2,4,2]{1,2,0:T(2,128)S(1)}, s32[2,4,2]{1,2,0:T(2,128)}, u32[]{:S(2)}) copy-start(s32[2,4,2]{1,2,0:T(2,128)} %param.7) | copy-start | bytes 196
  54.9 6.8 %collective-permute-start.11 = (bf16[15,32,256]{2,1,0:T(8,128)(2,1)S(1)}, bf16[15,32,256]{2,1,0:T(8,128)(2,1)S(1)}, u32[]{:S(2)}, u32[]{:S(2)}) collective-permute-start(bf16[15,32,256]{2,1,0:T(8,128)(2,1)S(1)} %add_convert_fusion.3), channel_id=1, source_target_pairs={{0,48},{1,49},{2,50},{3,51},{4,52},{5,53},{6,54},{7,55},{8,11},{9,... | collective-permute-start | bytes 737288 | tf_op jit(solution)/shard_map/ppermute | solution.py:45
  59.5 5.0 %collective-permute-start.14 = (bf16[12,32,256]{2,1,0:T(8,128)(2,1)S(1)}, bf16[12,32,256]{2,1,0:T(8,128)(2,1)S(1)}, u32[]{:S(2)}, u32[]{:S(2)}) collective-permute-start(bf16[12,32,256]{2,1,0:T(8,128)(2,1)S(1)} %add_convert_fusion.7), channel_id=1, source_target_pairs={{0,16},{1,17},{2,18},{3,19},{4,20},{5,21},{6,22},{7,23},{8,9},{9,8... | collective-permute-start | bytes 589832 | tf_op jit(solution)/shard_map/ppermute | solution.py:45
  61.8 6.9 %collective-permute-start.13 = (bf16[15,32,256]{2,1,0:T(8,128)(2,1)S(1)}, bf16[15,32,256]{2,1,0:T(8,128)(2,1)S(1)}, u32[]{:S(2)}, u32[]{:S(2)}) collective-permute-start(bf16[15,32,256]{2,1,0:T(8,128)(2,1)S(1)} %add_convert_fusion.2), channel_id=1, source_target_pairs={{0,68},{1,69},{2,70},{3,71},{4,64},{5,65},{6,66},{7,67},{8,24},{9,... | collective-permute-start | bytes 737288 | tf_op jit(solution)/shard_map/ppermute | solution.py:45
  64.6 7.9 %collective-permute-start.16 = (bf16[12,32,256]{2,1,0:T(8,128)(2,1)S(1)}, bf16[12,32,256]{2,1,0:T(8,128)(2,1)S(1)}, u32[]{:S(2)}, u32[]{:S(2)}) collective-permute-start(bf16[12,32,256]{2,1,0:T(8,128)(2,1)S(1)} %add_convert_fusion.6), channel_id=1, source_target_pairs={{0,4},{1,5},{2,6},{3,7},{4,0},{5,1},{6,2},{7,3},{8,56},{9,57},{10,... | collective-permute-start | bytes 589832 | tf_op jit(solution)/shard_map/ppermute | solution.py:45
  68.7 6.8 %collective-permute-start.15 = (bf16[15,32,256]{2,1,0:T(8,128)(2,1)S(1)}, bf16[15,32,256]{2,1,0:T(8,128)(2,1)S(1)}, u32[]{:S(2)}, u32[]{:S(2)}) collective-permute-start(bf16[15,32,256]{2,1,0:T(8,128)(2,1)S(1)} %add_convert_fusion.1), channel_id=1, source_target_pairs={{0,3},{1,2},{2,1},{3,0},{4,7},{5,6},{6,5},{7,4},{8,12},{9,13},{10,... | collective-permute-start | bytes 737288 | tf_op jit(solution)/shard_map/ppermute | solution.py:45
  72.5 5.9 %collective-permute-start.18 = (bf16[12,32,256]{2,1,0:T(8,128)(2,1)S(1)}, bf16[12,32,256]{2,1,0:T(8,128)(2,1)S(1)}, u32[]{:S(2)}, u32[]{:S(2)}) collective-permute-start(bf16[12,32,256]{2,1,0:T(8,128)(2,1)S(1)} %add_convert_fusion.5), channel_id=1, source_target_pairs={{0,1},{1,0},{2,3},{3,2},{4,5},{5,4},{6,7},{7,6},{8,76},{9,77},{10,... | collective-permute-start | bytes 589832 | tf_op jit(solution)/shard_map/ppermute | solution.py:45
  75.6 6.3 %collective-permute-start.17 = (bf16[15,32,256]{2,1,0:T(8,128)(2,1)S(1)}, bf16[15,32,256]{2,1,0:T(8,128)(2,1)S(1)}, u32[]{:S(2)}, u32[]{:S(2)}) collective-permute-start(bf16[15,32,256]{2,1,0:T(8,128)(2,1)S(1)} %add_convert_fusion), channel_id=1, source_target_pairs={{0,4},{1,5},{2,6},{3,7},{4,0},{5,1},{6,2},{7,3},{8,56},{9,57},{10,... | collective-permute-start | bytes 737288 | tf_op jit(solution)/shard_map/ppermute | solution.py:45
  78.5 4.9 %collective-permute-start.20 = (bf16[12,32,256]{2,1,0:T(8,128)(2,1)S(1)}, bf16[12,32,256]{2,1,0:T(8,128)(2,1)S(1)}, u32[]{:S(2)}, u32[]{:S(2)}) collective-permute-start(bf16[12,32,256]{2,1,0:T(8,128)(2,1)S(1)} %add_convert_fusion.4), channel_id=1, source_target_pairs={{0,68},{1,69},{2,70},{3,71},{4,64},{5,65},{6,66},{7,67},{8,24},{9,... | collective-permute-start | bytes 589832 | tf_op jit(solution)/shard_map/ppermute | solution.py:45
  82.0 8.1 %collective-permute-start.19 = (bf16[2,15,32,256]{3,2,1,0:T(8,128)(2,1)S(1)}, bf16[2,15,32,256]{3,2,1,0:T(8,128)(2,1)S(1)}, u32[]{:S(2)}, u32[]{:S(2)}) collective-permute-start(bf16[2,15,32,256]{3,2,1,0:T(8,128)(2,1)S(1)} %pad_maximum_fusion.1.refs_0_), channel_id=1, source_target_pairs={{0,16},{1,17},{2,18},{3,19},{4,20},{5,21},{6,22},{7,23},{8,9},{9,8... | collective-permute-start | bytes 1474568 | tf_op jit(solution)/shard_map/ppermute | solution.py:45
  83.4 11.7 %collective-permute-start.22 = (bf16[2,12,32,256]{3,2,1,0:T(8,128)(2,1)S(1)}, bf16[2,12,32,256]{3,2,1,0:T(8,128)(2,1)S(1)}, u32[]{:S(2)}, u32[]{:S(2)}) collective-permute-start(bf16[2,12,32,256]{3,2,1,0:T(8,128)(2,1)S(1)} %pad_maximum_fusion.2.refs_1_), channel_id=1, source_target_pairs={{0,48},{1,49},{2,50},{3,51},{4,52},{5,53},{6,54},{7,55},{8,11},{9,... | collective-permute-start | bytes 1179656 | tf_op jit(solution)/shard_map/ppermute | solution.py:45
  90.0 8.6 %collective-permute-start.24 = (bf16[2,15,32,256]{3,2,1,0:T(8,128)(2,1)S(1)}, bf16[2,15,32,256]{3,2,1,0:T(8,128)(2,1)S(1)}, u32[]{:S(2)}, u32[]{:S(2)}) collective-permute-start(bf16[2,15,32,256]{3,2,1,0:T(8,128)(2,1)S(1)} %pad_maximum_fusion.1.refs_0_), channel_id=1, source_target_pairs={{0,8},{1,9},{2,10},{3,11},{4,12},{5,13},{6,14},{7,15},{8,0},{9,1},... | collective-permute-start | bytes 1474568 | tf_op jit(solution)/shard_map/ppermute | solution.py:45
  94.6 6.5 %collective-permute-start.21 = (bf16[2,15,32,256]{3,2,1,0:T(8,128)(2,1)S(1)}, bf16[2,15,32,256]{3,2,1,0:T(8,128)(2,1)S(1)}, u32[]{:S(2)}, u32[]{:S(2)}) collective-permute-start(bf16[2,15,32,256]{3,2,1,0:T(8,128)(2,1)S(1)} %collective-permute-done.19.refs_0_), channel_id=1, source_target_pairs={{0,8},{1,9},{2,10},{3,11},{4,12},{5,13},{6,14},{7,15},{8,0},{9,1},... | collective-permute-start | bytes 1474568 | tf_op jit(solution)/shard_map/ppermute | solution.py:45
  94.7 3.9 %collective-permute-start.25 = (bf16[2,12,32,256]{3,2,1,0:T(8,128)(2,1)S(1)}, bf16[2,12,32,256]{3,2,1,0:T(8,128)(2,1)S(1)}, u32[]{:S(2)}, u32[]{:S(2)}) collective-permute-start(bf16[2,12,32,256]{3,2,1,0:T(8,128)(2,1)S(1)} %pad_maximum_fusion.2.refs_1_), channel_id=1, source_target_pairs={{0,8},{1,9},{2,10},{3,11},{4,12},{5,13},{6,14},{7,15},{8,0},{9,1},... | collective-permute-start | bytes 1179656 | tf_op jit(solution)/shard_map/ppermute | solution.py:45
  95.2 6.0 %collective-permute-start.23 = (bf16[2,12,32,256]{3,2,1,0:T(8,128)(2,1)S(1)}, bf16[2,12,32,256]{3,2,1,0:T(8,128)(2,1)S(1)}, u32[]{:S(2)}, u32[]{:S(2)}) collective-permute-start(bf16[2,12,32,256]{3,2,1,0:T(8,128)(2,1)S(1)} %collective-permute-done.22.refs_1_), channel_id=1, source_target_pairs={{0,8},{1,9},{2,10},{3,11},{4,12},{5,13},{6,14},{7,15},{8,0},{9,1},... | collective-permute-start | bytes 1179656 | tf_op jit(solution)/shard_map/ppermute | solution.py:45

commit v5 on v4

--- a/solution.py
+++ b/solution.py
@@ -10,7 +10,7 @@
 AXES = ("gx", "gy")
 F32, BF16 = jnp.float32, jnp.bfloat16
 COUNT = 128
-FIRSTS = ((0, 2), (3, 5))
+FIRSTS = ((0, 4), (3, 1))
 ORDERS = tuple(
     tuple(tuple((first + step) % 6 for step in range(6)) for first in firsts) for firsts in FIRSTS
 )

time: 103 us -> 106 us (1.029)
  waiting for transfers between devices: 22.6 us -> 25.7 us
    ppermute x22, waiting for transfers between devices: 20.7 us -> 23.8 us  [send(): return lax.ppermute(array, AXES, pairs)]
  transfers between devices with their start and end apart: 26 -> 26, of which waited for: 10 -> 11; matrix products, arithmetic and copies ran while one was open for 3% -> 3% of each run, Pallas kernels for 18% -> 18%
where the time goes in v5:
time: 106 us
  starting transfers between devices  47.6 us (45%)
  waiting for transfers between devices  25.7 us (24%)
  Pallas kernels  24.6 us (23%)
  other arithmetic  3.98 us (4%)
  local copies, waits for them, and re-layouts  3.02 us (3%)
  between operations  1.32 us (1%)
    ppermute x22, starting transfers between devices, send(): return lax.ppermute(array, AXES, pairs)  36.6 us
    pallas_call x10, Pallas kernels, kernel(): pl.pallas_call(body, out_shape=outs, in_specs=specs, out_specs=out_specs...  24.6 us
    ppermute x22, waiting for transfers between devices, send(): return lax.ppermute(array, AXES, pairs)  23.8 us
    ppermute x4, starting transfers between devices, pair_swap(): return lax.ppermute(array, axis, pairs + [(b, a) for a, b in pairs])  11 us
    unnamed x20, local copies, waits for them, and re-layouts  2.75 us
  transfers between devices with their start and end apart: 26, of which 11 were waited for; matrix products, arithmetic and copies ran while one was open for 3% of the time, Pallas kernels for 18%

profile of v5, /device:TPU:1, one launch (start us, length us, event | category | flops | bytes accessed | tf_op | source)
XLA Modules:
  0.0 106.2 jit_solution(11758813213476467510)
XLA Ops:
  1.9 1.3 %fusion.15 = (bf16[8,16,8,256]{3,2,1,0:T(8,128)(2,1)S(1)}, bf16[8,16,8,256]{3,2,1,0:T(8,128)(2,1)S(1)}) fusion(bf16[8,16,8,256]{3,2,1,0:T(8,128)(2,1)} %param.4, bf16[8,16,8,256]{3,2,1,0:T(8,128)(2,1)S(1)} %bitcast.78, bf16[8,16,8,256]{3,2,1,0:T(8,128)(2,1)} %param.5), kind=kLoop, calls=%fused_computation.78 | loop fusion | flops 524288 | bytes 2621440 | tf_op jit(solution)/shard_map/mul | solution.py:359
  4.0 5.4 %collective-permute-start.1 = (bf16[192,256]{1,0:T(8,128)(2,1)S(1)}, bf16[192,256]{1,0:T(8,128)(2,1)S(1)}, u32[]{:S(2)}, u32[]{:S(2)}) collective-permute-start(bf16[192,256]{1,0:T(8,128)(2,1)S(1)} %get-tuple-element.92), channel_id=1, source_target_pairs={{0,1},{2,3},{4,5},{6,7},{1,0},{3,2},{5,4},{7,6},{8,9},{10,11},{12,... | collective-permute-start | bytes 294920 | tf_op jit(solution)/shard_map/ppermute | solution.py:64
  9.5 1.9 %collective-permute-done.1 = bf16[192,256]{1,0:T(8,128)(2,1)S(1)} collective-permute-done((bf16[192,256]{1,0:T(8,128)(2,1)S(1)}, bf16[192,256]{1,0:T(8,128)(2,1)S(1)}, u32[]{:S(2)}, u32[]{:S(2)}) %collective-permute-start.1) | collective-permute-done | bytes 98336 | tf_op jit(solution)/shard_map/ppermute | solution.py:64
  11.7 4.8 %collective-permute-start.2 = (bf16[464,256]{1,0:T(8,128)(2,1)S(1)}, bf16[464,256]{1,0:T(8,128)(2,1)S(1)}, u32[]{:S(2)}, u32[]{:S(2)}) collective-permute-start(bf16[464,256]{1,0:T(8,128)(2,1)S(1)} %get-tuple-element.89), channel_id=1, source_target_pairs={{8,16},{24,32},{40,48},{56,64},{72,80},{88,96},{104,112},{16,8},{3... | collective-permute-start | bytes 712712 | tf_op jit(solution)/shard_map/ppermute | solution.py:64
  16.6 2.0 %copy-done.2 = bf16[27,256,256]{2,1,0:T(8,128)(2,1)S(1)} copy-done((bf16[27,256,256]{2,1,0:T(8,128)(2,1)S(1)}, bf16[27,256,256]{2,1,0:T(8,128)(2,1)}, u32[]{:S(2)}) %copy-start.2) | copy-done | bytes 3538968
  18.6 5.0 %shard_map.60 = (f32[1024,256]{1,0:T(8,128)S(1)}, bf16[3,256,1024]{2,1,0:T(8,128)(2,1)S(1)}, bf16[9,3,256,256]{3,2,1,0:T(8,128)(2,1)S(1)}) custom-call(bf16[1024,256]{1,0:T(8,128)(2,1)S(1)} %bitcast.79, bf16[192,256]{1,0:T(8,128)(2,1)S(1)} %get-tuple-element.91.before, bf16[192,256]{1,0:T(8,128)(2,1)S(1)} %get-tuple-element.90.after, ...), custom_call_target="tpu_custom_call" | custom-call | flops 3623878656 | bytes 6000000 | tf_op jit(solution)/shard_map/pallas_call | solution.py:323
  23.7 3.5 %shard_map.61 = (bf16[1024,256]{1,0:T(8,128)(2,1)S(1)}, bf16[1024,768]{1,0:T(8,128)(2,1)S(1)}, bf16[2,3,256,128]{3,2,1,0:T(8,128)(2,1)S(1)}, bf16[2,2,15,32,256]...) custom-call(s32[5]{0:T(128)S(1)} %stack.41.at_ref, bf16[464,256]{1,0:T(8,128)(2,1)S(1)} %get-tuple-element.87.first, ...), custom_call_target="tpu_custom_call" | custom-call | flops 1811939328 | bytes 6000000 | tf_op jit(solution)/shard_map/pallas_call | solution.py:323
  27.8 2.4 %shard_map.62 = (bf16[2,2,12,32,256]{4,3,2,1,0:T(8,128)(2,1)S(1)}, f32[2,2,12,32,256]{4,3,2,1,0:T(8,128)S(1)}) custom-call(s32[5]{0:T(128)S(1)} %stack.41.at_ref, bf16[3,256,1024]{2,1,0:T(8,128)(2,1)S(1)} %get-tuple-element.39.turned, bf16[2,3,256,128]{3,2,1,0:T(8,128)(2,1)S(1)} %get-tuple-element.41.ends, bf16[1024,768]{1,0:T(8,128)(2,1)S(1)} %get-tuple-element.42.shifted), custom_call_target="tpu_custom_call" | custom-call | flops 1207959552 | bytes 6000000 | tf_op jit(solution)/shard_map/pallas_call | solution.py:323
  30.9 5.6 %collective-permute-start.5 = (bf16[2,15,32,256]{3,2,1,0:T(8,128)(2,1)S(1)}, bf16[2,15,32,256]{3,2,1,0:T(8,128)(2,1)S(1)}, u32[]{:S(2)}, u32[]{:S(2)}) collective-permute-start(bf16[2,15,32,256]{3,2,1,0:T(8,128)(2,1)S(1)} %fusion.2), channel_id=1, source_target_pairs={{0,16},{1,17},{2,18},{3,19},{4,20},{5,21},{6,22},{7,23},{8,76},{9,... | collective-permute-start | bytes 1474568 | tf_op jit(solution)/shard_map/ppermute | solution.py:45
  36.9 5.9 %collective-permute-done.5 = bf16[2,15,32,256]{3,2,1,0:T(8,128)(2,1)S(1)} collective-permute-done((bf16[2,15,32,256]{3,2,1,0:T(8,128)(2,1)S(1)}, bf16[2,15,32,256]{3,2,1,0:T(8,128)(2,1)S(1)}, u32[]{:S(2)}, u32[]{:S(2)}) %collective-permute-start.5) | collective-permute-done | bytes 491552 | tf_op jit(solution)/shard_map/ppermute | solution.py:45
  43.0 1.4 %collective-permute-start.6 = (bf16[15,32,256]{2,1,0:T(8,128)(2,1)S(1)}, bf16[15,32,256]{2,1,0:T(8,128)(2,1)S(1)}, u32[]{:S(2)}, u32[]{:S(2)}) collective-permute-start(bf16[15,32,256]{2,1,0:T(8,128)(2,1)S(1)} %fusion.7), channel_id=1, source_target_pairs={{0,4},{1,5},{2,6},{3,7},{4,0},{5,1},{6,2},{7,3},{8,11},{9,10},{10,... | collective-permute-start | bytes 737288 | tf_op jit(solution)/shard_map/ppermute | solution.py:45
  44.6 5.0 %collective-permute-done.6 = bf16[15,32,256]{2,1,0:T(8,128)(2,1)S(1)} collective-permute-done((bf16[15,32,256]{2,1,0:T(8,128)(2,1)S(1)}, bf16[15,32,256]{2,1,0:T(8,128)(2,1)S(1)}, u32[]{:S(2)}, u32[]{:S(2)}) %collective-permute-start.6) | collective-permute-done | bytes 245792 | tf_op jit(solution)/shard_map/ppermute | solution.py:45
  50.6 3.1 %collective-permute-start.12 = (bf16[12,32,256]{2,1,0:T(8,128)(2,1)S(1)}, bf16[12,32,256]{2,1,0:T(8,128)(2,1)S(1)}, u32[]{:S(2)}, u32[]{:S(2)}) collective-permute-start(bf16[12,32,256]{2,1,0:T(8,128)(2,1)S(1)} %fusion.6), channel_id=1, source_target_pairs={{0,3},{1,2},{2,1},{3,0},{4,7},{5,6},{6,5},{7,4},{8,56},{9,57},{10,... | collective-permute-start | bytes 589832 | tf_op jit(solution)/shard_map/ppermute | solution.py:45
  53.7 1.2 %collective-permute-done.9 = bf16[15,32,256]{2,1,0:T(8,128)(2,1)S(1)} collective-permute-done((bf16[15,32,256]{2,1,0:T(8,128)(2,1)S(1)}, bf16[15,32,256]{2,1,0:T(8,128)(2,1)S(1)}, u32[]{:S(2)}, u32[]{:S(2)}) %collective-permute-start.9) | collective-permute-done | bytes 245792 | tf_op jit(solution)/shard_map/ppermute | solution.py:45
  55.2 1.7 %shard_map.63.border = bf16[416,256]{1,0:T(8,128)(2,1)S(1)} custom-call(bf16[1024,256]{1,0:T(8,128)(2,1)S(1)} %bitcast.80, bf16[192,256]{1,0:T(8,128)(2,1)S(1)} %get-tuple-element.91.before, bf16[192,256]{1,0:T(8,128)(2,1)S(1)} %get-tuple-element.90.after, bf16[464,256]{1,0:T(8,128)(2,1)S(1)} %get-tuple-element.87.first, ...), custom_call_target="tpu_custom_call" | custom-call | flops 1811939328 | bytes 6000000 | tf_op jit(solution)/shard_map/pallas_call | solution.py:323
  57.1 3.3 %collective-permute-start.14 = (bf16[12,32,256]{2,1,0:T(8,128)(2,1)S(1)}, bf16[12,32,256]{2,1,0:T(8,128)(2,1)S(1)}, u32[]{:S(2)}, u32[]{:S(2)}) collective-permute-start(bf16[12,32,256]{2,1,0:T(8,128)(2,1)S(1)} %add_convert_fusion.7), channel_id=1, source_target_pairs={{0,16},{1,17},{2,18},{3,19},{4,20},{5,21},{6,22},{7,23},{8,76},{9,... | collective-permute-start | bytes 589832 | tf_op jit(solution)/shard_map/ppermute | solution.py:45
  60.7 2.6 %shard_map.64 = bf16[512,256]{1,0:T(8,128)(2,1)S(1)} custom-call(s32[2,2,4]{2,1,0:T(2,128)S(1)} %bitcast.82, bf16[1024,256]{1,0:T(8,128)(2,1)S(1)} %get-tuple-element.54.dpre, bf16[416,256]{1,0:T(8,128)(2,1)S(1)} %shard_map.63.border, bf16[9,3,256,256]{3,2,1,0:T(8,128)(2,1)S(1)} %bitcast.86), custom_call_target="tpu_custom_call" | custom-call | flops 1811939328 | bytes 6000000 | tf_op jit(solution)/shard_map/pallas_call | solution.py:323
  63.5 1.3 %collective-permute-start.16 = (bf16[12,32,256]{2,1,0:T(8,128)(2,1)S(1)}, bf16[12,32,256]{2,1,0:T(8,128)(2,1)S(1)}, u32[]{:S(2)}, u32[]{:S(2)}) collective-permute-start(bf16[12,32,256]{2,1,0:T(8,128)(2,1)S(1)} %add_convert_fusion.6), channel_id=1, source_target_pairs={{0,4},{1,5},{2,6},{3,7},{4,0},{5,1},{6,2},{7,3},{8,11},{9,10},{10,... | collective-permute-start | bytes 589832 | tf_op jit(solution)/shard_map/ppermute | solution.py:45
  64.7 1.3 %collective-permute-done.13 = bf16[15,32,256]{2,1,0:T(8,128)(2,1)S(1)} collective-permute-done((bf16[15,32,256]{2,1,0:T(8,128)(2,1)S(1)}, bf16[15,32,256]{2,1,0:T(8,128)(2,1)S(1)}, u32[]{:S(2)}, u32[]{:S(2)}) %collective-permute-start.13) | collective-permute-done | bytes 245792 | tf_op jit(solution)/shard_map/ppermute | solution.py:45
  66.1 3.3 %collective-permute-start.15 = (bf16[15,32,256]{2,1,0:T(8,128)(2,1)S(1)}, bf16[15,32,256]{2,1,0:T(8,128)(2,1)S(1)}, u32[]{:S(2)}, u32[]{:S(2)}) collective-permute-start(bf16[15,32,256]{2,1,0:T(8,128)(2,1)S(1)} %add_convert_fusion.1), channel_id=1, source_target_pairs={{0,3},{1,2},{2,1},{3,0},{4,7},{5,6},{6,5},{7,4},{8,56},{9,57},{10,... | collective-permute-start | bytes 737288 | tf_op jit(solution)/shard_map/ppermute | solution.py:45
  69.3 2.6 %shard_map.65 = bf16[512,256]{1,0:T(8,128)(2,1)S(1)} custom-call(s32[2,2,4]{2,1,0:T(2,128)S(1)} %bitcast.83, bf16[1024,256]{1,0:T(8,128)(2,1)S(1)} %get-tuple-element.54.dpre, bf16[416,256]{1,0:T(8,128)(2,1)S(1)} %shard_map.63.border, bf16[9,3,256,256]{3,2,1,0:T(8,128)(2,1)S(1)} %bitcast.87), custom_call_target="tpu_custom_call" | custom-call | flops 1811939328 | bytes 6000000 | tf_op jit(solution)/shard_map/pallas_call | solution.py:323
  73.0 2.3 %collective-permute-start.17 = (bf16[15,32,256]{2,1,0:T(8,128)(2,1)S(1)}, bf16[15,32,256]{2,1,0:T(8,128)(2,1)S(1)}, u32[]{:S(2)}, u32[]{:S(2)}) collective-permute-start(bf16[15,32,256]{2,1,0:T(8,128)(2,1)S(1)} %add_convert_fusion), channel_id=1, source_target_pairs={{0,4},{1,5},{2,6},{3,7},{4,0},{5,1},{6,2},{7,3},{8,11},{9,10},{10,... | collective-permute-start | bytes 737288 | tf_op jit(solution)/shard_map/ppermute | solution.py:45
  75.4 0.8 pad_maximum_fusion
  77.0 0.9 collective-permute-start.20
  77.8 2.6 %collective-permute-done.17 = bf16[15,32,256]{2,1,0:T(8,128)(2,1)S(1)} collective-permute-done((bf16[15,32,256]{2,1,0:T(8,128)(2,1)S(1)}, bf16[15,32,256]{2,1,0:T(8,128)(2,1)S(1)}, u32[]{:S(2)}, u32[]{:S(2)}) %collective-permute-start.17) | collective-permute-done | bytes 245792 | tf_op jit(solution)/shard_map/ppermute | solution.py:45
  80.5 3.0 %collective-permute-start.19 = (bf16[2,15,32,256]{3,2,1,0:T(8,128)(2,1)S(1)}, bf16[2,15,32,256]{3,2,1,0:T(8,128)(2,1)S(1)}, u32[]{:S(2)}, u32[]{:S(2)}) collective-permute-start(bf16[2,15,32,256]{3,2,1,0:T(8,128)(2,1)S(1)} %pad_maximum_fusion.1.refs_0_), channel_id=1, source_target_pairs={{0,16},{1,17},{2,18},{3,19},{4,20},{5,21},{6,22},{7,23},{8,76},{9,... | collective-permute-start | bytes 1474568 | tf_op jit(solution)/shard_map/ppermute | solution.py:45
  84.1 1.8 %shard_map.66.refs_4_ = f32[27,256,256]{2,1,0:T(8,128)} custom-call(s32[5]{0:T(128)S(1)} %stack.41.at_ref, bf16[2,15,32,256]{3,2,1,0:T(8,128)(2,1)S(1)} %pad_maximum_fusion.1.refs_0_, bf16[2,12,32,256]{3,2,1,0:T(8,128)(2,1)S(1)} %pad_maximum_fusion.2.refs_1_), custom_call_target="tpu_custom_call" | custom-call | bytes 10000000 | tf_op jit(solution)/shard_map/pallas_call | solution.py:323
  85.9 5.5 %collective-permute-done.19.refs_0_ = bf16[2,15,32,256]{3,2,1,0:T(8,128)(2,1)S(1)} collective-permute-done((bf16[2,15,32,256]{3,2,1,0:T(8,128)(2,1)S(1)}, bf16[2,15,32,256]{3,2,1,0:T(8,128)(2,1)S(1)}, u32[]{:S(2)}, u32[]{:S(2)}) %collective-permute-start.19) | collective-permute-done | bytes 491552 | tf_op jit(solution)/shard_map/ppermute | solution.py:45
  91.4 5.7 %collective-permute-start.24 = (bf16[2,15,32,256]{3,2,1,0:T(8,128)(2,1)S(1)}, bf16[2,15,32,256]{3,2,1,0:T(8,128)(2,1)S(1)}, u32[]{:S(2)}, u32[]{:S(2)}) collective-permute-start(bf16[2,15,32,256]{3,2,1,0:T(8,128)(2,1)S(1)} %pad_maximum_fusion.1.refs_0_), channel_id=1, source_target_pairs={{0,8},{1,9},{2,10},{3,11},{4,12},{5,13},{6,14},{7,15},{8,0},{9,1},... | collective-permute-start | bytes 1474568 | tf_op jit(solution)/shard_map/ppermute | solution.py:45
  97.7 4.0 %collective-permute-start.23 = (bf16[2,12,32,256]{3,2,1,0:T(8,128)(2,1)S(1)}, bf16[2,12,32,256]{3,2,1,0:T(8,128)(2,1)S(1)}, u32[]{:S(2)}, u32[]{:S(2)}) collective-permute-start(bf16[2,12,32,256]{3,2,1,0:T(8,128)(2,1)S(1)} %collective-permute-done.22.refs_1_), channel_id=1, source_target_pairs={{0,8},{1,9},{2,10},{3,11},{4,12},{5,13},{6,14},{7,15},{8,0},{9,1},... | collective-permute-start | bytes 1179656 | tf_op jit(solution)/shard_map/ppermute | solution.py:45
  101.7 2.5 %shard_map.67.refs_2_ = f32[27,256,256]{2,1,0:T(8,128)} custom-call(s32[5]{0:T(128)S(1)} %stack.41.at_ref, bf16[2,15,32,256]{3,2,1,0:T(8,128)(2,1)S(1)} %collective-permute-done.19.refs_0_, bf16[2,12,32,256]{3,2,1,0:T(8,128)(2,1)S(1)} %collective-permute-done.22.refs_1_, ...), custom_call_target="tpu_custom_call", output_to_operand_aliasing={{}: (5, {})} | custom-call | bytes 10000000 | tf_op jit(solution)/shard_map/pallas_call | solution.py:323
  104.2 1.8 %shard_map.68 = f32[27,256,256]{2,1,0:T(8,128)} custom-call(s32[5]{0:T(128)S(1)} %stack.41.at_ref, bf16[2,15,32,256]{3,2,1,0:T(8,128)(2,1)S(1)} %collective-permute-done.21.refs_0_, bf16[2,12,32,256]{3,2,1,0:T(8,128)(2,1)S(1)} %collective-permute-done.23.refs_1_, f32[27,256,256]{2,1,0:T(8,128)} %shard_map.67.refs_2_), custom_call_target="tpu_custom_call", output_to_operand_aliasing={{}: (3, {})} | custom-call | bytes 10000000 | tf_op jit(solution)/shard_map/pallas_call | solution.py:323
  (79 shorter events, 9.2 us)
Async XLA Ops:
  0.6 0.7 copy-start
  3.3 6.2 %collective-permute-start = (bf16[192,256]{1,0:T(8,128)(2,1)S(1)}, bf16[192,256]{1,0:T(8,128)(2,1)S(1)}, u32[]{:S(2)}, u32[]{:S(2)}) collective-permute-start(bf16[192,256]{1,0:T(8,128)(2,1)S(1)} %get-tuple-element.93), channel_id=1, source_target_pairs={{1,2},{3,4},{5,6},{2,1},{4,3},{6,5},{9,10},{11,12},{13,14},{10,9},... | collective-permute-start | bytes 294920 | tf_op jit(solution)/shard_map/ppermute | solution.py:64
  4.0 7.4 %collective-permute-start.1 = (bf16[192,256]{1,0:T(8,128)(2,1)S(1)}, bf16[192,256]{1,0:T(8,128)(2,1)S(1)}, u32[]{:S(2)}, u32[]{:S(2)}) collective-permute-start(bf16[192,256]{1,0:T(8,128)(2,1)S(1)} %get-tuple-element.92), channel_id=1, source_target_pairs={{0,1},{2,3},{4,5},{6,7},{1,0},{3,2},{5,4},{7,6},{8,9},{10,11},{12,... | collective-permute-start | bytes 294920 | tf_op jit(solution)/shard_map/ppermute | solution.py:64
  11.7 11.9 %collective-permute-start.2 = (bf16[464,256]{1,0:T(8,128)(2,1)S(1)}, bf16[464,256]{1,0:T(8,128)(2,1)S(1)}, u32[]{:S(2)}, u32[]{:S(2)}) collective-permute-start(bf16[464,256]{1,0:T(8,128)(2,1)S(1)} %get-tuple-element.89), channel_id=1, source_target_pairs={{8,16},{24,32},{40,48},{56,64},{72,80},{88,96},{104,112},{16,8},{3... | collective-permute-start | bytes 712712 | tf_op jit(solution)/shard_map/ppermute | solution.py:64
  16.5 7.1 %collective-permute-start.3 = (bf16[464,256]{1,0:T(8,128)(2,1)S(1)}, bf16[464,256]{1,0:T(8,128)(2,1)S(1)}, u32[]{:S(2)}, u32[]{:S(2)}) collective-permute-start(bf16[464,256]{1,0:T(8,128)(2,1)S(1)} %get-tuple-element.88), channel_id=1, source_target_pairs={{0,8},{16,24},{32,40},{48,56},{64,72},{80,88},{96,104},{112,120},{... | collective-permute-start | bytes 712712 | tf_op jit(solution)/shard_map/ppermute | solution.py:64
  16.6 2.0 %copy-start.2 = (bf16[27,256,256]{2,1,0:T(8,128)(2,1)S(1)}, bf16[27,256,256]{2,1,0:T(8,128)(2,1)}, u32[]{:S(2)}) copy-start(bf16[27,256,256]{2,1,0:T(8,128)(2,1)} %param.6) | copy-start | bytes 10616836
  27.2 2.9 %collective-permute-start.4 = (bf16[2,2,15,32,256]{4,3,2,1,0:T(8,128)(2,1)S(1)}, bf16[2,2,15,32,256]{4,3,2,1,0:T(8,128)(2,1)S(1)}, u32[]{:S(2)}, u32[]{:S(2)}) collective-permute-start(bf16[2,2,15,32,256]{4,3,2,1,0:T(8,128)(2,1)S(1)} %get-tuple-element.44), channel_id=1, source_target_pairs={{0,8},{1,9},{2,10},{3,11},{4,12},{5,13},{6,14},{7,15},{8,0},{9,1},... | collective-permute-start | bytes 2949128 | tf_op jit(solution)/shard_map/ppermute | solution.py:45
  30.2 6.4 %collective-permute-start.7 = (bf16[2,2,12,32,256]{4,3,2,1,0:T(8,128)(2,1)S(1)}, bf16[2,2,12,32,256]{4,3,2,1,0:T(8,128)(2,1)S(1)}, u32[]{:S(2)}, u32[]{:S(2)}) collective-permute-start(bf16[2,2,12,32,256]{4,3,2,1,0:T(8,128)(2,1)S(1)} %get-tuple-element.47), channel_id=1, source_target_pairs={{0,8},{1,9},{2,10},{3,11},{4,12},{5,13},{6,14},{7,15},{8,0},{9,1},... | collective-permute-start | bytes 2359304 | tf_op jit(solution)/shard_map/ppermute | solution.py:45
  30.9 11.9 %collective-permute-start.5 = (bf16[2,15,32,256]{3,2,1,0:T(8,128)(2,1)S(1)}, bf16[2,15,32,256]{3,2,1,0:T(8,128)(2,1)S(1)}, u32[]{:S(2)}, u32[]{:S(2)}) collective-permute-start(bf16[2,15,32,256]{3,2,1,0:T(8,128)(2,1)S(1)} %fusion.2), channel_id=1, source_target_pairs={{0,16},{1,17},{2,18},{3,19},{4,20},{5,21},{6,22},{7,23},{8,76},{9,... | collective-permute-start | bytes 1474568 | tf_op jit(solution)/shard_map/ppermute | solution.py:45
  36.8 7.5 %collective-permute-start.8 = (bf16[2,12,32,256]{3,2,1,0:T(8,128)(2,1)S(1)}, bf16[2,12,32,256]{3,2,1,0:T(8,128)(2,1)S(1)}, u32[]{:S(2)}, u32[]{:S(2)}) collective-permute-start(bf16[2,12,32,256]{3,2,1,0:T(8,128)(2,1)S(1)} %fusion.5), channel_id=1, source_target_pairs={{0,48},{1,49},{2,50},{3,51},{4,52},{5,53},{6,54},{7,55},{8,12},{9,... | collective-permute-start | bytes 1179656 | tf_op jit(solution)/shard_map/ppermute | solution.py:45
  43.0 12.2 %copy-start.3 = (bf16[27,256,256]{2,1,0:T(8,128)(2,1)S(1)}, bf16[27,256,256]{2,1,0:T(8,128)(2,1)}, u32[]{:S(2)}) copy-start(bf16[27,256,256]{2,1,0:T(8,128)(2,1)} %param.6) | copy-start | bytes 10616836
  43.0 6.6 %collective-permute-start.6 = (bf16[15,32,256]{2,1,0:T(8,128)(2,1)S(1)}, bf16[15,32,256]{2,1,0:T(8,128)(2,1)S(1)}, u32[]{:S(2)}, u32[]{:S(2)}) collective-permute-start(bf16[15,32,256]{2,1,0:T(8,128)(2,1)S(1)} %fusion.7), channel_id=1, source_target_pairs={{0,4},{1,5},{2,6},{3,7},{4,0},{5,1},{6,2},{7,3},{8,11},{9,10},{10,... | collective-permute-start | bytes 737288 | tf_op jit(solution)/shard_map/ppermute | solution.py:45
  44.5 6.0 %collective-permute-start.10 = (bf16[12,32,256]{2,1,0:T(8,128)(2,1)S(1)}, bf16[12,32,256]{2,1,0:T(8,128)(2,1)S(1)}, u32[]{:S(2)}, u32[]{:S(2)}) collective-permute-start(bf16[12,32,256]{2,1,0:T(8,128)(2,1)S(1)} %fusion.8), channel_id=1, source_target_pairs={{0,68},{1,69},{2,70},{3,71},{4,64},{5,65},{6,66},{7,67},{8,9},{9,8... | collective-permute-start | bytes 589832 | tf_op jit(solution)/shard_map/ppermute | solution.py:45
  49.7 5.1 %collective-permute-start.9 = (bf16[15,32,256]{2,1,0:T(8,128)(2,1)S(1)}, bf16[15,32,256]{2,1,0:T(8,128)(2,1)S(1)}, u32[]{:S(2)}, u32[]{:S(2)}) collective-permute-start(bf16[15,32,256]{2,1,0:T(8,128)(2,1)S(1)} %fusion.4), channel_id=1, source_target_pairs={{0,1},{1,0},{2,3},{3,2},{4,5},{5,4},{6,7},{7,6},{8,24},{9,25},{10,... | collective-permute-start | bytes 737288 | tf_op jit(solution)/shard_map/ppermute | solution.py:45
  50.6 6.4 %collective-permute-start.12 = (bf16[12,32,256]{2,1,0:T(8,128)(2,1)S(1)}, bf16[12,32,256]{2,1,0:T(8,128)(2,1)S(1)}, u32[]{:S(2)}, u32[]{:S(2)}) collective-permute-start(bf16[12,32,256]{2,1,0:T(8,128)(2,1)S(1)} %fusion.6), channel_id=1, source_target_pairs={{0,3},{1,2},{2,1},{3,0},{4,7},{5,6},{6,5},{7,4},{8,56},{9,57},{10,... | collective-permute-start | bytes 589832 | tf_op jit(solution)/shard_map/ppermute | solution.py:45
  54.9 5.8 %copy-start.1 = (s32[2,4,2]{1,2,0:T(2,128)S(1)}, s32[2,4,2]{1,2,0:T(2,128)}, u32[]{:S(2)}) copy-start(s32[2,4,2]{1,2,0:T(2,128)} %param.7) | copy-start | bytes 196
  55.0 5.6 %collective-permute-start.11 = (bf16[15,32,256]{2,1,0:T(8,128)(2,1)S(1)}, bf16[15,32,256]{2,1,0:T(8,128)(2,1)S(1)}, u32[]{:S(2)}, u32[]{:S(2)}) collective-permute-start(bf16[15,32,256]{2,1,0:T(8,128)(2,1)S(1)} %add_convert_fusion.3), channel_id=1, source_target_pairs={{0,48},{1,49},{2,50},{3,51},{4,52},{5,53},{6,54},{7,55},{8,12},{9,... | collective-permute-start | bytes 737288 | tf_op jit(solution)/shard_map/ppermute | solution.py:45
  57.1 6.3 %collective-permute-start.14 = (bf16[12,32,256]{2,1,0:T(8,128)(2,1)S(1)}, bf16[12,32,256]{2,1,0:T(8,128)(2,1)S(1)}, u32[]{:S(2)}, u32[]{:S(2)}) collective-permute-start(bf16[12,32,256]{2,1,0:T(8,128)(2,1)S(1)} %add_convert_fusion.7), channel_id=1, source_target_pairs={{0,16},{1,17},{2,18},{3,19},{4,20},{5,21},{6,22},{7,23},{8,76},{9,... | collective-permute-start | bytes 589832 | tf_op jit(solution)/shard_map/ppermute | solution.py:45
  60.6 5.4 %collective-permute-start.13 = (bf16[15,32,256]{2,1,0:T(8,128)(2,1)S(1)}, bf16[15,32,256]{2,1,0:T(8,128)(2,1)S(1)}, u32[]{:S(2)}, u32[]{:S(2)}) collective-permute-start(bf16[15,32,256]{2,1,0:T(8,128)(2,1)S(1)} %add_convert_fusion.2), channel_id=1, source_target_pairs={{0,68},{1,69},{2,70},{3,71},{4,64},{5,65},{6,66},{7,67},{8,9},{9,8... | collective-permute-start | bytes 737288 | tf_op jit(solution)/shard_map/ppermute | solution.py:45
  63.5 8.5 %collective-permute-start.16 = (bf16[12,32,256]{2,1,0:T(8,128)(2,1)S(1)}, bf16[12,32,256]{2,1,0:T(8,128)(2,1)S(1)}, u32[]{:S(2)}, u32[]{:S(2)}) collective-permute-start(bf16[12,32,256]{2,1,0:T(8,128)(2,1)S(1)} %add_convert_fusion.6), channel_id=1, source_target_pairs={{0,4},{1,5},{2,6},{3,7},{4,0},{5,1},{6,2},{7,3},{8,11},{9,10},{10,... | collective-permute-start | bytes 589832 | tf_op jit(solution)/shard_map/ppermute | solution.py:45
  66.1 6.8 %collective-permute-start.15 = (bf16[15,32,256]{2,1,0:T(8,128)(2,1)S(1)}, bf16[15,32,256]{2,1,0:T(8,128)(2,1)S(1)}, u32[]{:S(2)}, u32[]{:S(2)}) collective-permute-start(bf16[15,32,256]{2,1,0:T(8,128)(2,1)S(1)} %add_convert_fusion.1), channel_id=1, source_target_pairs={{0,3},{1,2},{2,1},{3,0},{4,7},{5,6},{6,5},{7,4},{8,56},{9,57},{10,... | collective-permute-start | bytes 737288 | tf_op jit(solution)/shard_map/ppermute | solution.py:45
  72.0 4.9 %collective-permute-start.18 = (bf16[12,32,256]{2,1,0:T(8,128)(2,1)S(1)}, bf16[12,32,256]{2,1,0:T(8,128)(2,1)S(1)}, u32[]{:S(2)}, u32[]{:S(2)}) collective-permute-start(bf16[12,32,256]{2,1,0:T(8,128)(2,1)S(1)} %add_convert_fusion.5), channel_id=1, source_target_pairs={{0,1},{1,0},{2,3},{3,2},{4,5},{5,4},{6,7},{7,6},{8,24},{9,25},{10,... | collective-permute-start | bytes 589832 | tf_op jit(solution)/shard_map/ppermute | solution.py:45
  73.0 7.5 %collective-permute-start.17 = (bf16[15,32,256]{2,1,0:T(8,128)(2,1)S(1)}, bf16[15,32,256]{2,1,0:T(8,128)(2,1)S(1)}, u32[]{:S(2)}, u32[]{:S(2)}) collective-permute-start(bf16[15,32,256]{2,1,0:T(8,128)(2,1)S(1)} %add_convert_fusion), channel_id=1, source_target_pairs={{0,4},{1,5},{2,6},{3,7},{4,0},{5,1},{6,2},{7,3},{8,11},{9,10},{10,... | collective-permute-start | bytes 737288 | tf_op jit(solution)/shard_map/ppermute | solution.py:45
  77.0 6.9 %collective-permute-start.20 = (bf16[12,32,256]{2,1,0:T(8,128)(2,1)S(1)}, bf16[12,32,256]{2,1,0:T(8,128)(2,1)S(1)}, u32[]{:S(2)}, u32[]{:S(2)}) collective-permute-start(bf16[12,32,256]{2,1,0:T(8,128)(2,1)S(1)} %add_convert_fusion.4), channel_id=1, source_target_pairs={{0,68},{1,69},{2,70},{3,71},{4,64},{5,65},{6,66},{7,67},{8,9},{9,8... | collective-permute-start | bytes 589832 | tf_op jit(solution)/shard_map/ppermute | solution.py:45
  80.5 10.9 %collective-permute-start.19 = (bf16[2,15,32,256]{3,2,1,0:T(8,128)(2,1)S(1)}, bf16[2,15,32,256]{3,2,1,0:T(8,128)(2,1)S(1)}, u32[]{:S(2)}, u32[]{:S(2)}) collective-permute-start(bf16[2,15,32,256]{3,2,1,0:T(8,128)(2,1)S(1)} %pad_maximum_fusion.1.refs_0_), channel_id=1, source_target_pairs={{0,16},{1,17},{2,18},{3,19},{4,20},{5,21},{6,22},{7,23},{8,76},{9,... | collective-permute-start | bytes 1474568 | tf_op jit(solution)/shard_map/ppermute | solution.py:45
  84.0 13.7 %collective-permute-start.22 = (bf16[2,12,32,256]{3,2,1,0:T(8,128)(2,1)S(1)}, bf16[2,12,32,256]{3,2,1,0:T(8,128)(2,1)S(1)}, u32[]{:S(2)}, u32[]{:S(2)}) collective-permute-start(bf16[2,12,32,256]{3,2,1,0:T(8,128)(2,1)S(1)} %pad_maximum_fusion.2.refs_1_), channel_id=1, source_target_pairs={{0,48},{1,49},{2,50},{3,51},{4,52},{5,53},{6,54},{7,55},{8,12},{9,... | collective-permute-start | bytes 1179656 | tf_op jit(solution)/shard_map/ppermute | solution.py:45
  91.4 10.2 %collective-permute-start.24 = (bf16[2,15,32,256]{3,2,1,0:T(8,128)(2,1)S(1)}, bf16[2,15,32,256]{3,2,1,0:T(8,128)(2,1)S(1)}, u32[]{:S(2)}, u32[]{:S(2)}) collective-permute-start(bf16[2,15,32,256]{3,2,1,0:T(8,128)(2,1)S(1)} %pad_maximum_fusion.1.refs_0_), channel_id=1, source_target_pairs={{0,8},{1,9},{2,10},{3,11},{4,12},{5,13},{6,14},{7,15},{8,0},{9,1},... | collective-permute-start | bytes 1474568 | tf_op jit(solution)/shard_map/ppermute | solution.py:45
  97.2 7.0 %collective-permute-start.21 = (bf16[2,15,32,256]{3,2,1,0:T(8,128)(2,1)S(1)}, bf16[2,15,32,256]{3,2,1,0:T(8,128)(2,1)S(1)}, u32[]{:S(2)}, u32[]{:S(2)}) collective-permute-start(bf16[2,15,32,256]{3,2,1,0:T(8,128)(2,1)S(1)} %collective-permute-done.19.refs_0_), channel_id=1, source_target_pairs={{0,8},{1,9},{2,10},{3,11},{4,12},{5,13},{6,14},{7,15},{8,0},{9,1},... | collective-permute-start | bytes 1474568 | tf_op jit(solution)/shard_map/ppermute | solution.py:45
  97.3 4.4 %collective-permute-start.25 = (bf16[2,12,32,256]{3,2,1,0:T(8,128)(2,1)S(1)}, bf16[2,12,32,256]{3,2,1,0:T(8,128)(2,1)S(1)}, u32[]{:S(2)}, u32[]{:S(2)}) collective-permute-start(bf16[2,12,32,256]{3,2,1,0:T(8,128)(2,1)S(1)} %pad_maximum_fusion.2.refs_1_), channel_id=1, source_target_pairs={{0,8},{1,9},{2,10},{3,11},{4,12},{5,13},{6,14},{7,15},{8,0},{9,1},... | collective-permute-start | bytes 1179656 | tf_op jit(solution)/shard_map/ppermute | solution.py:45
  97.7 6.5 %collective-permute-start.23 = (bf16[2,12,32,256]{3,2,1,0:T(8,128)(2,1)S(1)}, bf16[2,12,32,256]{3,2,1,0:T(8,128)(2,1)S(1)}, u32[]{:S(2)}, u32[]{:S(2)}) collective-permute-start(bf16[2,12,32,256]{3,2,1,0:T(8,128)(2,1)S(1)} %collective-permute-done.22.refs_1_), channel_id=1, source_target_pairs={{0,8},{1,9},{2,10},{3,11},{4,12},{5,13},{6,14},{7,15},{8,0},{9,1},... | collective-permute-start | bytes 1179656 | tf_op jit(solution)/shard_map/ppermute | solution.py:45
